TPU v7x, 32 devices: a whole 2x2x4 slice. The times are simulated.
32 devices in a mesh: dp: 8 (over y, x, core), section: 4 (over z).
Axes of the slice: x: 2, y: 2, z: 4, core: 2. Of those that a mesh axis runs over, the one named last changes fastest.
Arguments:
- encoder_input: bfloat16 [4, 8192, 768], P('section', 'dp'), may hold values from -6 to 6
- decoder_input: bfloat16 [4, 1024, 768], P('section', 'dp'), may hold values from -6 to 6
- cotangent: bfloat16 [4, 1024, 768], P('section', 'dp'), may hold values from -6 to 6
- pool_table: int32 [4, 8, 8, 256], P('section', 'dp'), may hold values from 0 to 1023, as said below
- retrieved: int32 [4, 1024, 1024], P('section', 'dp'), may hold values from 0 to 2047, as said below
- decoder_lengths: int32 [4, 8, 4], P('section', 'dp'), may hold values from 1 to 96, 128 in all within a row
- encoder_inward: bfloat16 [3, 768, 768], replicated, may hold values from -0.21875 to 0.21875
- encoder_outward: bfloat16 [768, 768], replicated, may hold values from -3.5 to 3.5
- encoder_biases: float32 [3, 768], replicated, may hold values from -3 to 3
- encoder_norms: float32 [2, 2, 768], replicated, may hold values from -3 to 3
- encoder_expand: bfloat16 [768, 3072], replicated, may hold values from -0.21875 to 0.21875
- encoder_expand_bias: float32 [3072], replicated, may hold values from -3 to 3
- encoder_shrink: bfloat16 [3072, 768], replicated, may hold values from -0.109375 to 0.109375
- encoder_shrink_bias: float32 [768], replicated, may hold values from -3 to 3
- self_inward: bfloat16 [3, 768, 768], replicated, may hold values from -0.21875 to 0.21875
- self_outward: bfloat16 [768, 768], replicated, may hold values from -0.625 to 0.625
- cross_inward: bfloat16 [3, 768, 768], replicated, may hold values from -0.21875 to 0.21875
- cross_outward: bfloat16 [768, 768], replicated, may hold values from -3.5 to 3.5
- decoder_biases: float32 [6, 768], replicated, may hold values from -3 to 3
- decoder_norms: float32 [3, 2, 768], replicated, may hold values from -3 to 3
- decoder_expand: bfloat16 [768, 3072], replicated, may hold values from -0.21875 to 0.21875
- decoder_expand_bias: float32 [3072], replicated, may hold values from -3 to 3
- decoder_shrink: bfloat16 [3072, 768], replicated, may hold values from -0.109375 to 0.109375
- decoder_shrink_bias: float32 [768], replicated, may hold values from -3 to 3
Outputs:
- decoder_output: bfloat16 [4, 1024, 768], P('section', 'dp')
- encoder_input_grad: float32 [4, 8192, 768], P('section', 'dp')
- decoder_input_grad: float32 [4, 1024, 768], P('section', 'dp')
- delta_encoder_inward: float32 [3, 768, 768], P(None, 'dp')
- delta_encoder_outward: float32 [768, 768], P('dp')
- delta_encoder_biases: float32 [3, 768], P(None, 'dp')
- delta_encoder_norms: float32 [2, 2, 768], P(None, None, 'dp')
- delta_encoder_expand: float32 [768, 3072], P('dp')
- delta_encoder_expand_bias: float32 [3072], P('dp')
- delta_encoder_shrink: float32 [3072, 768], P('dp')
- delta_encoder_shrink_bias: float32 [768], P('dp')
- delta_self_inward: float32 [3, 768, 768], P(None, 'dp')
- delta_self_outward: float32 [768, 768], P('dp')
- delta_cross_inward: float32 [3, 768, 768], P(None, 'dp')
- delta_cross_outward: float32 [768, 768], P('dp')
- delta_decoder_biases: float32 [6, 768], P(None, 'dp')
- delta_decoder_norms: float32 [3, 2, 768], P(None, None, 'dp')
- delta_decoder_expand: float32 [768, 3072], P('dp')
- delta_decoder_expand_bias: float32 [3072], P('dp')
- delta_decoder_shrink: float32 [3072, 768], P('dp')
- delta_decoder_shrink_bias: float32 [768], P('dp')
Inputs may be any that keep to these rules, and one draw needn't show every extreme that they name: `pool_table`: within one block of 256 entries (one micro-batch, owner and requesting device) the rows are distinct. `retrieved`: A query's 1024 slots are distinct. For each micro-batch and requesting device, the slots of owner o that any query names lie among the first k_o of that owner's 256, with k_o from 128 to 256.
All inputs are finite; a program needn't handle non-finite values.
Results may differ from a plain program's by a relative error of at most 0.025.
Values may be sent and summed in bfloat16 or wider, within the bound.
A program may use at most 384 MiB of HBM per device.

v0:
```python
import jax
import jax.numpy as jnp
from jax import lax
from jax.sharding import PartitionSpec as P

HEAD = 64


norm_eps = 1e-05
scale_scores = 0.125
low_type = jnp.bfloat16
wide_type = jnp.float32


def shifted(value, axis, by):
    length = lax.axis_size(axis)
    return lax.ppermute(value, axis, [(i, (i + by) % length) for i in range(length)])


def norm_apply(values, pair):
    centre = jnp.mean(values, -1, keepdims=True)
    centred = values - centre
    spread = jnp.mean(centred * centred, -1, keepdims=True)
    return centred * lax.rsqrt(spread + norm_eps) * (1.0 + pair[0]) + pair[1]


def norm_back(values, pair, incoming):
    return jax.vjp(norm_apply, values, pair)[1](incoming)


def gelu_exact(values):
    return jax.nn.gelu(values, approximate=False)


def project(left, right):
    return jnp.dot(left, right, preferred_element_type=wide_type)


def project_back(left, incoming):
    return lax.dot_general(
        left, incoming, (((0,), (0,)), ((), ())), preferred_element_type=wide_type
    )


def back_through(incoming, right):
    return lax.dot_general(
        incoming, right, (((1,), (1,)), ((), ())), preferred_element_type=wide_type
    )


def column_sum(values):
    return jnp.sum(values, 0, dtype=wide_type)


def split_heads(values):
    return values.reshape(values.shape[0], -1, HEAD).transpose(1, 0, 2)


def join_heads(values):
    return values.transpose(1, 0, 2).reshape(values.shape[1], -1)


def block_scores(query_heads, key_heads, allowed, row_start, block_rows):
    scores = (
        jnp.einsum(
            "hqe,hke->hqk",
            query_heads[:, row_start : row_start + block_rows],
            key_heads,
            preferred_element_type=wide_type,
        )
        * scale_scores
    )
    if allowed is not None:
        scores = jnp.where(allowed[None, row_start : row_start + block_rows], scores, -1e30)
    return scores


def attend_forward(query_heads, key_heads, value_heads, allowed):
    length = query_heads.shape[1]
    block_rows = min(512, length)
    contexts = []
    totals = []
    for row_start in range(0, length, block_rows):
        scores = block_scores(query_heads, key_heads, allowed, row_start, block_rows)
        row_max = jnp.max(scores, -1, keepdims=True)
        exponent = jnp.exp(scores - row_max)
        row_total = jnp.sum(exponent, -1, keepdims=True)
        weights_low = (exponent / row_total).astype(low_type)
        contexts.append(
            jnp.einsum("hqk,hke->hqe", weights_low, value_heads, preferred_element_type=wide_type)
        )
        totals.append(row_max + jnp.log(row_total))
    return (join_heads(jnp.concatenate(contexts, 1)), jnp.concatenate(totals, 1))


def attend_backward(query_heads, key_heads, value_heads, allowed, totals, context_grad):
    length = query_heads.shape[1]
    block_rows = min(512, length)
    query_grads = []
    key_grad = jnp.zeros(key_heads.shape, wide_type)
    value_grad = jnp.zeros(value_heads.shape, wide_type)
    for row_start in range(0, length, block_rows):
        scores = block_scores(query_heads, key_heads, allowed, row_start, block_rows)
        weights_full = jnp.exp(scores - totals[:, row_start : row_start + block_rows])
        grad_block = context_grad[:, row_start : row_start + block_rows]
        weights_grad = jnp.einsum(
            "hqe,hke->hqk", grad_block, value_heads, preferred_element_type=wide_type
        )
        inner = jnp.sum(weights_full * weights_grad, -1, keepdims=True)
        scores_grad = (weights_full * (weights_grad - inner)).astype(low_type)
        query_grads.append(
            jnp.einsum("hqk,hke->hqe", scores_grad, key_heads, preferred_element_type=wide_type)
            * scale_scores
        )
        key_grad = (
            key_grad
            + jnp.einsum(
                "hqk,hqe->hke",
                scores_grad,
                query_heads[:, row_start : row_start + block_rows],
                preferred_element_type=wide_type,
            )
            * scale_scores
        )
        value_grad = value_grad + jnp.einsum(
            "hqk,hqe->hke",
            weights_full.astype(low_type),
            grad_block,
            preferred_element_type=wide_type,
        )
    return (
        join_heads(jnp.concatenate(query_grads, 1)).astype(low_type),
        join_heads(key_grad).astype(low_type),
        join_heads(value_grad).astype(low_type),
    )


def attention_forward(source_query, source_keys, inward, outward, biases, allowed):
    query_rows = (project(source_query, inward[0]) + biases[0]).astype(low_type)
    key_rows = project(source_keys, inward[1]).astype(low_type)
    value_rows = (project(source_keys, inward[2]) + biases[1]).astype(low_type)
    context, totals = attend_forward(
        split_heads(query_rows), split_heads(key_rows), split_heads(value_rows), allowed
    )
    context = context.astype(low_type)
    return (
        project(context, outward) + biases[2],
        (query_rows, key_rows, value_rows, totals, context),
    )


def attention_backward(source_query, source_keys, inward, outward, allowed, saved_state, incoming):
    query_rows, key_rows, value_rows, totals, context = saved_state
    incoming_low = incoming.astype(low_type)
    context_grad = back_through(incoming_low, outward).astype(low_type)
    query_grad, key_grad, value_grad = attend_backward(
        split_heads(query_rows),
        split_heads(key_rows),
        split_heads(value_rows),
        allowed,
        totals,
        split_heads(context_grad),
    )
    inward_grad = jnp.stack(
        [
            project_back(source_query, query_grad),
            project_back(source_keys, key_grad),
            project_back(source_keys, value_grad),
        ]
    )
    bias_grad = jnp.stack(
        [column_sum(query_grad), column_sum(value_grad), column_sum(incoming_low)]
    )
    source_query_grad = back_through(query_grad, inward[0])
    source_keys_grad = back_through(key_grad, inward[1]) + back_through(value_grad, inward[2])
    return (
        source_query_grad,
        source_keys_grad,
        inward_grad,
        project_back(context, incoming_low),
        bias_grad,
    )


def feed_forward(normed, expand, expand_bias, shrink, shrink_bias):
    normed_low = normed.astype(low_type)
    before = project(normed_low, expand) + expand_bias
    hidden = gelu_exact(before).astype(low_type)
    return (project(hidden, shrink) + shrink_bias, (normed_low, before, hidden))


def feed_forward_back(expand, shrink, saved_state, incoming):
    normed_low, before, hidden = saved_state
    incoming_low = incoming.astype(low_type)
    hidden_grad = back_through(incoming_low, shrink)
    before_grad = jax.vjp(gelu_exact, before)[1](hidden_grad)[0].astype(low_type)
    return (
        back_through(before_grad, expand),
        project_back(normed_low, before_grad),
        column_sum(before_grad),
        project_back(hidden, incoming_low),
        column_sum(incoming_low),
    )


def encoder_pass(inputs, weight_set):
    inward, outward, biases, norms, expand, expand_bias, shrink, shrink_bias = weight_set
    branch, attention_saved = attention_forward(inputs, inputs, inward, outward, biases, None)
    mixed_rows = inputs.astype(wide_type) + branch
    first_norm = norm_apply(mixed_rows, norms[0])
    expand_out, feed_saved = feed_forward(first_norm, expand, expand_bias, shrink, shrink_bias)
    summed = first_norm + expand_out
    return (norm_apply(summed, norms[1]), (attention_saved, mixed_rows, feed_saved, summed))


def encoder_back(inputs, weight_set, saved_state, incoming):
    inward, outward, biases, norms, expand, expand_bias, shrink, shrink_bias = weight_set
    attention_saved, mixed_rows, feed_saved, summed = saved_state
    summed_grad, norm_two_grad = norm_back(summed, norms[1], incoming)
    first_grad, expand_grad, expand_bias_grad, shrink_grad, shrink_bias_grad = feed_forward_back(
        expand, shrink, feed_saved, summed_grad
    )
    mixed_grad, norm_one_grad = norm_back(mixed_rows, norms[0], first_grad + summed_grad)
    query_side, key_side, inward_grad, outward_grad, bias_grad = attention_backward(
        inputs, inputs, inward, outward, None, attention_saved, mixed_grad
    )
    return (
        mixed_grad + query_side + key_side,
        inward_grad,
        outward_grad,
        bias_grad,
        jnp.stack([norm_one_grad, norm_two_grad]),
        expand_grad,
        expand_bias_grad,
        shrink_grad,
        shrink_bias_grad,
    )


def decoder_pass(inputs, pooled, weight_set, self_allowed, cross_allowed):
    (
        self_inward,
        self_outward,
        cross_inward,
        cross_outward,
        biases,
        norms,
        expand,
        expand_bias,
        shrink,
        shrink_bias,
    ) = weight_set
    branch, self_saved = attention_forward(
        inputs, inputs, self_inward, self_outward, biases[0:3], self_allowed
    )
    mixed_rows = inputs.astype(wide_type) + branch
    first_norm = norm_apply(mixed_rows, norms[0])
    first_low = first_norm.astype(low_type)
    cross_out, cross_saved = attention_forward(
        first_low, pooled, cross_inward, cross_outward, biases[3:6], cross_allowed
    )
    joined = first_norm + cross_out
    second = norm_apply(joined, norms[1])
    expand_out, feed_saved = feed_forward(second, expand, expand_bias, shrink, shrink_bias)
    summed = second + expand_out
    return (
        norm_apply(summed, norms[2]),
        (self_saved, mixed_rows, first_low, cross_saved, joined, feed_saved, summed),
    )


def decoder_back(inputs, pooled, weight_set, self_allowed, cross_allowed, saved_state, incoming):
    (
        self_inward,
        self_outward,
        cross_inward,
        cross_outward,
        biases,
        norms,
        expand,
        expand_bias,
        shrink,
        shrink_bias,
    ) = weight_set
    self_saved, mixed_rows, first_low, cross_saved, joined, feed_saved, summed = saved_state
    summed_grad, norm_three_grad = norm_back(summed, norms[2], incoming)
    second_grad, expand_grad, expand_bias_grad, shrink_grad, shrink_bias_grad = feed_forward_back(
        expand, shrink, feed_saved, summed_grad
    )
    joined_grad, norm_two_grad = norm_back(joined, norms[1], second_grad + summed_grad)
    cross_query, pooled_grad, cross_inward_grad, cross_outward_grad, cross_bias_grad = (
        attention_backward(
            first_low, pooled, cross_inward, cross_outward, cross_allowed, cross_saved, joined_grad
        )
    )
    mixed_grad, norm_one_grad = norm_back(mixed_rows, norms[0], joined_grad + cross_query)
    query_side, key_side, self_inward_grad, self_outward_grad, self_bias_grad = attention_backward(
        inputs, inputs, self_inward, self_outward, self_allowed, self_saved, mixed_grad
    )
    return (
        mixed_grad + query_side + key_side,
        pooled_grad,
        self_inward_grad,
        self_outward_grad,
        cross_inward_grad,
        cross_outward_grad,
        jnp.concatenate([self_bias_grad, cross_bias_grad], 0),
        jnp.stack([norm_one_grad, norm_two_grad, norm_three_grad]),
        expand_grad,
        expand_bias_grad,
        shrink_grad,
        shrink_bias_grad,
    )


def encoder_section_total(shares):
    matrix_parts = (
        lax.psum_scatter(
            shares[0].astype(jnp.bfloat16), "section", scatter_dimension=2, tiled=True
        ).astype(jnp.float32),
        lax.psum_scatter(
            shares[1].astype(jnp.bfloat16), "section", scatter_dimension=1, tiled=True
        ).astype(jnp.float32),
        lax.psum_scatter(
            shares[4].astype(jnp.bfloat16), "section", scatter_dimension=1, tiled=True
        ).astype(jnp.float32),
        lax.psum_scatter(
            shares[6].astype(jnp.bfloat16), "section", scatter_dimension=1, tiled=True
        ).astype(jnp.float32),
    )
    matrix_whole = (
        lax.all_gather(matrix_parts[0].astype(jnp.bfloat16), "section", axis=2, tiled=True).astype(
            jnp.float32
        ),
        lax.all_gather(matrix_parts[1].astype(jnp.bfloat16), "section", axis=1, tiled=True).astype(
            jnp.float32
        ),
        lax.all_gather(matrix_parts[2].astype(jnp.bfloat16), "section", axis=1, tiled=True).astype(
            jnp.float32
        ),
        lax.all_gather(matrix_parts[3].astype(jnp.bfloat16), "section", axis=1, tiled=True).astype(
            jnp.float32
        ),
    )
    small_total = lax.psum((shares[2], shares[3], shares[5], shares[7]), "section")
    return (
        matrix_whole[0],
        matrix_whole[1],
        small_total[0],
        small_total[1],
        matrix_whole[2],
        small_total[2],
        matrix_whole[3],
        small_total[3],
    )


def decoder_section_total(shares):
    matrix_parts = (
        lax.psum_scatter(
            shares[0].astype(jnp.bfloat16), "section", scatter_dimension=2, tiled=True
        ).astype(jnp.float32),
        lax.psum_scatter(
            shares[1].astype(jnp.bfloat16), "section", scatter_dimension=1, tiled=True
        ).astype(jnp.float32),
        lax.psum_scatter(
            shares[2].astype(jnp.bfloat16), "section", scatter_dimension=2, tiled=True
        ).astype(jnp.float32),
        lax.psum_scatter(
            shares[3].astype(jnp.bfloat16), "section", scatter_dimension=1, tiled=True
        ).astype(jnp.float32),
        lax.psum_scatter(
            shares[6].astype(jnp.bfloat16), "section", scatter_dimension=1, tiled=True
        ).astype(jnp.float32),
        lax.psum_scatter(
            shares[8].astype(jnp.bfloat16), "section", scatter_dimension=1, tiled=True
        ).astype(jnp.float32),
    )
    matrix_whole = (
        lax.all_gather(matrix_parts[0].astype(jnp.bfloat16), "section", axis=2, tiled=True).astype(
            jnp.float32
        ),
        lax.all_gather(matrix_parts[1].astype(jnp.bfloat16), "section", axis=1, tiled=True).astype(
            jnp.float32
        ),
        lax.all_gather(matrix_parts[2].astype(jnp.bfloat16), "section", axis=2, tiled=True).astype(
            jnp.float32
        ),
        lax.all_gather(matrix_parts[3].astype(jnp.bfloat16), "section", axis=1, tiled=True).astype(
            jnp.float32
        ),
        lax.all_gather(matrix_parts[4].astype(jnp.bfloat16), "section", axis=1, tiled=True).astype(
            jnp.float32
        ),
        lax.all_gather(matrix_parts[5].astype(jnp.bfloat16), "section", axis=1, tiled=True).astype(
            jnp.float32
        ),
    )
    small_total = lax.psum((shares[4], shares[5], shares[7], shares[9]), "section")
    return (
        matrix_whole[0],
        matrix_whole[1],
        matrix_whole[2],
        matrix_whole[3],
        small_total[0],
        small_total[1],
        matrix_whole[4],
        small_total[2],
        matrix_whole[5],
        small_total[3],
    )


def on_device(
    encoder_input,
    decoder_input,
    cotangent,
    pool_table,
    retrieved,
    decoder_lengths,
    encoder_inward,
    encoder_outward,
    encoder_biases,
    encoder_norms,
    encoder_expand,
    encoder_expand_bias,
    encoder_shrink,
    encoder_shrink_bias,
    self_inward,
    self_outward,
    cross_inward,
    cross_outward,
    decoder_biases,
    decoder_norms,
    decoder_expand,
    decoder_expand_bias,
    decoder_shrink,
    decoder_shrink_bias,
):
    encoder_weights = (
        encoder_inward,
        encoder_outward,
        encoder_biases,
        encoder_norms,
        encoder_expand,
        encoder_expand_bias,
        encoder_shrink,
        encoder_shrink_bias,
    )
    decoder_weights = (
        self_inward,
        self_outward,
        cross_inward,
        cross_outward,
        decoder_biases,
        decoder_norms,
        decoder_expand,
        decoder_expand_bias,
        decoder_shrink,
        decoder_shrink_bias,
    )
    encoder_rows = encoder_input[0]
    encoder_final, encoder_saved = encoder_pass(encoder_rows, encoder_weights)
    half_way = lax.axis_size("section") // 2
    arrived = shifted(encoder_final.astype(low_type), "section", half_way)
    owner_table = pool_table[0, 0]
    picked_rows = jnp.take(arrived, owner_table, axis=0)
    fetched = lax.all_to_all(picked_rows, "dp", split_axis=0, concat_axis=0, tiled=True)
    owners, slot_count, feature_count = fetched.shape
    pooled = fetched.reshape(owners * slot_count, feature_count)
    decoder_rows = decoder_input[0]
    positions = jnp.arange(decoder_rows.shape[0], dtype=jnp.int32)
    seq_ends = jnp.cumsum(decoder_lengths[0, 0], dtype=jnp.int32)
    segment_id = jnp.sum((positions[:, None] >= seq_ends[None, :-1]).astype(jnp.int32), 1)
    self_allowed = (segment_id[:, None] == segment_id[None, :]) & (
        positions[None, :] <= positions[:, None]
    )
    cross_allowed = (
        jnp.zeros((decoder_rows.shape[0], pooled.shape[0]), jnp.bool_)
        .at[positions[:, None], retrieved[0]]
        .set(True)
    )
    decoder_final, decoder_saved = decoder_pass(
        decoder_rows, pooled, decoder_weights, self_allowed, cross_allowed
    )
    (
        decoder_grad,
        pooled_grad,
        delta_self_inward,
        delta_self_outward,
        delta_cross_inward,
        delta_cross_outward,
        delta_decoder_biases,
        delta_decoder_norms,
        delta_decoder_expand,
        delta_decoder_expand_bias,
        delta_decoder_shrink,
        delta_decoder_shrink_bias,
    ) = decoder_back(
        decoder_rows,
        pooled,
        decoder_weights,
        self_allowed,
        cross_allowed,
        decoder_saved,
        cotangent[0].astype(wide_type),
    )
    returned = lax.all_to_all(
        pooled_grad.astype(low_type).reshape(owners, slot_count, feature_count),
        "dp",
        split_axis=0,
        concat_axis=0,
        tiled=True,
    )
    spread = (
        jnp.arange(arrived.shape[0], dtype=jnp.int32)[:, None] == owner_table.reshape(1, -1)
    ).astype(low_type)
    state_grad = jnp.dot(
        spread, returned.reshape(-1, feature_count), preferred_element_type=wide_type
    )
    encoder_incoming = shifted(state_grad.astype(low_type), "section", -half_way).astype(wide_type)
    (
        encoder_grad,
        delta_encoder_inward,
        delta_encoder_outward,
        delta_encoder_biases,
        delta_encoder_norms,
        delta_encoder_expand,
        delta_encoder_expand_bias,
        delta_encoder_shrink,
        delta_encoder_shrink_bias,
    ) = encoder_back(encoder_rows, encoder_weights, encoder_saved, encoder_incoming)
    shares = (
        lax.psum_scatter(delta_encoder_inward, "dp", scatter_dimension=1, tiled=True),
        lax.psum_scatter(delta_encoder_outward, "dp", scatter_dimension=0, tiled=True),
        lax.psum_scatter(delta_encoder_biases, "dp", scatter_dimension=1, tiled=True),
        lax.psum_scatter(delta_encoder_norms, "dp", scatter_dimension=2, tiled=True),
        lax.psum_scatter(delta_encoder_expand, "dp", scatter_dimension=0, tiled=True),
        lax.psum_scatter(delta_encoder_expand_bias, "dp", scatter_dimension=0, tiled=True),
        lax.psum_scatter(delta_encoder_shrink, "dp", scatter_dimension=0, tiled=True),
        lax.psum_scatter(delta_encoder_shrink_bias, "dp", scatter_dimension=0, tiled=True),
        lax.psum_scatter(delta_self_inward, "dp", scatter_dimension=1, tiled=True),
        lax.psum_scatter(delta_self_outward, "dp", scatter_dimension=0, tiled=True),
        lax.psum_scatter(delta_cross_inward, "dp", scatter_dimension=1, tiled=True),
        lax.psum_scatter(delta_cross_outward, "dp", scatter_dimension=0, tiled=True),
        lax.psum_scatter(delta_decoder_biases, "dp", scatter_dimension=1, tiled=True),
        lax.psum_scatter(delta_decoder_norms, "dp", scatter_dimension=2, tiled=True),
        lax.psum_scatter(delta_decoder_expand, "dp", scatter_dimension=0, tiled=True),
        lax.psum_scatter(delta_decoder_expand_bias, "dp", scatter_dimension=0, tiled=True),
        lax.psum_scatter(delta_decoder_shrink, "dp", scatter_dimension=0, tiled=True),
        lax.psum_scatter(delta_decoder_shrink_bias, "dp", scatter_dimension=0, tiled=True),
    )
    results = tuple(encoder_section_total(tuple(shares[0:8]))) + tuple(
        decoder_section_total(tuple(shares[8:18]))
    )
    return (decoder_final.astype(low_type)[None], encoder_grad[None], decoder_grad[None]) + results


def solution(mesh):
    in_specs = (
        P("section", "dp", None),
        P("section", "dp", None),
        P("section", "dp", None),
        P("section", "dp", None, None),
        P("section", "dp", None),
        P("section", "dp", None),
        P(),
        P(),
        P(),
        P(),
        P(),
        P(),
        P(),
        P(),
        P(),
        P(),
        P(),
        P(),
        P(),
        P(),
        P(),
        P(),
        P(),
        P(),
    )
    out_specs = (
        P("section", "dp", None),
        P("section", "dp", None),
        P("section", "dp", None),
        P(None, "dp", None),
        P("dp", None),
        P(None, "dp"),
        P(None, None, "dp"),
        P("dp", None),
        P("dp"),
        P("dp", None),
        P("dp"),
        P(None, "dp", None),
        P("dp", None),
        P(None, "dp", None),
        P("dp", None),
        P(None, "dp"),
        P(None, None, "dp"),
        P("dp", None),
        P("dp"),
        P("dp", None),
        P("dp"),
    )
    return jax.shard_map(
        on_device, mesh=mesh, in_specs=in_specs, out_specs=out_specs, check_vma=False
    )
```

profile of v0, /device:TPU:0, one launch (start us, length us, event | category | flops | bytes accessed | tf_op | source)
XLA Modules:
  0.0 2015.1 jit_solution(3526209359591223062)
XLA Ops:
  89.0 35.8 %multiply_convert_fusion.3 = (bf16[1024,3072]{1,0:T(8,128)(2,1)}, f32[1024,3072]{1,0:T(8,128)}, f32[1024,3072]{1,0:T(8,128)}) fusion(f32[3072]{0:T(1024)S(1)} %copy-done.156, bf16[768,3072]{1,0:T(8,128)(2,1)S(1)} %bitcast.479, f32[1024,768]{0,1:T(8,128)S(1)} %get-tuple-element.181, f32[768]{0:T(1024)S(1)} %get-tuple-element.133, ...), kind=kOutput, calls=%fused_computation.32 | convolution fusion | flops 5043388416 | bytes 39348224 | tf_op jit(solution)/shard_map/dot_general | solution.py:36
  152.3 54.4 %collective-permute-done = bf16[1024,768]{0,1:T(8,128)(2,1)} collective-permute-done((bf16[1024,768]{0,1:T(8,128)(2,1)S(1)}, bf16[1024,768]{0,1:T(8,128)(2,1)}, u32[]{:S(2)}, u32[]{:S(2)}) %collective-permute-start) | collective-permute-done | bytes 1572896 | tf_op jit(solution)/shard_map/ppermute | solution.py:17
  231.1 544.8 %scatter_custom_fusion = pred[262144]{0:T(1024)(128)(4,1)S(1)} fusion(s32[131072]{0:T(1024)S(1)} %bitcast.464, pred[131072]{0:T(1024)(128)(4,1)S(1)} %broadcast.602, pred[]{:T(512)} %constant.52.clone.1), kind=kCustom, calls=%fused_computation.242 | custom fusion | bytes 262145
  878.7 24.9 %all-to-all-done.1 = bf16[8,256,768]{2,1,0:T(8,128)(2,1)} async-done(((bf16[8,256,768]{2,1,0:T(8,128)(2,1)}), bf16[8,256,768]{2,1,0:T(8,128)(2,1)}, u32[]{:S(2)}, u32[]{:S(2)}) %all-to-all-start.1) | async-done | bytes 3145760 | tf_op jit(solution)/shard_map/all_to_all | solution.py:508
  912.4 66.3 %collective-permute-done.1 = bf16[1024,768]{0,1:T(8,128)(2,1)} collective-permute-done((bf16[1024,768]{0,1:T(8,128)(2,1)}, bf16[1024,768]{0,1:T(8,128)(2,1)}, u32[]{:S(2)}, u32[]{:S(2)}) %collective-permute-start.1) | collective-permute-done | bytes 1572896 | tf_op jit(solution)/shard_map/ppermute | solution.py:17
  990.7 19.1 convert_reduce_fusion
  1113.8 22.1 %multiply_convert_fusion = bf16[12,512,1024]{2,1,0:T(8,128)(2,1)} fusion(f32[12,512,1024]{2,1,0:T(8,128)} %get-tuple-element.203, f32[12,512,1024]{2,1,0:T(8,128)} %get-tuple-element.177, f32[12,512]{1,0:T(8,128)S(1)} %get-tuple-element.202, f32[12,512]{1,0:T(8,128)S(1)} %log_add_fusion), kind=kLoop, calls=%fused_computation.2 | loop fusion | flops 31457280 | bytes 62963712 | tf_op jit(solution)/shard_map/convert_element_type | solution.py:110
  1144.9 20.5 %multiply_reduce_fusion.1 = (f32[12,512]{1,0:T(8,128)}, f32[12,512,1024]{2,1,0:T(8,128)}) fusion(f32[12,512,1024]{2,1,0:T(8,128)} %get-tuple-element.179, f32[12,512]{1,0:T(8,128)} %log_add_fusion.1, bf16[12,1024,64]{1,2,0:T(8,128)(2,1)S(1)} %bitcast.398, bf16[12,1024,64]{1,2,0:T(8,128)(2,1)} %bitcast.407), kind=kOutput, calls=%fused_computation.6 | convolution fusion | flops 830466048 | bytes 52748288 | tf_op jit(solution)/shard_map/hqe,hke->hqk/dot_general | solution.py:106
  1165.4 23.3 %multiply_convert_fusion.1 = bf16[12,512,1024]{2,1,0:T(8,128)(2,1)} fusion(f32[12,512,1024]{2,1,0:T(8,128)} %get-tuple-element.201, f32[12,512,1024]{2,1,0:T(8,128)} %get-tuple-element.179, f32[12,512]{1,0:T(8,128)} %get-tuple-element.200, f32[12,512]{1,0:T(8,128)} %log_add_fusion.1), kind=kLoop, calls=%fused_computation.5 | loop fusion | flops 31457280 | bytes 62963712 | tf_op jit(solution)/shard_map/convert_element_type | solution.py:110
  1320.0 50.6 %reduce-scatter.71.cloned.1.call-done = f32[384,768]{1,0:T(8,128)} async-done(((f32[3072,768]{1,0:T(8,128)}), f32[384,768]{1,0:T(8,128)}) %reduce-scatter.71.cloned.1.call-update) | async-done | bytes 1179664 | tf_op jit(solution)/shard_map/reduce_scatter | solution.py:550
  1373.0 67.0 %reduce-scatter.73.cloned.1.call-done = f32[96,2304]{1,0:T(8,128)} async-done(((f32[768,2304]{1,0:T(8,128)}), f32[96,2304]{1,0:T(8,128)}) %reduce-scatter.73.cloned.1.call-update) | async-done | bytes 884752
  1451.1 26.4 %reduce-scatter.93.cloned.1.call-done = f32[96,6]{1,0:T(8,128)} async-done(((f32[768,6]{1,0:T(8,128)}), f32[96,6]{1,0:T(8,128)}) %reduce-scatter.93.cloned.1.call-update) | async-done | bytes 2320
  1478.6 36.3 %reduce-scatter.91.cloned.1.call-done = f32[96,6]{1,0:T(8,128)} async-done(((f32[768,6]{1,0:T(8,128)}), f32[96,6]{1,0:T(8,128)}) %reduce-scatter.91.cloned.1.call-update) | async-done | bytes 2320
  1515.8 20.8 %reduce-scatter.85.cloned.1.call-done = bf16[192,96]{1,0:T(8,128)(2,1)} async-done(((bf16[768,96]{1,0:T(8,128)(2,1)}), bf16[192,96]{1,0:T(8,128)(2,1)}) %reduce-scatter.85.cloned.1.call-update) | async-done | bytes 36880
  1571.0 63.6 %reduce-scatter.53.cloned.1.call-done = f32[96,3072]{1,0:T(8,128)} async-done(((f32[768,3072]{1,0:T(8,128)}), f32[96,3072]{1,0:T(8,128)}) %reduce-scatter.53.cloned.1.call-update) | async-done | bytes 1179664 | tf_op jit(solution)/shard_map/reduce_scatter | solution.py:538
  1641.8 23.5 %all-reduce.14 = (f32[3072]{0:T(1024)S(1)}, f32[768]{0:T(1024)S(1)}, f32[3072]{0:T(1024)S(1)}, f32[768]{0:T(1024)S(1)}) all-reduce(f32[3072]{0:T(1024)S(1)} %copy-done.127, f32[768]{0:T(1024)S(1)} %copy-done.116, f32[3072]{0:T(1024)S(1)} %copy-done.126, f32[768]{0:T(1024)S(1)} %copy-done.115), channel_id=10, replica_groups=mesh['dp'=8,'section'=4] {'dp'}, use_global_device_ids=true, to_apply=%region_53.54.clone | all-reduce | flops 7680 | bytes 61440
  1678.1 30.7 %reduce-scatter.79.cloned.1.call-done = f32[96,4]{1,0:T(8,128)} async-done(((f32[768,4]{1,0:T(8,128)}), f32[96,4]{1,0:T(8,128)}) %reduce-scatter.79.cloned.1.call-update) | async-done | bytes 1552
  1709.8 19.4 all-reduce.15
  1729.2 59.5 %reduce-scatter.57.cloned.1.call-done = f32[384,768]{1,0:T(8,128)} async-done(((f32[3072,768]{1,0:T(8,128)}), f32[384,768]{1,0:T(8,128)}) %reduce-scatter.57.cloned.1.call-update) | async-done | bytes 1179664 | tf_op jit(solution)/shard_map/reduce_scatter | solution.py:540
  1791.1 19.1 reduce-scatter.75.cloned.1.call-done
  1834.4 23.4 %all_gather.36 = bf16[3,96,768]{1,0,2:T(4,128)(2,1)S(1)} all-gather(bf16[3,96,192]{1,0,2:T(4,128)(2,1)S(1)} %bitcast.455), channel_id=1, replica_groups=mesh['dp'=8,'section'=4] {'section'}, dimensions={2}, use_global_device_ids=true | all-gather | bytes 552960 | tf_op jit(solution)/shard_map/all_gather | solution.py:386
  1860.9 20.0 all_gather.34
  1913.1 19.6 all_gather.39
  1964.7 19.5 all_gather.32
  (669 shorter events, 686.1 us)
Async XLA Ops:
  221.8 554.3 %all-to-all-start = ((bf16[8,256,768]{2,1,0:T(8,128)(2,1)}), bf16[8,256,768]{2,1,0:T(8,128)(2,1)}, u32[]{:S(2)}, u32[]{:S(2)}) async-start(bf16[8,256,768]{2,1,0:T(8,128)(2,1)} %broadcast_select_fusion), calls=%async_computation | async-start | bytes 6291456 | tf_op jit(solution)/shard_map/all_to_all | solution.py:468
  865.8 410.3 %reduce-scatter.61.cloned.1.call-start = ((), (), s32[]{:S(2)}) async-start(), calls=%async_computation.32 | async-start | bytes 2654208 | tf_op jit(solution)/shard_map/reduce_scatter | solution.py:543
  878.6 399.3 %reduce-scatter.65.cloned.1.call-start = ((), (), s32[]{:S(2)}) async-start(), calls=%async_computation.34 | async-start | bytes 2654208 | tf_op jit(solution)/shard_map/reduce_scatter | solution.py:545
  912.2 397.5 %reduce-scatter.51.cloned.1.call-start = ((), (), s32[]{:S(2)}) async-start(), calls=%async_computation.27 | async-start | bytes 2654208 | tf_op jit(solution)/shard_map/reduce_scatter | solution.py:535
  1029.4 282.2 %reduce-scatter.63.cloned.1.call-start = ((), (), s32[]{:S(2)}) async-start(), calls=%async_computation.33 | async-start | bytes 7962624 | tf_op jit(solution)/shard_map/reduce_scatter | solution.py:544
  1044.2 270.5 %reduce-scatter.83.cloned.1.call-start = ((), (), s32[]{:S(2)}) async-start(), calls=%async_computation.43 | async-start | bytes 7962624
  1078.5 239.2 %reduce-scatter.67.cloned.1.call-start = ((), (), s32[]{:S(2)}) async-start(), calls=%async_computation.35 | async-start | bytes 10616832 | tf_op jit(solution)/shard_map/reduce_scatter | solution.py:548
  1085.5 285.0 %reduce-scatter.71.cloned.1.call-start = ((), (), s32[]{:S(2)}) async-start(), calls=%async_computation.37 | async-start | bytes 10616832 | tf_op jit(solution)/shard_map/reduce_scatter | solution.py:550
  1092.3 347.7 %reduce-scatter.73.cloned.1.call-start = ((), (), s32[]{:S(2)}) async-start(), calls=%async_computation.38 | async-start | bytes 7962624
  1271.2 243.7 %reduce-scatter.91.cloned.1.call-start = ((), (), s32[]{:S(2)}) async-start(), calls=%async_computation.47 | async-start | bytes 442368
  1276.0 260.6 %reduce-scatter.85.cloned.1.call-start = ((), (), s32[]{:S(2)}) async-start(), calls=%async_computation.44 | async-start | bytes 245760
  1277.9 278.5 %reduce-scatter.89.cloned.1.call-start = ((), (), s32[]{:S(2)}) async-start(), calls=%async_computation.46 | async-start | bytes 245760
  1279.8 354.8 %reduce-scatter.53.cloned.1.call-start = ((), (), s32[]{:S(2)}) async-start(), calls=%async_computation.28 | async-start | bytes 10616832 | tf_op jit(solution)/shard_map/reduce_scatter | solution.py:538
  1290.7 386.5 %reduce-scatter.77.cloned.1.call-start = ((), (), s32[]{:S(2)}) async-start(), calls=%async_computation.40 | async-start | bytes 442368
  1295.9 412.9 %reduce-scatter.79.cloned.1.call-start = ((), (), s32[]{:S(2)}) async-start(), calls=%async_computation.41 | async-start | bytes 442368
  1298.4 490.3 %reduce-scatter.57.cloned.1.call-start = ((), (), s32[]{:S(2)}) async-start(), calls=%async_computation.30 | async-start | bytes 10616832 | tf_op jit(solution)/shard_map/reduce_scatter | solution.py:540
  1309.6 500.6 %reduce-scatter.75.cloned.1.call-start = ((), (), s32[]{:S(2)}) async-start(), calls=%async_computation.39 | async-start | bytes 245760
  1311.5 521.9 %reduce-scatter.87.cloned.1.call-start = ((), (), s32[]{:S(2)}) async-start(), calls=%async_computation.45 | async-start | bytes 737280
  1314.7 546.2 %reduce-scatter.59.cloned.1.call-start = ((), (), s32[]{:S(2)}) async-start(), calls=%async_computation.31 | async-start | bytes 737280 | tf_op jit(solution)/shard_map/reduce_scatter | solution.py:360
  1317.6 569.5 %reduce-scatter.69.cloned.1.call-start = ((), (), s32[]{:S(2)}) async-start(), calls=%async_computation.36 | async-start | bytes 737280 | tf_op jit(solution)/shard_map/reduce_scatter | solution.py:372
  1319.9 593.2 %reduce-scatter.95.cloned.1.call-start = ((), (), s32[]{:S(2)}) async-start(), calls=%async_computation.49 | async-start | bytes 737280
  1373.0 565.8 %reduce-scatter.49.cloned.1.call-start = ((), (), s32[]{:S(2)}) async-start(), calls=%async_computation.26 | async-start | bytes 737280 | tf_op jit(solution)/shard_map/reduce_scatter | solution.py:318
  1442.9 521.8 %reduce-scatter.55.cloned.1.call-start = ((), (), s32[]{:S(2)}) async-start(), calls=%async_computation.29 | async-start | bytes 737280 | tf_op jit(solution)/shard_map/reduce_scatter | solution.py:324
  1636.8 353.8 %reduce-scatter.81.cloned.1.call-start = ((), (), s32[]{:S(2)}) async-start(), calls=%async_computation.42 | async-start | bytes 737280
  (181 other events, 3711.3 us)
Sparse Core Ops, SparseCore 0:
  878.8 44.0 reduce-scatter.60
  926.6 42.4 reduce-scatter.64
  1029.5 42.1 reduce-scatter.50
  1075.5 65.4 reduce-scatter.62
  1144.4 65.5 reduce-scatter.82
  1213.7 76.4 reduce-scatter.66
  1294.1 76.4 reduce-scatter.70
  1374.5 65.5 reduce-scatter.72
  1443.7 33.8 reduce-scatter.92
  1481.0 33.8 reduce-scatter.90
  1517.2 19.3 reduce-scatter.84
  1538.8 17.5 reduce-scatter.88
  1559.9 74.6 reduce-scatter.52
  1638.1 33.8 reduce-scatter.76
  1674.9 33.8 reduce-scatter.78
  1712.2 76.4 reduce-scatter.56
  1790.8 19.3 reduce-scatter.74
  1813.0 20.3 reduce-scatter.86
  1836.3 24.5 reduce-scatter.58
  1863.7 23.3 reduce-scatter.68
  1890.1 22.9 reduce-scatter.94
  1916.1 22.6 reduce-scatter.48
  1941.8 22.9 reduce-scatter.54
  1967.0 23.6 reduce-scatter.80
where the time goes:
time: 2020 us
  local copies, waits for them, and re-layouts  667 us (33%)
  waiting for transfers between devices  562 us (28%)
  matrix products  394 us (20%)
  blocking collectives  222 us (11%)
  other arithmetic  137 us (7%)
    unnamed x402, local copies, waits for them, and re-layouts  643 us
    unnamed x36, waiting for transfers between devices  225 us
    ppermute x2, waiting for transfers between devices, shifted(): lax.ppermute(value, axis, [(i, (i + by) % length) for i in range(length)])  121 us
    dot_general x16, matrix products, project(): return jnp.dot(left, right, preferred_element_type=wide_type)  82.3 us
    dot_general x16, matrix products, back_through(): lax.dot_general(incoming, right, (((1,), (1,)), ((), ())), preferred_elem...  70.6 us
    reduce_scatter x1, waiting for transfers between devices, on_device(): lax.psum_scatter(delta_encoder_expand, 'dp', scatter_dimension=0, tiled=T...  63.6 us
    dot_general x16, matrix products, project_back(): lax.dot_general(left, incoming, (((0,), (0,)), ((), ())), preferred_eleme...  62.5 us
    reduce_scatter x1, waiting for transfers between devices, on_device(): lax.psum_scatter(delta_encoder_shrink, 'dp', scatter_dimension=0, tiled=T...  59.5 us
  transfers between devices with their start and end apart: 28, of which 20 were waited for; matrix products, arithmetic and copies ran while one was open for 48% of the time, Pallas kernels for 0%

commit v1 on v0

--- a/solution.py
+++ b/solution.py
@@ -1,9 +1,12 @@
 import jax
 import jax.numpy as jnp
 from jax import lax
+from jax.experimental import pallas as pl
+from jax.experimental.pallas import tpu as pltpu
 from jax.sharding import PartitionSpec as P
 
 HEAD = 64
+WIDTH = 768
 
 
 norm_eps = 1e-05
@@ -313,102 +316,83 @@
     )
 
 
-def encoder_section_total(shares):
-    matrix_parts = (
-        lax.psum_scatter(
-            shares[0].astype(jnp.bfloat16), "section", scatter_dimension=2, tiled=True
-        ).astype(jnp.float32),
-        lax.psum_scatter(
-            shares[1].astype(jnp.bfloat16), "section", scatter_dimension=1, tiled=True
-        ).astype(jnp.float32),
-        lax.psum_scatter(
-            shares[4].astype(jnp.bfloat16), "section", scatter_dimension=1, tiled=True
-        ).astype(jnp.float32),
-        lax.psum_scatter(
-            shares[6].astype(jnp.bfloat16), "section", scatter_dimension=1, tiled=True
-        ).astype(jnp.float32),
-    )
-    matrix_whole = (
-        lax.all_gather(matrix_parts[0].astype(jnp.bfloat16), "section", axis=2, tiled=True).astype(
-            jnp.float32
-        ),
-        lax.all_gather(matrix_parts[1].astype(jnp.bfloat16), "section", axis=1, tiled=True).astype(
-            jnp.float32
-        ),
-        lax.all_gather(matrix_parts[2].astype(jnp.bfloat16), "section", axis=1, tiled=True).astype(
-            jnp.float32
-        ),
-        lax.all_gather(matrix_parts[3].astype(jnp.bfloat16), "section", axis=1, tiled=True).astype(
-            jnp.float32
-        ),
-    )
-    small_total = lax.psum((shares[2], shares[3], shares[5], shares[7]), "section")
-    return (
-        matrix_whole[0],
-        matrix_whole[1],
-        small_total[0],
-        small_total[1],
-        matrix_whole[2],
-        small_total[2],
-        matrix_whole[3],
-        small_total[3],
-    )
-
-
-def decoder_section_total(shares):
-    matrix_parts = (
-        lax.psum_scatter(
-            shares[0].astype(jnp.bfloat16), "section", scatter_dimension=2, tiled=True
-        ).astype(jnp.float32),
-        lax.psum_scatter(
-            shares[1].astype(jnp.bfloat16), "section", scatter_dimension=1, tiled=True
-        ).astype(jnp.float32),
-        lax.psum_scatter(
-            shares[2].astype(jnp.bfloat16), "section", scatter_dimension=2, tiled=True
-        ).astype(jnp.float32),
-        lax.psum_scatter(
-            shares[3].astype(jnp.bfloat16), "section", scatter_dimension=1, tiled=True
-        ).astype(jnp.float32),
-        lax.psum_scatter(
-            shares[6].astype(jnp.bfloat16), "section", scatter_dimension=1, tiled=True
-        ).astype(jnp.float32),
-        lax.psum_scatter(
-            shares[8].astype(jnp.bfloat16), "section", scatter_dimension=1, tiled=True
-        ).astype(jnp.float32),
-    )
-    matrix_whole = (
-        lax.all_gather(matrix_parts[0].astype(jnp.bfloat16), "section", axis=2, tiled=True).astype(
-            jnp.float32
-        ),
-        lax.all_gather(matrix_parts[1].astype(jnp.bfloat16), "section", axis=1, tiled=True).astype(
-            jnp.float32
-        ),
-        lax.all_gather(matrix_parts[2].astype(jnp.bfloat16), "section", axis=2, tiled=True).astype(
-            jnp.float32
-        ),
-        lax.all_gather(matrix_parts[3].astype(jnp.bfloat16), "section", axis=1, tiled=True).astype(
-            jnp.float32
-        ),
-        lax.all_gather(matrix_parts[4].astype(jnp.bfloat16), "section", axis=1, tiled=True).astype(
-            jnp.float32
-        ),
-        lax.all_gather(matrix_parts[5].astype(jnp.bfloat16), "section", axis=1, tiled=True).astype(
-            jnp.float32
-        ),
-    )
-    small_total = lax.psum((shares[4], shares[5], shares[7], shares[9]), "section")
-    return (
-        matrix_whole[0],
-        matrix_whole[1],
-        matrix_whole[2],
-        matrix_whole[3],
-        small_total[0],
-        small_total[1],
-        matrix_whole[4],
-        small_total[2],
-        matrix_whole[5],
-        small_total[3],
-    )
+def mask_kernel(slots_ref, mask_ref):
+    count, width = slots_ref.shape
+    words = mask_ref.shape[0] // 32
+    block = 16
+    row = lax.broadcasted_iota(jnp.int32, (32, width), 0)
+    for start in range(0, words, block):
+
+        def step(i, totals):
+            piece = slots_ref[pl.ds(pl.multiple_of(i * 8, 8), 8), :]
+            word = lax.shift_right_logical(piece, 5)
+            bit = jnp.left_shift(jnp.int32(1), piece & 31)
+            return tuple(
+                total | jnp.where(word == start + w, bit, 0) for w, total in enumerate(totals)
+            )
+
+        zero = jnp.zeros((8, width), jnp.int32)
+        totals = lax.fori_loop(0, count // 8, step, (zero,) * block)
+        for w, total in enumerate(totals):
+            joined = total[0:1]
+            for k in range(1, 8):
+                joined = joined | total[k : k + 1]
+            bits = lax.shift_right_logical(jnp.broadcast_to(joined, (32, width)), row) & 1
+            at = (start + w) * 32
+            mask_ref[at : at + 32, :] = bits.astype(jnp.float32).astype(mask_ref.dtype)
+
+
+def slot_mask(slots, pool):
+    return pl.pallas_call(
+        mask_kernel,
+        out_shape=jax.ShapeDtypeStruct((pool, slots.shape[0]), jnp.bfloat16),
+        in_specs=[pl.BlockSpec(memory_space=pltpu.VMEM)],
+        out_specs=pl.BlockSpec(memory_space=pltpu.VMEM),
+        cost_estimate=pl.CostEstimate(flops=10**8, bytes_accessed=10**6, transcendentals=0),
+    )(slots.T)
+
+
+def rows_of(matrix, parts):
+    lead = matrix.shape[:-2]
+    rows, columns = matrix.shape[-2:]
+    cut = matrix.reshape(-1, parts, rows // parts, columns // WIDTH, WIDTH)
+    return cut.transpose(1, 0, 3, 2, 4).reshape(parts, -1, WIDTH)
+
+
+def rows_back(shard, lead, rows, columns):
+    cut = shard.reshape(-1, columns // WIDTH, rows, WIDTH)
+    return cut.transpose(0, 2, 1, 3).reshape(lead + (rows, columns))
+
+
+def sum_matrices(matrices):
+    parts = lax.axis_size("dp")
+    packed = jnp.concatenate([rows_of(m, parts).astype(low_type) for m in matrices], 1)
+    shard = lax.psum_scatter(packed, "dp", scatter_dimension=0, tiled=True)[0]
+    total = lax.psum(shard, "section").astype(wide_type)
+    outs = []
+    at = 0
+    for m in matrices:
+        size = m.size // parts // WIDTH
+        outs.append(
+            rows_back(total[at : at + size], m.shape[:-2], m.shape[-2] // parts, m.shape[-1])
+        )
+        at += size
+    return outs
+
+
+def sum_vectors(vectors):
+    parts = lax.axis_size("dp")
+    flat = jnp.concatenate([v.reshape(-1) for v in vectors])
+    total = lax.psum(flat, ("dp", "section"))
+    mine = lax.axis_index("dp")
+    outs = []
+    at = 0
+    for v in vectors:
+        whole = total[at : at + v.size].reshape(v.shape)
+        at += v.size
+        size = v.shape[-1] // parts
+        outs.append(lax.dynamic_slice_in_dim(whole, mine * size, size, v.ndim - 1))
+    return outs
 
 
 def on_device(
@@ -460,26 +444,33 @@
         decoder_shrink_bias,
     )
     encoder_rows = encoder_input[0]
+    half_way = lax.axis_size("section") // 2
+    queries, width = decoder_input.shape[1:]
+    topk = retrieved.shape[2]
+    rows_low = shifted(jnp.concatenate([decoder_input[0], cotangent[0]], 0), "section", -half_way)
+    decoder_rows, cotangent_rows = rows_low[:queries], rows_low[queries:]
+    lengths_row = jnp.pad(decoder_lengths[0], ((0, 0), (0, topk - decoder_lengths.shape[2])))
+    integers = shifted(
+        jnp.concatenate([retrieved[0], pool_table[0, 0].reshape(-1, topk), lengths_row], 0),
+        "section",
+        -half_way,
+    )
+    retrieved_rows = integers[:queries]
+    owner_table = integers[queries:-1].reshape(pool_table.shape[2:])
+    lengths = integers[-1, : decoder_lengths.shape[2]]
     encoder_final, encoder_saved = encoder_pass(encoder_rows, encoder_weights)
-    half_way = lax.axis_size("section") // 2
-    arrived = shifted(encoder_final.astype(low_type), "section", half_way)
-    owner_table = pool_table[0, 0]
-    picked_rows = jnp.take(arrived, owner_table, axis=0)
+    states = encoder_final.astype(low_type)
+    picked_rows = jnp.take(states, owner_table, axis=0)
     fetched = lax.all_to_all(picked_rows, "dp", split_axis=0, concat_axis=0, tiled=True)
     owners, slot_count, feature_count = fetched.shape
     pooled = fetched.reshape(owners * slot_count, feature_count)
-    decoder_rows = decoder_input[0]
-    positions = jnp.arange(decoder_rows.shape[0], dtype=jnp.int32)
-    seq_ends = jnp.cumsum(decoder_lengths[0, 0], dtype=jnp.int32)
+    positions = jnp.arange(queries, dtype=jnp.int32)
+    seq_ends = jnp.cumsum(lengths, dtype=jnp.int32)
     segment_id = jnp.sum((positions[:, None] >= seq_ends[None, :-1]).astype(jnp.int32), 1)
     self_allowed = (segment_id[:, None] == segment_id[None, :]) & (
         positions[None, :] <= positions[:, None]
     )
-    cross_allowed = (
-        jnp.zeros((decoder_rows.shape[0], pooled.shape[0]), jnp.bool_)
-        .at[positions[:, None], retrieved[0]]
-        .set(True)
-    )
+    cross_allowed = slot_mask(retrieved_rows, pooled.shape[0]).T > 0
     decoder_final, decoder_saved = decoder_pass(
         decoder_rows, pooled, decoder_weights, self_allowed, cross_allowed
     )
@@ -503,7 +494,7 @@
         self_allowed,
         cross_allowed,
         decoder_saved,
-        cotangent[0].astype(wide_type),
+        cotangent_rows.astype(wide_type),
     )
     returned = lax.all_to_all(
         pooled_grad.astype(low_type).reshape(owners, slot_count, feature_count),
@@ -513,12 +504,12 @@
         tiled=True,
     )
     spread = (
-        jnp.arange(arrived.shape[0], dtype=jnp.int32)[:, None] == owner_table.reshape(1, -1)
+        jnp.arange(states.shape[0], dtype=jnp.int32)[:, None] == owner_table.reshape(1, -1)
     ).astype(low_type)
     state_grad = jnp.dot(
         spread, returned.reshape(-1, feature_count), preferred_element_type=wide_type
     )
-    encoder_incoming = shifted(state_grad.astype(low_type), "section", -half_way).astype(wide_type)
+    encoder_incoming = state_grad.astype(low_type).astype(wide_type)
     (
         encoder_grad,
         delta_encoder_inward,
@@ -530,30 +521,55 @@
         delta_encoder_shrink,
         delta_encoder_shrink_bias,
     ) = encoder_back(encoder_rows, encoder_weights, encoder_saved, encoder_incoming)
-    shares = (
-        lax.psum_scatter(delta_encoder_inward, "dp", scatter_dimension=1, tiled=True),
-        lax.psum_scatter(delta_encoder_outward, "dp", scatter_dimension=0, tiled=True),
-        lax.psum_scatter(delta_encoder_biases, "dp", scatter_dimension=1, tiled=True),
-        lax.psum_scatter(delta_encoder_norms, "dp", scatter_dimension=2, tiled=True),
-        lax.psum_scatter(delta_encoder_expand, "dp", scatter_dimension=0, tiled=True),
-        lax.psum_scatter(delta_encoder_expand_bias, "dp", scatter_dimension=0, tiled=True),
-        lax.psum_scatter(delta_encoder_shrink, "dp", scatter_dimension=0, tiled=True),
-        lax.psum_scatter(delta_encoder_shrink_bias, "dp", scatter_dimension=0, tiled=True),
-        lax.psum_scatter(delta_self_inward, "dp", scatter_dimension=1, tiled=True),
-        lax.psum_scatter(delta_self_outward, "dp", scatter_dimension=0, tiled=True),
-        lax.psum_scatter(delta_cross_inward, "dp", scatter_dimension=1, tiled=True),
-        lax.psum_scatter(delta_cross_outward, "dp", scatter_dimension=0, tiled=True),
-        lax.psum_scatter(delta_decoder_biases, "dp", scatter_dimension=1, tiled=True),
-        lax.psum_scatter(delta_decoder_norms, "dp", scatter_dimension=2, tiled=True),
-        lax.psum_scatter(delta_decoder_expand, "dp", scatter_dimension=0, tiled=True),
-        lax.psum_scatter(delta_decoder_expand_bias, "dp", scatter_dimension=0, tiled=True),
-        lax.psum_scatter(delta_decoder_shrink, "dp", scatter_dimension=0, tiled=True),
-        lax.psum_scatter(delta_decoder_shrink_bias, "dp", scatter_dimension=0, tiled=True),
-    )
-    results = tuple(encoder_section_total(tuple(shares[0:8]))) + tuple(
-        decoder_section_total(tuple(shares[8:18]))
-    )
-    return (decoder_final.astype(low_type)[None], encoder_grad[None], decoder_grad[None]) + results
+    decoder_matrices = sum_matrices(
+        [
+            delta_self_inward,
+            delta_self_outward,
+            delta_cross_inward,
+            delta_cross_outward,
+            delta_decoder_expand,
+            delta_decoder_shrink,
+        ]
+    )
+    feed_matrices = sum_matrices([delta_encoder_expand, delta_encoder_shrink])
+    attention_matrices = sum_matrices([delta_encoder_inward, delta_encoder_outward])
+    vectors = sum_vectors(
+        [
+            delta_encoder_biases,
+            delta_encoder_norms,
+            delta_encoder_expand_bias,
+            delta_encoder_shrink_bias,
+            delta_decoder_biases,
+            delta_decoder_norms,
+            delta_decoder_expand_bias,
+            delta_decoder_shrink_bias,
+        ]
+    )
+    decoder_out = shifted(decoder_final.astype(low_type), "section", half_way)
+    decoder_grad_out = shifted(decoder_grad, "section", half_way)
+    return (
+        decoder_out[None],
+        encoder_grad[None],
+        decoder_grad_out[None],
+        attention_matrices[0],
+        attention_matrices[1],
+        vectors[0],
+        vectors[1],
+        feed_matrices[0],
+        vectors[2],
+        feed_matrices[1],
+        vectors[3],
+        decoder_matrices[0],
+        decoder_matrices[1],
+        decoder_matrices[2],
+        decoder_matrices[3],
+        vectors[4],
+        vectors[5],
+        decoder_matrices[4],
+        vectors[6],
+        decoder_matrices[5],
+        vectors[7],
+    )
 
 
 def solution(mesh):

time: 2020 us -> 1030 us (0.51)
  local copies, waits for them, and re-layouts: 667 us -> 131 us
  blocking collectives: 222 us -> 0 us
  waiting for transfers between devices: 562 us -> 368 us
  other arithmetic: 137 us -> 110 us
  matrix products: 394 us -> 371 us
    unnamed x402 -> x376, local copies, waits for them, and re-layouts: 643 us -> 49.6 us
    unnamed x36 -> x5, waiting for transfers between devices: 225 us -> 0.08 us
    all_gather x10 -> x0, blocking collectives: 179 us -> none  [the longest x1 23.4 us: decoder_section_total(): lax.all_gather(matrix_parts[2].astype(jnp.bfloat16), 'section', axis=2, t...]
    psum x0 -> x2, waiting for transfers between devices: none -> 113 us  [the longest x1 113 us: sum_matrices(): total = lax.psum(shard, 'section').astype(wide_type)]
    ppermute x2 -> x4, waiting for transfers between devices: 121 us -> 38.5 us  [shifted(): lax.ppermute(value, axis, [(i, (i + by) % length) for i in range(length)])]
    reduce_scatter x12 -> x3, waiting for transfers between devices: 191 us -> 149 us  [sum_matrices(): shard = lax.psum_scatter(packed, 'dp', scatter_dimension=0, tiled=True)[0]]
    convert_element_type x0 -> x8, local copies, waits for them, and re-layouts: none -> 32 us  [the longest x7 30.2 us: sum_matrices(): rows_of(m, parts).astype(low_type)]
    all_to_all x1, waiting for transfers between devices: 0.01 us -> 30.2 us  [on_device(): lax.all_to_all(picked_rows, 'dp', split_axis=0, concat_axis=0, tiled=True)]
  transfers between devices with their start and end apart: 28 -> 11, of which waited for: 20 -> 6; matrix products, arithmetic and copies ran while one was open for 48% -> 28% of each run, Pallas kernels for 0% -> 0%
where the time goes in v1:
time: 1030 us; the launch traced here: 1020 us
  matrix products  371 us (36%)
  waiting for transfers between devices  368 us (36%)
  local copies, waits for them, and re-layouts  131 us (13%)
  other arithmetic  110 us (11%)
  between operations  18.1 us (2%)
  starting transfers between devices  16.5 us (2%)
    reduce_scatter x3, waiting for transfers between devices, sum_matrices(): shard = lax.psum_scatter(packed, 'dp', scatter_dimension=0, tiled=True)[0]  149 us
    psum x1, waiting for transfers between devices, sum_matrices(): total = lax.psum(shard, 'section').astype(wide_type)  113 us
    dot_general x16, matrix products, project(): return jnp.dot(left, right, preferred_element_type=wide_type)  90.1 us
    dot_general x16, matrix products, back_through(): lax.dot_general(incoming, right, (((1,), (1,)), ((), ())), preferred_elem...  60.6 us
    unnamed x376, local copies, waits for them, and re-layouts  49.6 us
    convert_element_type x4, other arithmetic, attend_backward(): scores_grad = (weights_full * (weights_grad - inner)).astype(low_type)  49.6 us
    dot_general x4, matrix products, attend_backward(): jnp.einsum('hqe,hke->hqk', grad_block, value_heads, preferred_element_typ...  44 us
    dot_general x16, matrix products, project_back(): lax.dot_general(left, incoming, (((0,), (0,)), ((), ())), preferred_eleme...  43.9 us
  transfers between devices with their start and end apart: 11, of which 6 were waited for; matrix products, arithmetic and copies ran while one was open for 28% of the time, Pallas kernels for 0%

profile of v1, /device:TPU:0, one launch (start us, length us, event | category | flops | bytes accessed | tf_op | source)
XLA Modules:
  0.0 1023.1 jit_solution(18050763474257803680)
XLA Ops:
  24.5 10.2 multiply_reduce_fusion.2
  34.6 10.1 multiply_reduce_fusion.3
  46.8 11.5 %fusion.1 = f32[12,512]{1,0:T(8,128)S(1)} fusion(f32[12,512,1024]{2,1,0:T(8,128)} %get-tuple-element.187, f32[12,512]{1,0:T(8,128)S(1)} %get-tuple-element.186), kind=kLoop, calls=%fused_computation.12 | loop fusion | flops 18868224 | bytes 25214976 | tf_op jit(solution)/shard_map/reduce_sum | solution.py:90
  58.4 10.8 %fusion.76 = bf16[12,512,64]{1,2,0:T(8,128)(2,1)S(1)} fusion(bf16[12,1024,64]{1,2,0:T(8,128)(2,1)S(1)} %bitcast.412, f32[12,512,1024]{2,1,0:T(8,128)} %get-tuple-element.187, f32[12,512]{1,0:T(8,128)S(1)} %fusion.1, f32[12,512]{1,0:T(8,128)S(1)} %get-tuple-element.186), kind=kOutput, calls=%fused_computation.160 | convolution fusion | flops 830865408 | bytes 27574272 | tf_op jit(solution)/shard_map/hqk,hke->hqe/dot_general | solution.py:93
  69.2 11.2 %fusion = f32[12,512]{1,0:T(8,128)S(1)} fusion(f32[12,512,1024]{2,1,0:T(8,128)} %get-tuple-element.189, f32[12,512]{1,0:T(8,128)S(1)} %get-tuple-element.188), kind=kLoop, calls=%fused_computation.11 | loop fusion | flops 18868224 | bytes 25214976 | tf_op jit(solution)/shard_map/reduce_sum | solution.py:90
  80.5 10.8 %fusion.77 = bf16[12,512,64]{1,2,0:T(8,128)(2,1)S(1)} fusion(bf16[12,1024,64]{1,2,0:T(8,128)(2,1)S(1)} %bitcast.413, f32[12,512,1024]{2,1,0:T(8,128)} %get-tuple-element.189, f32[12,512]{1,0:T(8,128)S(1)} %fusion, f32[12,512]{1,0:T(8,128)S(1)} %get-tuple-element.188), kind=kOutput, calls=%fused_computation.161 | convolution fusion | flops 830865408 | bytes 27574272 | tf_op jit(solution)/shard_map/hqk,hke->hqe/dot_general | solution.py:93
  96.1 35.8 %multiply_convert_fusion.3 = (bf16[1024,3072]{1,0:T(8,128)(2,1)}, f32[1024,3072]{1,0:T(8,128)}, f32[1024,3072]{1,0:T(8,128)}) fusion(f32[3072]{0:T(1024)S(1)} %copy-done.158, bf16[768,3072]{1,0:T(8,128)(2,1)S(1)} %bitcast.500, f32[1024,768]{0,1:T(8,128)S(1)} %get-tuple-element.191, f32[768]{0:T(1024)S(1)} %get-tuple-element.134, ...), kind=kOutput, calls=%fused_computation.31 | convolution fusion | flops 5043388416 | bytes 39348224 | tf_op jit(solution)/shard_map/dot_general | solution.py:39
  132.0 18.8 %fusion.200 = (f32[1024]{0:T(1024)S(1)}, f32[1024,768]{0,1:T(8,128)S(1)}) fusion(f32[768]{0:T(1024)S(1)} %copy-done.160, bf16[1024,3072]{1,0:T(8,128)(2,1)} %get-tuple-element.165, bf16[3072,768]{1,0:T(8,128)(2,1)S(1)} %bitcast.498, f32[768]{0:T(1024)S(1)} %get-tuple-element.134, f32[768]{0:T(1024)S(1)} %get-tuple-element.135, f32[1024]{0:T(1024)S(1)} %fusion.169, ...), kind=kOutput, calls=%fused_computation.399 | convolution fusion | flops 4837342208 | bytes 17323008 | tf_op jit(solution)/shard_map/dot_general | solution.py:39
  200.0 30.2 %all-to-all-done = bf16[8,256,768]{2,1,0:T(8,128)(2,1)} async-done(((bf16[8,256,768]{2,1,0:T(8,128)(2,1)}), bf16[8,256,768]{2,1,0:T(8,128)(2,1)}, u32[]{:S(2)}, u32[]{:S(2)}) %all-to-all-start) | async-done | bytes 3145760 | tf_op jit(solution)/shard_map/all_to_all | solution.py:464
  285.9 10.4 %multiply_reduce_fusion.4 = (f32[12,128]{1,0:T(8,128)S(1)}, f32[12,128,2048]{2,1,0:T(8,128)}) fusion(f32[12,128,2048]{2,1,0:T(8,128)} %copy-done.1, f32[12,128]{1,0:T(8,128)S(1)} %log_add_fusion.3, bf16[12,128,64]{1,2,0:T(8,128)(2,1)S(1)} %bitcast.452, bf16[12,2048,64]{1,2,0:T(8,128)(2,1)S(1)} %bitcast.438), kind=kOutput, calls=%fused_computation.26 | convolution fusion | flops 412088832 | bytes 28520448 | tf_op jit(solution)/shard_map/hqe,hke->hqk/dot_general | solution.py:109
  319.1 37.7 %all-to-all-done.1 = bf16[8,256,768]{2,1,0:T(8,128)(2,1)} async-done(((bf16[8,256,768]{2,1,0:T(8,128)(2,1)}), bf16[8,256,768]{2,1,0:T(8,128)(2,1)}, u32[]{:S(2)}, u32[]{:S(2)}) %all-to-all-start.1) | async-done | bytes 3145760 | tf_op jit(solution)/shard_map/all_to_all | solution.py:499
  369.6 19.1 %convert_reduce_fusion = (f32[3072]{0:T(1024)}, bf16[1024,3072]{1,0:T(8,128)(2,1)}) fusion(f32[1024,3072]{1,0:T(8,128)} %get-tuple-element.166, bf16[1024,768]{0,1:T(8,128)(2,1)} %get-tuple-element.152, bf16[3072,768]{1,0:T(8,128)(2,1)} %param.36, f32[1024,3072]{1,0:T(8,128)} %get-tuple-element.192, f32[3072]{0:T(1024)S(1)} %copy-done.159), kind=kOutput, calls=%fused_computation.21 | convolution fusion | flops 4885312512 | bytes 37773312 | tf_op jit(solution)/shard_map/dot_general | solution.py:49
  388.7 11.6 %multiply_reduce_fusion.5 = (f32[768]{0:T(1024)}, f32[1024]{0:T(1024)S(1)}, f32[768]{0:T(1024)}, f32[1024,768]{0,1:T(8,128)S(1)}) fusion(f32[1024,768]{0,1:T(8,128)} %copy-done.13, f32[1024]{0:T(1024)S(1)} %copy-done.133, f32[1024]{0:T(1024)S(1)} %copy-done.109, f32[768]{0:T(1024)S(1)} %copy-done.124, f32[1024]{0:T(1024)S(1)} %negate_multiply_fusion.3, ...), kind=kOutput, calls=%fused_computation.83 | convolution fusion | flops 4845204480 | bytes 22061056 | tf_op jit(solution)/shard_map/dot_general | solution.py:49
  405.0 12.3 %fusion.4 = f32[12,1024,64]{1,2,0:T(8,128)} fusion(f32[12,512,1024]{2,1,0:T(8,128)} %get-tuple-element.187, f32[12,512]{1,0:T(8,128)S(1)} %log_add_fusion, bf16[12,1024,64]{1,2,0:T(8,128)(2,1)S(1)} %bitcast.422), kind=kOutput, calls=%fused_computation.18 | convolution fusion | flops 824180736 | bytes 29130752 | tf_op jit(solution)/shard_map/hqk,hqe->hke/dot_general | solution.py:128
  417.2 16.7 %multiply_reduce_fusion = (f32[12,512]{1,0:T(8,128)}, f32[12,512,1024]{2,1,0:T(8,128)}) fusion(f32[12,512,1024]{2,1,0:T(8,128)} %get-tuple-element.187, f32[12,512]{1,0:T(8,128)S(1)} %log_add_fusion, bf16[12,1024,64]{1,2,0:T(8,128)(2,1)S(1)} %bitcast.414, bf16[12,1024,64]{1,2,0:T(8,128)(2,1)} %bitcast.423), kind=kOutput, calls=%fused_computation.2 | convolution fusion | flops 830466048 | bytes 52740096 | tf_op jit(solution)/shard_map/hqe,hke->hqk/dot_general | solution.py:109
  433.9 16.6 %multiply_reduce_fusion.1 = (f32[12,512]{1,0:T(8,128)S(1)}, f32[12,512,1024]{2,1,0:T(8,128)}) fusion(f32[12,512,1024]{2,1,0:T(8,128)} %get-tuple-element.189, f32[12,512]{1,0:T(8,128)S(1)} %log_add_fusion.1, bf16[12,1024,64]{1,2,0:T(8,128)(2,1)S(1)} %bitcast.415, bf16[12,1024,64]{1,2,0:T(8,128)(2,1)} %bitcast.424), kind=kOutput, calls=%fused_computation.5 | convolution fusion | flops 830466048 | bytes 52740096 | tf_op jit(solution)/shard_map/hqe,hke->hqk/dot_general | solution.py:109
  450.5 21.5 %multiply_convert_fusion.1 = bf16[12,512,1024]{2,1,0:T(8,128)(2,1)} fusion(f32[12,512,1024]{2,1,0:T(8,128)} %get-tuple-element.212, f32[12,512,1024]{2,1,0:T(8,128)} %get-tuple-element.189, f32[12,512]{1,0:T(8,128)S(1)} %get-tuple-element.211, f32[12,512]{1,0:T(8,128)S(1)} %log_add_fusion.1), kind=kLoop, calls=%fused_computation.4 | loop fusion | flops 31457280 | bytes 62963712 | tf_op jit(solution)/shard_map/convert_element_type | solution.py:113
  492.4 11.8 %convert_reduce_fusion.5 = (f32[12,64]{1,0:T(8,128)}, bf16[12,1024,64]{1,2,0:T(8,128)(2,1)S(1)}) fusion(f32[12,1024,64]{1,2,0:T(8,128)S(1)} %copy-done.15, f32[12,512,1024]{2,1,0:T(8,128)} %get-tuple-element.189, f32[12,512]{1,0:T(8,128)S(1)} %copy-done.85, bf16[12,1024,64]{1,2,0:T(8,128)(2,1)S(1)} %bitcast.425), kind=kOutput, calls=%fused_computation.85 | convolution fusion | flops 827325696 | bytes 30706688 | tf_op jit(solution)/shard_map/hqk,hqe->hke/dot_general | solution.py:128
  506.7 21.5 %multiply_convert_fusion = bf16[12,512,1024]{2,1,0:T(8,128)(2,1)} fusion(f32[12,512,1024]{2,1,0:T(8,128)} %get-tuple-element.214, f32[12,512,1024]{2,1,0:T(8,128)} %get-tuple-element.187, f32[12,512]{1,0:T(8,128)S(1)} %copy-done.98, f32[12,512]{1,0:T(8,128)S(1)} %copy-done.87), kind=kLoop, calls=%fused_computation.1 | loop fusion | flops 31457280 | bytes 62963712 | tf_op jit(solution)/shard_map/convert_element_type | solution.py:113
  556.3 10.0 convolution_convert_fusion.1
  672.0 18.0 %reduce-scatter.6.cloned.1.call-done = bf16[1,768,768]{2,1,0:T(8,128)(2,1)} async-done(((bf16[8,768,768]{2,1,0:T(8,128)(2,1)}), bf16[1,768,768]{2,1,0:T(8,128)(2,1)}) %reduce-scatter.6.cloned.1.call-update) | async-done | bytes 1179664 | tf_op jit(solution)/shard_map/reduce_scatter | solution.py:370
  689.9 130.7 %reduce-scatter.8.cloned.1.call-done = bf16[1,1536,768]{2,1,0:T(8,128)(2,1)} async-done(((bf16[8,1536,768]{2,1,0:T(8,128)(2,1)}), bf16[1,1536,768]{2,1,0:T(8,128)(2,1)}) %reduce-scatter.8.cloned.1.call-update) | async-done | bytes 2359312 | tf_op jit(solution)/shard_map/reduce_scatter | solution.py:370
  829.3 38.5 %collective-permute-done.2 = bf16[128,768]{1,0:T(8,128)(2,1)} collective-permute-done((bf16[128,768]{1,0:T(8,128)(2,1)}, bf16[128,768]{1,0:T(8,128)(2,1)}, u32[]{:S(2)}, u32[]{:S(2)}) %collective-permute-start.2) | collective-permute-done | bytes 196640 | tf_op jit(solution)/shard_map/ppermute | solution.py:20
  888.0 112.7 %all-reduce.17.cloned.1.call-done = (bf16[384,768]{1,0:T(8,128)(2,1)}, bf16[768,768]{1,0:T(8,128)(2,1)}, bf16[1536,768]{1,0:T(8,128)(2,1)}) async-done(((bf16[384,768]{1,0:T(8,128)(2,1)}, bf16[768,768]{1,0:T(8,128)(2,1)}, bf16[1536,768]{1,0:T(8,128)(2,1)}), (bf16[384,768]{1,0:T(8,128)(2,1)}, bf16[768,768]{1,0:T(8,128)(2,1)}, bf16[1536,768]{1,0:T(8,128)(2,1)})) %all-reduce.17.cloned.1.call-update) | async-done | bytes 4128784 | tf_op jit(solution)/shard_map/psum | solution.py:371
  (614 shorter events, 366.5 us)
Async XLA Ops:
  8.0 83.5 %copy-start = (bf16[768,768]{1,0:T(8,128)(2,1)S(1)}, bf16[768,768]{1,0:T(8,128)(2,1)}, u32[]{:S(2)}) copy-start(bf16[768,768]{1,0:T(8,128)(2,1)} %param.31) | copy-start | bytes 3538948
  10.0 146.0 %collective-permute-start = (bf16[256,768]{1,0:T(8,128)(2,1)}, bf16[256,768]{1,0:T(8,128)(2,1)}, u32[]{:S(2)}, u32[]{:S(2)}) collective-permute-start(bf16[256,768]{1,0:T(8,128)(2,1)} %pad_maximum_fusion.4), channel_id=1, source_target_pairs={{0,2},{1,3},{2,0},{3,1},{4,6},{5,7},{6,4},{7,5},{8,10},{9,11},{10,... | collective-permute-start | bytes 1179656 | tf_op jit(solution)/shard_map/ppermute | solution.py:20
  16.7 146.3 %collective-permute-start.1 = (s32[131,1024]{1,0:T(8,128)}, s32[131,1024]{1,0:T(8,128)}, u32[]{:S(2)}, u32[]{:S(2)}) collective-permute-start(s32[131,1024]{1,0:T(8,128)} %pad_add_fusion), channel_id=1, source_target_pairs={{0,2},{1,3},{2,0},{3,1},{4,6},{5,7},{6,4},{7,5},{8,10},{9,11},{10,... | collective-permute-start | bytes 1609736 | tf_op jit(solution)/shard_map/ppermute | solution.py:20
  45.4 86.5 %copy-start.123 = (f32[768]{0:T(1024)}, f32[768]{0:T(1024)S(1)}, u32[]{:S(2)}) copy-start(f32[768]{0:T(1024)S(1)} %get-tuple-element.135) | copy-start | bytes 9220
  45.4 86.5 %copy-start.143 = (f32[768]{0:T(1024)}, f32[768]{0:T(1024)S(1)}, u32[]{:S(2)}) copy-start(f32[768]{0:T(1024)S(1)} %get-tuple-element.134) | copy-start | bytes 9220
  155.9 102.2 %copy-start.110 = (f32[768]{0:T(1024)}, f32[768]{0:T(1024)S(1)}, u32[]{:S(2)}) copy-start(f32[768]{0:T(1024)S(1)} %get-tuple-element.130) | copy-start | bytes 9220
  155.9 102.2 %copy-start.112 = (f32[768]{0:T(1024)}, f32[768]{0:T(1024)S(1)}, u32[]{:S(2)}) copy-start(f32[768]{0:T(1024)S(1)} %get-tuple-element.131) | copy-start | bytes 9220
  155.9 108.9 %copy-start.96 = (f32[768]{0:T(1024)}, f32[768]{0:T(1024)S(1)}, u32[]{:S(2)}) copy-start(f32[768]{0:T(1024)S(1)} %get-tuple-element.128) | copy-start | bytes 9220
  155.9 119.6 %copy-start.94 = (f32[768]{0:T(1024)}, f32[768]{0:T(1024)S(1)}, u32[]{:S(2)}) copy-start(f32[768]{0:T(1024)S(1)} %get-tuple-element.129) | copy-start | bytes 9220
  187.7 42.5 %all-to-all-start = ((bf16[8,256,768]{2,1,0:T(8,128)(2,1)}), bf16[8,256,768]{2,1,0:T(8,128)(2,1)}, u32[]{:S(2)}, u32[]{:S(2)}) async-start(bf16[8,256,768]{2,1,0:T(8,128)(2,1)} %broadcast_select_fusion), calls=%async_computation | async-start | bytes 6291456 | tf_op jit(solution)/shard_map/all_to_all | solution.py:464
  197.9 60.2 %copy-start.23 = (f32[128,768]{1,0:T(8,128)}, f32[128,768]{1,0:T(8,128)S(1)}, u32[]{:S(2)}) copy-start(f32[128,768]{1,0:T(8,128)S(1)} %get-tuple-element.198) | copy-start | bytes 1179652
  314.3 42.5 %all-to-all-start.1 = ((bf16[8,256,768]{2,1,0:T(8,128)(2,1)}), bf16[8,256,768]{2,1,0:T(8,128)(2,1)}, u32[]{:S(2)}, u32[]{:S(2)}) async-start(bf16[8,256,768]{2,1,0:T(8,128)(2,1)} %bitcast.444), calls=%async_computation.1 | async-start | bytes 6291456 | tf_op jit(solution)/shard_map/all_to_all | solution.py:499
  319.0 353.0 %reduce-scatter.4.cloned.1.call-start = ((), (), s32[]{:S(2)}) async-start(), calls=%async_computation.5 | async-start | bytes 5308416 | tf_op jit(solution)/shard_map/reduce_scatter | solution.py:370
  319.1 98.2 %copy-start.86 = (f32[12,512]{1,0:T(8,128)}, f32[12,512]{1,0:T(8,128)S(1)}, u32[]{:S(2)}) copy-start(f32[12,512]{1,0:T(8,128)S(1)} %log_add_fusion) | copy-start | bytes 73732
  319.1 131.4 %copy-start.84 = (f32[12,512]{1,0:T(8,128)}, f32[12,512]{1,0:T(8,128)S(1)}, u32[]{:S(2)}) copy-start(f32[12,512]{1,0:T(8,128)S(1)} %log_add_fusion.1) | copy-start | bytes 73732
  481.1 64.8 %copy-start.38 = (bf16[12,512,64]{1,2,0:T(8,128)(2,1)}, bf16[12,512,64]{1,2,0:T(8,128)(2,1)S(1)}, u32[]{:S(2)}) copy-start(bf16[12,512,64]{1,2,0:T(8,128)(2,1)S(1)} %multiply_convert_fusion.7) | copy-start | bytes 2359300
  555.7 134.2 %reduce-scatter.6.cloned.1.call-start = ((), (), s32[]{:S(2)}) async-start(), calls=%async_computation.7 | async-start | bytes 10616832 | tf_op jit(solution)/shard_map/reduce_scatter | solution.py:370
  590.6 230.0 %reduce-scatter.8.cloned.1.call-start = ((), (), s32[]{:S(2)}) async-start(), calls=%async_computation.8 | async-start | bytes 21233664 | tf_op jit(solution)/shard_map/reduce_scatter | solution.py:370
  655.8 224.0 %all-reduce.15.cloned.1.call-start = ((), (), s32[]{:S(2)}) async-start(), calls=%async_computation.6 | async-start | bytes 180224 | tf_op jit(solution)/shard_map/psum | solution.py:386
  657.5 163.2 %copy-start.57 = (bf16[12,128,64]{1,2,0:T(8,128)(2,1)S(1)}, bf16[12,128,64]{1,2,0:T(8,128)(2,1)}, u32[]{:S(2)}) copy-start(bf16[12,128,64]{1,2,0:T(8,128)(2,1)} %copy-done.56) | copy-start | bytes 589828
  660.4 162.3 %copy-start.49 = (bf16[12,128,64]{1,2,0:T(8,128)(2,1)S(1)}, bf16[12,128,64]{1,2,0:T(8,128)(2,1)}, u32[]{:S(2)}) copy-start(bf16[12,128,64]{1,2,0:T(8,128)(2,1)} %copy-done.48) | copy-start | bytes 589828
  671.9 328.8 %all-reduce.17.cloned.1.call-start = ((), (), s32[]{:S(2)}) async-start(), calls=%async_computation.9 | async-start | bytes 8257536 | tf_op jit(solution)/shard_map/psum | solution.py:371
  826.3 41.5 %collective-permute-start.3 = (f32[128,768]{1,0:T(8,128)S(1)}, f32[128,768]{1,0:T(8,128)S(1)}, u32[]{:S(2)}, u32[]{:S(2)}) collective-permute-start(f32[128,768]{1,0:T(8,128)S(1)} %fusion.80), channel_id=1, source_target_pairs={{0,2},{1,3},{2,0},{3,1},{4,6},{5,7},{6,4},{7,5},{8,10},{9,11},{10,... | collective-permute-start | bytes 1179656 | tf_op jit(solution)/shard_map/ppermute | solution.py:20
  828.8 39.0 %collective-permute-start.2 = (bf16[128,768]{1,0:T(8,128)(2,1)}, bf16[128,768]{1,0:T(8,128)(2,1)}, u32[]{:S(2)}, u32[]{:S(2)}) collective-permute-start(bf16[128,768]{1,0:T(8,128)(2,1)} %get-tuple-element.178), channel_id=1, source_target_pairs={{0,2},{1,3},{2,0},{3,1},{4,6},{5,7},{6,4},{7,5},{8,10},{9,11},{10,... | collective-permute-start | bytes 589832 | tf_op jit(solution)/shard_map/ppermute | solution.py:20
  (165 other events, 1357.5 us)
Sparse Core Ops, SparseCore 0:
  555.8 53.6 reduce-scatter.3
  613.4 76.5 reduce-scatter.5
  694.0 126.6 reduce-scatter.7
Sparse Core Ops, SparseCore 1:
  672.0 156.5 all-reduce.14
  831.2 169.5 all-reduce.16

commit v2 on v1

v2 whole, which is shorter than its diff:
```python
import functools

import jax
import jax.numpy as jnp
from jax import lax
from jax.experimental import pallas as pl
from jax.experimental.pallas import tpu as pltpu
from jax.sharding import PartitionSpec as P

HEAD = 64
WIDTH = 768


norm_eps = 1e-05
scale_scores = 0.125
low_type = jnp.bfloat16
wide_type = jnp.float32

NN = (((1,), (0,)), ((), ()))
NT = (((1,), (1,)), ((), ()))
TN = (((0,), (0,)), ((), ()))
GROUP = 256
VMEM = pltpu.VMEM


def dot(left, right, dims=NN):
    return lax.dot_general(left, right, dims, preferred_element_type=wide_type)


def low(value):
    return value.astype(low_type)


def wide(value):
    return value.astype(wide_type)


def head_lanes(dtype):
    lane = lax.broadcasted_iota(jnp.int32, (1, GROUP), 1) // HEAD
    return [(lane == h).astype(wide_type).astype(dtype) for h in range(GROUP // HEAD)]


def centred_of(values):
    centred = values - jnp.mean(values, -1, keepdims=True)
    spread = jnp.mean(centred * centred, -1, keepdims=True)
    return centred, lax.rsqrt(spread + norm_eps)


def norm_rows(values, gain, offset):
    centred, scale = centred_of(values)
    return centred * scale * (1.0 + gain) + offset


def norm_rows_back(values, gain, incoming):
    centred, scale = centred_of(values)
    unit = centred * scale
    inner = incoming * (1.0 + gain)
    mean_inner = jnp.mean(inner, -1, keepdims=True)
    mean_along = jnp.mean(inner * unit, -1, keepdims=True)
    return (
        scale * (inner - mean_inner - unit * mean_along),
        jnp.sum(incoming * unit, 0, keepdims=True),
        jnp.sum(incoming, 0, keepdims=True),
    )


def gelu_parts(u):
    size = jnp.abs(u) * 0.7071067811865476
    t = 1.0 / (1.0 + 0.3275911 * size)
    bell = jnp.exp(-0.5 * u * u)
    series = t * (
        0.254829592
        + t * (-0.284496736 + t * (1.421413741 + t * (-1.453152027 + t * 1.061405429)))
    )
    tail = 0.5 * series * bell
    share = jnp.where(u < 0.0, tail, 1.0 - tail)
    return u * share, share + u * (bell * 0.3989422804014327)


def params(limit=60, **rest):
    return pltpu.CompilerParams(vmem_limit_bytes=limit * 2**20, **rest)


def cost(flops, size, exps=0):
    return pl.CostEstimate(flops=int(flops), bytes_accessed=int(size), transcendentals=int(exps))


def full(*shape):
    return pl.BlockSpec(shape, lambda *_: (0,) * len(shape))


def like(shape, dtype):
    return jax.ShapeDtypeStruct(shape, dtype)


def paired():
    return lax.axis_size("dp") == 8


def grad_shapes(parts, rows, columns):
    if paired():
        return [like((4, parts * rows // 8, columns), low_type)] * 2
    return [like((parts, rows, columns), low_type)]


def grad_specs(parts, rows, columns, index=None):
    if paired():
        block, count = (4, parts * rows // 8, columns), 2
    else:
        block, count = (parts, rows, columns), 1
    return [pl.BlockSpec(block, index or (lambda *_: (0, 0, 0)))] * count


def emit(outs, part, hold):
    if len(outs) == 1:
        outs[0][part] = low(hold[...])
        return
    keep, send = outs
    me = lax.axis_index("dp")
    rows = hold.shape[0] // 8
    to = pl.ds(pl.multiple_of(part * rows, rows), rows)
    for at in range(4):
        mine = pl.multiple_of((me ^ (2 * at)) * rows, rows)
        other = pl.multiple_of((me ^ (2 * at + 1)) * rows, rows)
        keep[at, to, :] = low(hold[pl.ds(mine, rows), :])
        send[at, to, :] = low(hold[pl.ds(other, rows), :])


def emit_tall(outs, block, hold):
    if len(outs) == 1:
        size = hold.shape[0]
        outs[0][0, pl.ds(pl.multiple_of(block * size, size), size), :] = low(hold[...])
        return
    keep, send = outs
    me = lax.axis_index("dp")
    rows = hold.shape[0] // 2
    at = block ^ lax.shift_right_logical(me, 1)
    core = me & 1
    keep[at, 0:rows, :] = low(hold[pl.ds(pl.multiple_of(core * rows, rows), rows), :])
    send[at, 0:rows, :] = low(hold[pl.ds(pl.multiple_of((1 - core) * rows, rows), rows), :])


def thirds(items):
    third = len(items) // 3
    return items[:third], items[third : 2 * third], items[2 * third :]


def encoder_attend_kernel(
    x_ref, w_ref, wo_ref, bg_ref, b_ref, qkv_ref, c_ref, stat_ref, mixed_ref, stats
):
    group = pl.program_id(0)
    tokens = x_ref.shape[0]
    block = 256
    x = x_ref[...]
    qkv_ref[0] = low(dot(x, w_ref[0]) + bg_ref[0:1])
    qkv_ref[1] = low(dot(x, w_ref[1]))
    qkv_ref[2] = low(dot(x, w_ref[2]) + bg_ref[1:2])
    lanes_low, lanes = head_lanes(low_type), head_lanes(wide_type)
    lane = lax.broadcasted_iota(jnp.int32, (1, 128), 1)

    @pl.when(group == 0)
    def _():
        mixed_ref[...] = wide(x) + b_ref[2:3]

    def rows_step(i, carry):
        rows = pl.ds(pl.multiple_of(i * block, block), block)
        q = qkv_ref[0, rows, :] * jnp.asarray(scale_scores, low_type)
        context = jnp.zeros((block, GROUP), wide_type)
        stat = jnp.zeros((block, 128), wide_type)
        for h in range(GROUP // HEAD):
            scores = dot(q * lanes_low[h], qkv_ref[1], NT)
            top = jnp.max(scores, -1, keepdims=True)
            weights = jnp.exp(scores - top)
            total = jnp.sum(weights, -1, keepdims=True)
            context += dot(low(weights), qkv_ref[2]) * (lanes[h] * (1.0 / total))
            stat = jnp.where(lane == h, top + jnp.log(total), stat)
        c_ref[rows, :] = context
        stats[rows, :] = stat
        mixed_ref[rows, :] += dot(low(context), wo_ref[...])
        return carry

    lax.fori_loop(0, tokens // block, rows_step, 0)
    stat_ref[0] = stats[...].T[0:8]


def encoder_attend(x, inward, outward, biases):
    tokens, width = x.shape
    groups = width // GROUP
    return pl.pallas_call(
        encoder_attend_kernel,
        grid=(groups,),
        in_specs=[
            full(tokens, width),
            pl.BlockSpec((3, width, GROUP), lambda g: (0, 0, g)),
            pl.BlockSpec((GROUP, width), lambda g: (g, 0)),
            pl.BlockSpec((3, GROUP), lambda g: (0, g)),
            full(3, width),
        ],
        out_specs=[
            pl.BlockSpec((3, tokens, GROUP), lambda g: (0, 0, g)),
            pl.BlockSpec((tokens, GROUP), lambda g: (0, g)),
            pl.BlockSpec((1, 8, tokens), lambda g: (g, 0, 0)),
            full(tokens, width),
        ],
        out_shape=[
            like((3, tokens, width), low_type),
            like((tokens, width), wide_type),
            like((groups, 8, tokens), wide_type),
            like((tokens, width), wide_type),
        ],
        scratch_shapes=[VMEM((tokens, 128), wide_type)],
        compiler_params=params(),
        cost_estimate=cost(3e10, 2e7, 1.3e7),
        name="encoder_attend",
    )(x, inward, outward, biases, biases)


def encoder_feed_kernel(
    mixed_ref, n_ref, e_ref, eb_ref, s_ref, sb_ref, h_ref, d_ref, sum_ref, out_ref, a_low
):
    step = pl.program_id(0)
    tokens = mixed_ref.shape[0]
    block = 256

    @pl.when(step == 0)
    def _():
        first = norm_rows(mixed_ref[...], n_ref[0, 0:1], n_ref[0, 1:2])
        a_low[...] = low(first)
        sum_ref[...] = first + sb_ref[...]

    for i in range(tokens // block):
        rows = slice(i * block, (i + 1) * block)
        hidden, slope = gelu_parts(dot(a_low[rows, :], e_ref[...]) + eb_ref[...])
        h_ref[rows, :] = low(hidden)
        d_ref[rows, :] = low(slope)
        sum_ref[rows, :] += dot(low(hidden), s_ref[...])

    @pl.when(step == pl.num_programs(0) - 1)
    def _():
        out_ref[...] = low(norm_rows(sum_ref[...], n_ref[1, 0:1], n_ref[1, 1:2]))


def encoder_feed(mixed, norms, expand, expand_bias, shrink, shrink_bias):
    tokens, width = mixed.shape
    hidden = expand.shape[1]
    cut = hidden // 4
    return pl.pallas_call(
        encoder_feed_kernel,
        grid=(4,),
        in_specs=[
            full(tokens, width),
            full(2, 2, width),
            pl.BlockSpec((width, cut), lambda i: (0, i)),
            pl.BlockSpec((1, cut), lambda i: (0, i)),
            pl.BlockSpec((cut, width), lambda i: (i, 0)),
            full(1, width),
        ],
        out_specs=[
            pl.BlockSpec((tokens, cut), lambda i: (0, i)),
            pl.BlockSpec((tokens, cut), lambda i: (0, i)),
            full(tokens, width),
            full(tokens, width),
        ],
        out_shape=[
            like((tokens, hidden), low_type),
            like((tokens, hidden), low_type),
            like((tokens, width), wide_type),
            like((tokens, width), low_type),
        ],
        scratch_shapes=[VMEM((tokens, width), low_type)],
        compiler_params=params(),
        cost_estimate=cost(2e10, 3e7, 3e6),
        name="encoder_feed",
    )(mixed, norms, expand, expand_bias[None], shrink, shrink_bias[None])


def encoder_feed_back_kernel(
    g_ref, sum_ref, mixed_ref, h_ref, d_ref, c_ref, n_ref, e_ref, s_ref, *rest
):
    dmix_ref, vec_ref, eb_ref = rest[:3]
    back_low, a_turned, between, hold = rest[-4:]
    wide_outs, tall_outs, out_outs = thirds(rest[3:-4])
    step = pl.program_id(0)
    tokens = sum_ref.shape[0]
    block = 256

    @pl.when(step == 0)
    def _():
        grad, gain, offset = norm_rows_back(sum_ref[...], n_ref[1, 0:1], wide(g_ref[...]))
        dmix_ref[...] = grad
        back_low[...] = low(grad)
        vec_ref[...] = jnp.zeros(vec_ref.shape, wide_type)
        vec_ref[0:1] = gain
        vec_ref[1:2] = offset
        vec_ref[2:3] = jnp.sum(wide(back_low[...]), 0, keepdims=True)
        a_turned[...] = low(norm_rows(mixed_ref[...], n_ref[0, 0:1], n_ref[0, 1:2])).T

    column = jnp.zeros(eb_ref.shape, wide_type)
    for i in range(tokens // block):
        rows = slice(i * block, (i + 1) * block)
        before = low(dot(back_low[rows, :], s_ref[...], NT) * wide(d_ref[rows, :]))
        between[rows, :] = before
        column += jnp.sum(wide(before), 0, keepdims=True)
        dmix_ref[rows, :] += dot(before, e_ref[...], NT)
    eb_ref[...] = column
    hold[...] = dot(a_turned[...], between[...])
    emit(wide_outs, step, hold)
    hold[...] = dot(h_ref[...], back_low[...], TN)
    emit_tall(tall_outs, step, hold)

    @pl.when(step == pl.num_programs(0) - 1)
    def _():
        grad, gain, offset = norm_rows_back(mixed_ref[...], n_ref[0, 0:1], dmix_ref[...])
        dmix_ref[...] = grad
        back_low[...] = low(grad)
        vec_ref[3:4] = gain
        vec_ref[4:5] = offset
        vec_ref[5:6] = jnp.sum(wide(back_low[...]), 0, keepdims=True)
        hold[...] = dot(low(c_ref[...]), back_low[...], TN)
        emit(out_outs, 0, hold)


def encoder_feed_back(grad, summed, mixed, hidden, slope, context, norms, expand, shrink):
    tokens, width = mixed.shape
    total = expand.shape[1]
    cut = total // 4
    outs = pl.pallas_call(
        encoder_feed_back_kernel,
        grid=(4,),
        in_specs=[
            full(tokens, width),
            full(tokens, width),
            full(tokens, width),
            pl.BlockSpec((tokens, cut), lambda i: (0, i)),
            pl.BlockSpec((tokens, cut), lambda i: (0, i)),
            full(tokens, width),
            full(2, 2, width),
            pl.BlockSpec((width, cut), lambda i: (0, i)),
            pl.BlockSpec((cut, width), lambda i: (i, 0)),
        ],
        out_specs=[
            full(tokens, width),
            full(8, width),
            pl.BlockSpec((1, cut), lambda i: (0, i)),
            *grad_specs(4, width, width),
            *grad_specs(1, total, width),
            *grad_specs(1, width, width),
        ],
        out_shape=[
            like((tokens, width), wide_type),
            like((8, width), wide_type),
            like((1, total), wide_type),
            *grad_shapes(4, width, width),
            *grad_shapes(1, total, width),
            *grad_shapes(1, width, width),
        ],
        scratch_shapes=[
            VMEM((tokens, width), low_type),
            VMEM((width, tokens), low_type),
            VMEM((tokens, cut), low_type),
            VMEM((width, width), wide_type),
        ],
        compiler_params=params(),
        cost_estimate=cost(4e10, 5e7),
        name="encoder_feed_back",
    )(grad, summed, mixed, hidden, slope, context, norms, expand, shrink)
    return outs[:3], thirds(outs[3:])


def encoder_attend_back_kernel(
    dmix_ref, x_ref, qkv_ref, c_ref, stat_ref, w_ref, wo_ref, *rest
):
    dx_ref, vec_ref = rest[:2]
    outs, (dmix_low, x_turned, dc, weights, scores_back, dk, dv, dq_turned, hold) = (
        rest[2:-9],
        rest[-9:],
    )
    group = pl.program_id(0)
    tokens = x_ref.shape[0]
    block = 256
    heads = GROUP // HEAD

    @pl.when(group == 0)
    def _():
        dx_ref[...] = dmix_ref[...]
        dmix_low[...] = low(dmix_ref[...])
        x_turned[...] = x_ref[...].T

    dc[...] = low(dot(dmix_low[...], wo_ref[...], NT))
    lanes_low = head_lanes(low_type)
    eighth = jnp.asarray(scale_scores, low_type)
    pick = (
        lax.broadcasted_iota(jnp.int32, (8, GROUP), 1) // HEAD
        == lax.broadcasted_iota(jnp.int32, (8, GROUP), 0)
    ).astype(wide_type)
    pick = low(pick)
    product = wide(dc[...]) * c_ref[...]
    product_high = low(product)
    product_rest = low(product - wide(product_high))
    inner = dot(pick, product_high, NT) + dot(pick, product_rest, NT)
    k_turned = qkv_ref[1].T
    dk[...] = jnp.zeros(dk.shape, wide_type)
    dv[...] = jnp.zeros(dv.shape, wide_type)
    for i in range(tokens // block):
        rows = slice(i * block, (i + 1) * block)
        q = qkv_ref[0, rows, :] * eighth
        q_heads = jnp.concatenate([q * lanes_low[h] for h in range(heads)], 0)
        dc_heads = jnp.concatenate([dc[rows, :] * lanes_low[h] for h in range(heads)], 0)
        for h in range(heads):
            part = slice(h * block, (h + 1) * block)
            scores = dot(qkv_ref[1], q_heads[part], NT)
            weight = jnp.exp(scores - stat_ref[0, h : h + 1, rows])
            weight_back = dot(qkv_ref[2], dc_heads[part], NT)
            weights[:, part] = low(weight)
            back = low(weight * (weight_back - inner[h : h + 1, rows]))
            scores_back[:, part] = back
            dq_turned[h * HEAD : (h + 1) * HEAD, rows] = dot(
                k_turned[h * HEAD : (h + 1) * HEAD], back
            )
        dv[...] += dot(weights[...], dc_heads)
        dk[...] += dot(scores_back[...], q_heads)
    dq = low(dq_turned[...].T * scale_scores)
    dk_low, dv_low = low(dk[...]), low(dv[...])
    vec_ref[...] = jnp.zeros(vec_ref.shape, wide_type)
    vec_ref[0:1] = jnp.sum(wide(dq), 0, keepdims=True)
    vec_ref[1:2] = jnp.sum(wide(dv_low), 0, keepdims=True)
    dx_ref[...] += (
        dot(dq, w_ref[0], NT) + dot(dk_low, w_ref[1], NT) + dot(dv_low, w_ref[2], NT)
    )
    for part, grad in enumerate((dq, dk_low, dv_low)):
        hold[...] = dot(x_turned[...], grad)
        emit(outs, part, hold)


def encoder_attend_back(dmix, x, qkv, context, stats, inward, outward):
    tokens, width = x.shape
    groups = width // GROUP
    specs = grad_specs(3, width, GROUP, lambda g: (0, 0, g))
    outs = pl.pallas_call(
        encoder_attend_back_kernel,
        grid=(groups,),
        in_specs=[
            full(tokens, width),
            full(tokens, width),
            pl.BlockSpec((3, tokens, GROUP), lambda g: (0, 0, g)),
            pl.BlockSpec((tokens, GROUP), lambda g: (0, g)),
            pl.BlockSpec((1, 8, tokens), lambda g: (g, 0, 0)),
            pl.BlockSpec((3, width, GROUP), lambda g: (0, 0, g)),
            pl.BlockSpec((GROUP, width), lambda g: (g, 0)),
        ],
        out_specs=[
            full(tokens, width),
            pl.BlockSpec((8, GROUP), lambda g: (0, g)),
            *specs,
        ],
        out_shape=[
            like((tokens, width), wide_type),
            like((8, width), wide_type),
            *grad_shapes(3, width, width),
        ],
        scratch_shapes=[
            VMEM((tokens, width), low_type),
            VMEM((width, tokens), low_type),
            VMEM((tokens, GROUP), low_type),
            VMEM((tokens, 4 * 256), low_type),
            VMEM((tokens, 4 * 256), low_type),
            VMEM((tokens, GROUP), wide_type),
            VMEM((tokens, GROUP), wide_type),
            VMEM((GROUP, tokens), wide_type),
            VMEM((width, GROUP), wide_type),
        ],
        compiler_params=params(),
        cost_estimate=cost(5e10, 4e7, 1.3e7),
        name="encoder_attend_back",
    )(dmix, x, qkv, context, stats, inward, outward)
    return outs[:2], outs[2:]


def mask_kernel(slots_ref, across_ref, down_ref):
    count, width = slots_ref.shape
    words = down_ref.shape[0] // 32
    block = 32
    row = lax.broadcasted_iota(jnp.int32, (32, width), 0)
    for start in range(0, words, block):

        def step(i, totals):
            piece = slots_ref[pl.ds(pl.multiple_of(i * 8, 8), 8), :]
            word = lax.shift_right_logical(piece, 5)
            bit = jnp.left_shift(jnp.int32(1), piece & 31)
            return tuple(
                total | jnp.where(word == start + w, bit, 0) for w, total in enumerate(totals)
            )

        zero = jnp.zeros((8, width), jnp.int32)
        totals = lax.fori_loop(0, count // 8, step, (zero,) * block)
        for w, total in enumerate(totals):
            joined = total[0:1]
            for k in range(1, 8):
                joined = joined | total[k : k + 1]
            bits = lax.shift_right_logical(jnp.broadcast_to(joined, (32, width)), row) & 1
            at = (start + w) * 32
            down_ref[at : at + 32, :] = (wide(bits) - 1.0) * 1e30
    across_ref[...] = down_ref[...].T


def slot_mask(slots, pool):
    queries = slots.shape[0]
    return pl.pallas_call(
        mask_kernel,
        out_shape=[like((queries, pool), wide_type), like((pool, queries), wide_type)],
        in_specs=[pl.BlockSpec(memory_space=VMEM)],
        out_specs=[pl.BlockSpec(memory_space=VMEM)] * 2,
        compiler_params=params(24),
        cost_estimate=cost(1e10, 1e6),
        name="slot_mask",
    )(slots.T)


def pick_kernel(table_ref, states_ref, out_ref):
    spot = lax.broadcasted_iota(jnp.int32, (table_ref.shape[0], states_ref.shape[0]), 1)
    chosen = low((spot == table_ref[...]).astype(wide_type))
    out_ref[...] = low(dot(chosen, states_ref[...]))


def pick_rows(table, states):
    tokens, width = states.shape
    return pl.pallas_call(
        pick_kernel,
        grid=(table.size // 256,),
        in_specs=[pl.BlockSpec((256, 1), lambda i: (i, 0)), full(tokens, width)],
        out_specs=pl.BlockSpec((256, width), lambda i: (i, 0)),
        out_shape=like((table.size, width), low_type),
        compiler_params=params(24),
        cost_estimate=cost(4e9, 5e6),
        name="pick_rows",
    )(table.reshape(-1, 1), states)


def spread_kernel(table_ref, rows_ref, out_ref, total):
    step = pl.program_id(0)
    spot = lax.broadcasted_iota(jnp.int32, (out_ref.shape[0], table_ref.shape[1]), 0)
    chosen = low((spot == table_ref[...]).astype(wide_type))
    part = dot(chosen, rows_ref[...])

    @pl.when(step == 0)
    def _():
        total[...] = part

    @pl.when(step != 0)
    def _():
        total[...] += part

    @pl.when(step == pl.num_programs(0) - 1)
    def _():
        out_ref[...] = low(total[...])


def spread_rows(table, rows, tokens):
    width = rows.shape[1]
    return pl.pallas_call(
        spread_kernel,
        grid=(table.size // 512,),
        in_specs=[
            pl.BlockSpec((1, 512), lambda i: (0, i)),
            pl.BlockSpec((512, width), lambda i: (i, 0)),
        ],
        out_specs=full(tokens, width),
        out_shape=like((tokens, width), low_type),
        scratch_shapes=[VMEM((tokens, width), wide_type)],
        compiler_params=params(24),
        cost_estimate=cost(4e9, 5e6),
        name="spread_rows",
    )(table.reshape(1, -1), rows)


def by_head(value, lanes):
    return jnp.concatenate([value * lane for lane in lanes], 0)


def own_lanes(stacked, lanes):
    rows = stacked.shape[0] // len(lanes)
    return sum(stacked[h * rows : (h + 1) * rows] * lane for h, lane in enumerate(lanes))


def softmax_rows(scores):
    top = jnp.max(scores, -1, keepdims=True)
    weights = jnp.exp(scores - top)
    return weights * (1.0 / jnp.sum(weights, -1, keepdims=True))


def self_mask(lengths_ref, size):
    row = lax.broadcasted_iota(jnp.int32, (size, size), 0)
    column = lax.broadcasted_iota(jnp.int32, (size, size), 1)
    row_part, column_part = jnp.zeros_like(row), jnp.zeros_like(row)
    end = jnp.int32(0)
    for n in range(lengths_ref.shape[0] - 1):
        end = end + lengths_ref[n]
        row_part += (row >= end).astype(jnp.int32)
        column_part += (column >= end).astype(jnp.int32)
    allowed = (row_part == column_part) & (column <= row)
    added = jnp.where(allowed, 0.0, -1e30)
    return jnp.concatenate([added] * (GROUP // HEAD), 0)


def groups_of(width):
    return [slice(g, g + GROUP) for g in range(0, width, GROUP)]


def self_kernel(
    lengths_ref, y_ref, w_ref, wo_ref, b_ref, n_ref, cw_ref, qkv_ref, c_ref, mixed_ref, cq_ref
):
    y = y_ref[...]
    lanes_low, lanes = head_lanes(low_type), head_lanes(wide_type)
    mask = self_mask(lengths_ref, y.shape[0])
    qkv_ref[0] = low(dot(y, w_ref[0]) + b_ref[0:1])
    qkv_ref[1] = low(dot(y, w_ref[1]))
    qkv_ref[2] = low(dot(y, w_ref[2]) + b_ref[1:2])
    for part in groups_of(y.shape[1]):
        q = qkv_ref[0, :, part] * jnp.asarray(scale_scores, low_type)
        scores = dot(by_head(q, lanes_low), qkv_ref[1, :, part], NT) + mask
        weights = low(softmax_rows(scores))
        c_ref[:, part] = low(own_lanes(dot(weights, qkv_ref[2, :, part]), lanes))
    mixed = wide(y) + (dot(c_ref[...], wo_ref[...]) + b_ref[2:3])
    mixed_ref[...] = mixed
    first = low(norm_rows(mixed, n_ref[0, 0:1], n_ref[0, 1:2]))
    cq_ref[...] = low(dot(first, cw_ref[0]) + b_ref[3:4])


def self_forward(lengths, y, inward, outward, biases, norms, cross_inward):
    rows, width = y.shape
    return pl.pallas_call(
        self_kernel,
        grid=(1,),
        in_specs=[
            pl.BlockSpec(memory_space=pltpu.SMEM),
            full(rows, width),
            full(3, width, width),
            full(width, width),
            full(6, width),
            full(3, 2, width),
            full(1, width, width),
        ],
        out_specs=[
            full(3, rows, width),
            full(rows, width),
            full(rows, width),
            full(rows, width),
        ],
        out_shape=[
            like((3, rows, width), low_type),
            like((rows, width), low_type),
            like((rows, width), wide_type),
            like((rows, width), low_type),
        ],
        compiler_params=params(40),
        cost_estimate=cost(2e10, 7e6),
        name="self_forward",
    )(lengths, y, inward, outward, biases, norms, cross_inward)


def cross_kernel(pooled_ref, q_ref, mask_ref, w_ref, bg_ref, kv_ref, c_ref, stat_ref, scores, weights):
    rows = q_ref.shape[0]
    heads = GROUP // HEAD
    lanes_low, lanes = head_lanes(low_type), head_lanes(wide_type)
    kv_ref[0] = low(dot(pooled_ref[...], w_ref[1]))
    kv_ref[1] = low(dot(pooled_ref[...], w_ref[2]) + bg_ref[4:5])
    q = q_ref[...] * jnp.asarray(scale_scores, low_type)
    scores[...] = dot(by_head(q, lanes_low), kv_ref[0], NT)
    stats, scales = [], []
    for h in range(heads):
        part = slice(h * rows, (h + 1) * rows)
        masked = scores[part, :] + mask_ref[...]
        top = jnp.max(masked, -1, keepdims=True)
        weight = jnp.exp(masked - top)
        total = jnp.sum(weight, -1, keepdims=True)
        weights[part, :] = low(weight)
        stats.append(top + jnp.log(total))
        scales.append(lanes[h] * (1.0 / total))
    mixed = dot(weights[...], kv_ref[1])
    c_ref[...] = sum(mixed[h * rows : (h + 1) * rows] * scales[h] for h in range(heads))
    column = jnp.concatenate(stats, 0)
    stat_ref[0] = jnp.broadcast_to(column, (heads * rows, 128)).T[0:8]


def cross_forward(pooled, q, mask, inward, biases):
    slots, width = pooled.shape
    rows = q.shape[0]
    groups = width // GROUP
    stacked = rows * (GROUP // HEAD)
    return pl.pallas_call(
        cross_kernel,
        grid=(groups,),
        in_specs=[
            full(slots, width),
            pl.BlockSpec((rows, GROUP), lambda g: (0, g)),
            full(rows, slots),
            pl.BlockSpec((3, width, GROUP), lambda g: (0, 0, g)),
            pl.BlockSpec((6, GROUP), lambda g: (0, g)),
        ],
        out_specs=[
            pl.BlockSpec((2, slots, GROUP), lambda g: (0, 0, g)),
            pl.BlockSpec((rows, GROUP), lambda g: (0, g)),
            pl.BlockSpec((1, 8, stacked), lambda g: (g, 0, 0)),
        ],
        out_shape=[
            like((2, slots, width), low_type),
            like((rows, width), wide_type),
            like((groups, 8, stacked), wide_type),
        ],
        scratch_shapes=[VMEM((stacked, slots), wide_type), VMEM((stacked, slots), low_type)],
        compiler_params=params(),
        cost_estimate=cost(2e10, 1.2e7, 3e6),
        name="cross_forward",
    )(pooled, q, mask, inward, biases)


def middle_kernel(
    mixed_ref, c_ref, co_ref, b_ref, n_ref, e_ref, eb_ref, s_ref, sb_ref, grad_ref, *rest
):
    out_ref, joined_back_ref, dc_ref, vec_ref, deb_ref = rest[:5]
    hidden, slope, between, hold = rest[-4:]
    wide_outs, tall_outs, out_outs = thirds(rest[5:-4])
    width = mixed_ref.shape[1]
    blocks = [slice(i * width, (i + 1) * width) for i in range(e_ref.shape[1] // width)]
    first = norm_rows(mixed_ref[...], n_ref[0, 0:1], n_ref[0, 1:2])
    context = low(c_ref[...])
    joined = first + (dot(context, co_ref[...]) + b_ref[5:6])
    second = norm_rows(joined, n_ref[1, 0:1], n_ref[1, 1:2])
    second_low = low(second)
    total = jnp.zeros(joined.shape, wide_type)
    for part in blocks:
        value, rate = gelu_parts(dot(second_low, e_ref[:, part]) + eb_ref[:, part])
        hidden[:, part] = low(value)
        slope[:, part] = rate
        total += dot(hidden[:, part], s_ref[part, :])
    summed = second + (total + sb_ref[...])
    out_ref[...] = low(norm_rows(summed, n_ref[2, 0:1], n_ref[2, 1:2]))
    summed_back, gain, offset = norm_rows_back(summed, n_ref[2, 0:1], wide(grad_ref[...]))
    summed_low = low(summed_back)
    vec_ref[...] = jnp.zeros(vec_ref.shape, wide_type)
    vec_ref[0:1] = gain
    vec_ref[1:2] = offset
    vec_ref[2:3] = jnp.sum(wide(summed_low), 0, keepdims=True)
    second_back = summed_back
    for part in blocks:
        before = low(dot(summed_low, s_ref[part, :], NT) * slope[:, part])
        between[:, part] = before
        deb_ref[:, part] = jnp.sum(wide(before), 0, keepdims=True)
        second_back += dot(before, e_ref[:, part], NT)
    joined_back, gain, offset = norm_rows_back(joined, n_ref[1, 0:1], second_back)
    joined_low = low(joined_back)
    joined_back_ref[...] = joined_back
    vec_ref[3:4] = gain
    vec_ref[4:5] = offset
    vec_ref[5:6] = jnp.sum(wide(joined_low), 0, keepdims=True)
    dc_ref[...] = low(dot(joined_low, co_ref[...], NT))
    for i, part in enumerate(blocks):
        hold[...] = dot(second_low, between[:, part], TN)
        emit(wide_outs, i, hold)
        hold[...] = dot(hidden[:, part], summed_low, TN)
        emit_tall(tall_outs, i, hold)
    hold[...] = dot(context, joined_low, TN)
    emit(out_outs, 0, hold)


def middle(mixed, context, outward, biases, norms, expand, expand_bias, shrink, shrink_bias, grad):
    rows, width = mixed.shape
    total = expand.shape[1]
    ins = (
        mixed,
        context,
        outward,
        biases,
        norms,
        expand,
        expand_bias[None],
        shrink,
        shrink_bias[None],
        grad,
    )
    outs = pl.pallas_call(
        middle_kernel,
        grid=(1,),
        in_specs=[full(*value.shape) for value in ins],
        out_specs=[
            full(rows, width),
            full(rows, width),
            full(rows, width),
            full(8, width),
            full(1, total),
            *grad_specs(4, width, width),
            *grad_specs(1, total, width),
            *grad_specs(1, width, width),
        ],
        out_shape=[
            like((rows, width), low_type),
            like((rows, width), wide_type),
            like((rows, width), low_type),
            like((8, width), wide_type),
            like((1, total), wide_type),
            *grad_shapes(4, width, width),
            *grad_shapes(1, total, width),
            *grad_shapes(1, width, width),
        ],
        scratch_shapes=[
            VMEM((rows, total), low_type),
            VMEM((rows, total), wide_type),
            VMEM((rows, total), low_type),
            VMEM((width, width), wide_type),
        ],
        compiler_params=params(),
        cost_estimate=cost(2e10, 2.2e7),
        name="middle",
    )(*ins)
    return outs[:5], thirds(outs[5:])


def cross_back_kernel(
    kv_ref, q_ref, c_ref, dc_ref, stat_ref, mask_ref, w_ref, dkv_ref, dq_ref, vec_ref, dpool_ref,
    total, weights, scores_back
):
    group = pl.program_id(0)
    rows = q_ref.shape[0]
    heads = GROUP // HEAD
    lanes_low, lanes = head_lanes(low_type), head_lanes(wide_type)
    q_heads = by_head(q_ref[...] * jnp.asarray(scale_scores, low_type), lanes_low)
    dc_heads = by_head(dc_ref[...], lanes_low)
    product = wide(dc_heads) * jnp.concatenate([c_ref[...]] * heads, 0)
    column = jnp.sum(product, -1, keepdims=True)
    inner = jnp.broadcast_to(column, (heads * rows, 128)).T[0:1]
    stat = stat_ref[0, 0:1]
    for h in range(heads):
        part = slice(h * rows, (h + 1) * rows)
        weight = jnp.exp(dot(kv_ref[0], q_heads[part], NT) + mask_ref[...] - stat[:, part])
        weight_back = dot(kv_ref[1], dc_heads[part], NT)
        weights[:, part] = low(weight)
        scores_back[:, part] = low(weight * (weight_back - inner[:, part]))
    dk = low(dot(scores_back[...], q_heads))
    dv = low(dot(weights[...], dc_heads))
    dkv_ref[0] = dk
    dkv_ref[1] = dv
    dq = low(own_lanes(dot(scores_back[...], kv_ref[0], TN), lanes) * scale_scores)
    dq_ref[...] = dq
    vec_ref[...] = jnp.zeros(vec_ref.shape, wide_type)
    vec_ref[0:1] = jnp.sum(wide(dq), 0, keepdims=True)
    vec_ref[1:2] = jnp.sum(wide(dv), 0, keepdims=True)
    part = dot(dk, w_ref[1], NT) + dot(dv, w_ref[2], NT)

    @pl.when(group == 0)
    def _():
        total[...] = part

    @pl.when(group != 0)
    def _():
        total[...] += part

    @pl.when(group == pl.num_programs(0) - 1)
    def _():
        dpool_ref[...] = low(total[...])


def cross_back(kv, q, context, dc, stats, mask, inward):
    slots, width = kv.shape[1:]
    rows = q.shape[0]
    groups = width // GROUP
    stacked = rows * (GROUP // HEAD)
    column = pl.BlockSpec((rows, GROUP), lambda g: (0, g))
    return pl.pallas_call(
        cross_back_kernel,
        grid=(groups,),
        in_specs=[
            pl.BlockSpec((2, slots, GROUP), lambda g: (0, 0, g)),
            column,
            column,
            column,
            pl.BlockSpec((1, 8, stacked), lambda g: (g, 0, 0)),
            full(slots, rows),
            pl.BlockSpec((3, width, GROUP), lambda g: (0, 0, g)),
        ],
        out_specs=[
            pl.BlockSpec((2, slots, GROUP), lambda g: (0, 0, g)),
            column,
            pl.BlockSpec((8, GROUP), lambda g: (0, g)),
            full(slots, width),
        ],
        out_shape=[
            like((2, slots, width), low_type),
            like((rows, width), low_type),
            like((8, width), wide_type),
            like((slots, width), low_type),
        ],
        scratch_shapes=[
            VMEM((slots, width), wide_type),
            VMEM((slots, stacked), low_type),
            VMEM((slots, stacked), low_type),
        ],
        compiler_params=params(),
        cost_estimate=cost(3e10, 2.2e7, 3e6),
        name="cross_back",
    )(kv, q, context, dc, stats, mask, inward)


def cross_grads_kernel(pooled_ref, dkv_ref, mixed_ref, dq_ref, n_ref, *rest):
    outs, (turned, hold) = rest[:-2], rest[-2:]

    @pl.when(pl.program_id(0) == 0)
    def _():
        turned[...] = pooled_ref[...].T

    first = low(norm_rows(mixed_ref[...], n_ref[0, 0:1], n_ref[0, 1:2]))
    hold[...] = dot(first, dq_ref[...], TN)
    emit(outs, 0, hold)
    hold[...] = dot(turned[...], dkv_ref[0])
    emit(outs, 1, hold)
    hold[...] = dot(turned[...], dkv_ref[1])
    emit(outs, 2, hold)


def cross_grads(pooled, dkv, mixed, dq, norms):
    slots, width = pooled.shape
    rows = mixed.shape[0]
    return pl.pallas_call(
        cross_grads_kernel,
        grid=(width // GROUP,),
        in_specs=[
            full(slots, width),
            pl.BlockSpec((2, slots, GROUP), lambda g: (0, 0, g)),
            full(rows, width),
            pl.BlockSpec((rows, GROUP), lambda g: (0, g)),
            full(3, 2, width),
        ],
        out_specs=grad_specs(3, width, GROUP, lambda g: (0, 0, g)),
        out_shape=grad_shapes(3, width, width),
        scratch_shapes=[VMEM((width, slots), low_type), VMEM((width, GROUP), wide_type)],
        compiler_params=params(48),
        cost_estimate=cost(1e10, 1.5e7),
        name="cross_grads",
    )(pooled, dkv, mixed, dq, norms)


def self_back_kernel(
    lengths_ref, y_ref, mixed_ref, jb_ref, cdq_ref, qkv_ref, c_ref, w_ref, wo_ref, cw_ref, n_ref,
    dy_ref, vec_ref, *rest
):
    outs, (dqkv, hold) = rest[:-2], rest[-2:]
    width = y_ref.shape[1]
    y = y_ref[...]
    lanes_low, lanes = head_lanes(low_type), head_lanes(wide_type)
    mask = self_mask(lengths_ref, y.shape[0])
    first_back = jb_ref[...] + dot(cdq_ref[...], cw_ref[0], NT)
    mixed_back, gain, offset = norm_rows_back(mixed_ref[...], n_ref[0, 0:1], first_back)
    mixed_low = low(mixed_back)
    vec_ref[...] = jnp.zeros(vec_ref.shape, wide_type)
    vec_ref[0:1] = gain
    vec_ref[1:2] = offset
    vec_ref[2:3] = jnp.sum(wide(mixed_low), 0, keepdims=True)
    dc = low(dot(mixed_low, wo_ref[...], NT))
    for part in groups_of(width):
        q_heads = by_head(qkv_ref[0, :, part] * jnp.asarray(scale_scores, low_type), lanes_low)
        dc_heads = by_head(dc[:, part], lanes_low)
        weights = softmax_rows(dot(q_heads, qkv_ref[1, :, part], NT) + mask)
        weights_back = dot(dc_heads, qkv_ref[2, :, part], NT)
        inner = jnp.sum(weights * weights_back, -1, keepdims=True)
        scores_back = low(weights * (weights_back - inner))
        dq = own_lanes(dot(scores_back, qkv_ref[1, :, part]), lanes) * scale_scores
        dqkv[0, :, part] = low(dq)
        dqkv[1, :, part] = low(dot(scores_back, q_heads, TN))
        dqkv[2, :, part] = low(dot(low(weights), dc_heads, TN))
    vec_ref[3:4] = jnp.sum(wide(dqkv[0]), 0, keepdims=True)
    vec_ref[4:5] = jnp.sum(wide(dqkv[2]), 0, keepdims=True)
    dy_ref[...] = (
        mixed_back
        + dot(dqkv[0], w_ref[0], NT)
        + (dot(dqkv[1], w_ref[1], NT) + dot(dqkv[2], w_ref[2], NT))
    )
    for part in range(3):
        hold[...] = dot(y, dqkv[part], TN)
        emit(outs, part, hold)
    hold[...] = dot(c_ref[...], mixed_low, TN)
    emit(outs, 3, hold)


def self_back(lengths, y, mixed, joined_back, dq, qkv, context, inward, outward, cross_inward, norms):
    rows, width = y.shape
    ins = (y, mixed, joined_back, dq, qkv, context, inward, outward)
    outs = pl.pallas_call(
        self_back_kernel,
        grid=(1,),
        in_specs=[
            pl.BlockSpec(memory_space=pltpu.SMEM),
            *[full(*value.shape) for value in ins],
            full(1, width, width),
            full(3, 2, width),
        ],
        out_specs=[full(rows, width), full(8, width), *grad_specs(4, width, width)],
        out_shape=[
            like((rows, width), wide_type),
            like((8, width), wide_type),
            *grad_shapes(4, width, width),
        ],
        scratch_shapes=[VMEM((3, rows, width), low_type), VMEM((width, width), wide_type)],
        compiler_params=params(48),
        cost_estimate=cost(2e10, 1.5e7),
        name="self_back",
    )(lengths, *ins, cross_inward, norms)
    return outs[:2], outs[2:]


def shifted(value, axis, by):
    length = lax.axis_size(axis)
    return lax.ppermute(value, axis, [(i, (i + by) % length) for i in range(length)])


COUNT = 7
ROWS = 384
HALF = ROWS // 2
QUARTER = ROWS // 4
VEC_ROWS = 32


def add_rows(to, other, rows):
    def step(i, carry):
        at = pl.ds(pl.multiple_of(i * 32, 32), 32)
        to[at, :] = low(wide(to[at, :]) + wide(other[at, :]))
        return carry

    lax.fori_loop(0, rows // 32, step, 0)


def partners():
    me, section = lax.axis_index("dp"), lax.axis_index("section")
    return (
        {"dp": me + 1 - 2 * (me % 2)},
        {"dp": me + 2 - 4 * ((me // 2) % 2)},
        {"dp": me + 4 - 8 * (me // 4)},
        {"section": section + 1 - 2 * (section % 2)},
        {"section": section + 2 - 4 * (section // 2)},
    )


def greet():
    barrier = pltpu.get_barrier_semaphore()
    for partner in partners():
        pl.semaphore_signal(barrier, 1, device_id=partner, device_id_type=pl.DeviceIdType.MESH)
    pl.semaphore_wait(barrier, 5)


def sum_kernel(sources, *refs):
    count = len(sources)
    keeps, sends, vec_ref = refs[:count], refs[count : 2 * count], refs[2 * count]
    out_ref, vec_out = refs[2 * count + 1 : 2 * count + 3]
    own, from_core, from_one, from_two, from_three, from_four, whole, vec_in = refs[
        2 * count + 3 : 2 * count + 11
    ]
    load_sems, core_send, core_recv, send_sems, recv_sems, vec_send, vec_recv, out_sems = refs[
        2 * count + 11 :
    ]
    core, over_x, over_y, near, far = partners()
    section = lax.axis_index("section")
    side = section % 2
    far_side = section // 2
    half_at = pl.multiple_of(side * HALF, HALF)
    half_other = pl.multiple_of((1 - side) * HALF, HALF)
    quarter_at = pl.multiple_of(side * HALF + far_side * QUARTER, QUARTER)
    quarter_other = pl.multiple_of(side * HALF + (1 - far_side) * QUARTER, QUARTER)
    upper, lower = pl.ds(0, HALF), pl.ds(HALF, HALF)

    def remote(source, to, send, recv, partner):
        return pltpu.make_async_remote_copy(
            src_ref=source,
            dst_ref=to,
            send_sem=send,
            recv_sem=recv,
            device_id=partner,
            device_id_type=pl.DeviceIdType.MESH,
        )

    loads, first = [], []
    for n, (chunk, row) in enumerate(sources):
        rows = pl.ds(row, keeps[n].shape[1])
        loads.append(
            pltpu.make_async_copy(
                keeps[n], own.at[chunk, :, rows], load_sems.at[n]
            )
        )
        first.append(
            remote(sends[n], from_core.at[chunk, :, rows], core_send.at[n], core_recv.at[n], core)
        )

    def pairs(stage, c):
        total = own.at[c, 0]
        if stage == 1:
            return (
                (own.at[c, pl.ds(1, 1), upper], from_one.at[c, 0, pl.ds(0, 1)], over_x),
                (own.at[c, pl.ds(3, 1), upper], from_one.at[c, 0, pl.ds(1, 1)], over_x),
                (own.at[c, pl.ds(2, 2), lower], from_one.at[c, 1], over_y),
            )
        if stage == 2:
            return (
                (own.at[c, 2, upper], from_two.at[c, 0], over_y),
                (own.at[c, 1, lower], from_two.at[c, 1], over_x),
            )
        if stage == 3:
            return ((total.at[pl.ds(half_other, HALF)], from_three.at[c], near),)
        if stage == 4:
            return ((total.at[pl.ds(quarter_other, QUARTER)], from_four.at[c], far),)
        if stage == 5:
            rows = pl.ds(quarter_at, QUARTER)
            return ((whole.at[c, rows], whole.at[c, rows], far),)
        rows = pl.ds(half_at, HALF)
        return ((whole.at[c, rows], whole.at[c, rows], near),)

    def copies(stage, c):
        return [
            remote(source, to, send_sems.at[stage, c, k], recv_sems.at[stage, c, k], partner)
            for k, (source, to, partner) in enumerate(pairs(stage, c))
        ]

    def start(stage, c):
        for copy in copies(stage, c):
            copy.start()

    def land(stage, c):
        for copy in copies(stage, c):
            copy.wait_recv()

    def out_copy(c):
        return pltpu.make_async_copy(whole.at[c], out_ref.at[c], out_sems.at[c])

    def vec_copy(stage):
        return remote(
            vec_out, vec_in.at[stage], vec_send.at[stage], vec_recv.at[stage], partners()[stage]
        )

    def vec_step(stage):
        if stage:
            vec_copy(stage - 1).wait()
            vec_out[...] += vec_in[stage - 1]
        else:
            vec_out[...] = vec_ref[...]
        if stage < 5:
            vec_copy(stage).start()

    def step(stage, c):
        if stage == 0:
            for n, (chunk, _) in enumerate(sources):
                if chunk == c:
                    loads[n].wait()
                    first[n].wait_recv()
            for at in range(4):
                add_rows(own.at[c, at], from_core.at[c, at], ROWS)
            start(1, c)
            return
        land(stage, c)
        if stage == 1:
            for k in range(2):
                add_rows(own.at[c, 2 * k, upper], from_one.at[c, 0, k], HALF)
                add_rows(own.at[c, k, lower], from_one.at[c, 1, k], HALF)
        elif stage == 2:
            add_rows(own.at[c, 0, upper], from_two.at[c, 0], HALF)
            add_rows(own.at[c, 0, lower], from_two.at[c, 1], HALF)
        elif stage == 3:
            add_rows(own.at[c, 0, pl.ds(half_at, HALF)], from_three.at[c], HALF)
        elif stage == 4:
            rows = pl.ds(quarter_at, QUARTER)
            whole[c, rows, :] = low(wide(own[c, 0, rows, :]) + wide(from_four[c]))
        if stage < 6:
            start(stage + 1, c)
        else:
            out_copy(c).start()

    greet()
    for n in range(count):
        first[n].start()
        loads[n].start()
    vec_step(0)
    for time in range(COUNT + 6):
        for stage in reversed(range(7)):
            if 0 <= time - stage < COUNT:
                step(stage, time - stage)
        if 1 <= time + 1 <= 5:
            vec_step(time + 1)
    for n in range(count):
        first[n].wait_send()
    for c in range(COUNT):
        for stage in range(1, 7):
            for copy in copies(stage, c):
                copy.wait_send()
        out_copy(c).wait()


def sum_pairs(pairs, sources, vector):
    count = len(pairs)
    width = pairs[0][0].shape[2]
    anywhere = pl.BlockSpec(memory_space=pl.ANY)
    here = pl.BlockSpec(memory_space=VMEM)
    dma = pltpu.SemaphoreType.DMA
    return pl.pallas_call(
        functools.partial(sum_kernel, sources),
        in_specs=[anywhere] * (2 * count) + [here],
        out_specs=[anywhere, here],
        out_shape=[
            like((COUNT, ROWS, width), low_type),
            like((VEC_ROWS, width), wide_type),
        ],
        scratch_shapes=[
            VMEM((COUNT, 4, ROWS, width), low_type),
            VMEM((COUNT, 4, ROWS, width), low_type),
            VMEM((COUNT, 2, 2, HALF, width), low_type),
            VMEM((COUNT, 2, HALF, width), low_type),
            VMEM((COUNT, HALF, width), low_type),
            VMEM((COUNT, QUARTER, width), low_type),
            VMEM((COUNT, ROWS, width), low_type),
            VMEM((5, VEC_ROWS, width), wide_type),
            dma((count,)),
            dma((count,)),
            dma((count,)),
            dma((7, COUNT, 3)),
            dma((7, COUNT, 3)),
            dma((5,)),
            dma((5,)),
            dma((COUNT,)),
        ],
        compiler_params=params(60, collective_id=1, has_side_effects=True),
        cost_estimate=cost(1e8, 1e8),
        name="sum_pairs",
    )(*[p[0] for p in pairs], *[p[1] for p in pairs], vector)


def sum_whole(grads):
    parts = lax.axis_size("dp")
    packed = []
    for grad in grads:
        count, rows, columns = grad.shape
        cut = grad.reshape(count, parts, rows // parts, columns // WIDTH, WIDTH)
        packed.append(cut.transpose(1, 0, 3, 2, 4).reshape(parts, -1, WIDTH))
    shard = lax.psum_scatter(jnp.concatenate(packed, 1), "dp", scatter_dimension=0, tiled=True)[0]
    total = wide(lax.psum(shard, "section"))
    outs, at = [], 0
    for grad in grads:
        count, rows, columns = grad.shape
        size = grad.size // parts // WIDTH
        cut = total[at : at + size].reshape(count, columns // WIDTH, rows // parts, WIDTH)
        outs.append(cut.transpose(0, 2, 1, 3).reshape(count * rows // parts, columns))
        at += size
    return outs


def sum_all(grads, vectors):
    flat = jnp.concatenate([v.reshape(-1) for v in vectors])
    if paired():
        sources = ((0, 0), (1, 0), (2, 0), (2, 288), (3, 0), (4, 0), (5, 0), (6, 0), (6, 288))
        rows = [grad[0].shape[1] for grad in grads]
        padded = jnp.pad(flat, (0, VEC_ROWS * WIDTH - flat.size)).reshape(VEC_ROWS, WIDTH)
        total, flat = sum_pairs(grads, sources, padded)
        flat = flat.reshape(-1)
        shards = [
            wide(total[chunk, row : row + size]) for (chunk, row), size in zip(sources, rows)
        ]
    else:
        shards = sum_whole([grad[0] for grad in grads])
        flat = lax.psum(flat, ("dp", "section"))
    parts, mine = lax.axis_size("dp"), lax.axis_index("dp")
    outs, at = [], 0
    for v in vectors:
        whole = flat[at : at + v.size].reshape(v.shape)
        at += v.size
        size = v.shape[-1] // parts
        outs.append(lax.dynamic_slice_in_dim(whole, mine * size, size, v.ndim - 1))
    return shards, outs


def beside(shard):
    rows = shard.shape[0] // 4
    return shard.reshape(4, rows, WIDTH).transpose(1, 0, 2).reshape(rows, 4 * WIDTH)


def on_device(
    encoder_input,
    decoder_input,
    cotangent,
    pool_table,
    retrieved,
    decoder_lengths,
    encoder_inward,
    encoder_outward,
    encoder_biases,
    encoder_norms,
    encoder_expand,
    encoder_expand_bias,
    encoder_shrink,
    encoder_shrink_bias,
    self_inward,
    self_outward,
    cross_inward,
    cross_outward,
    decoder_biases,
    decoder_norms,
    decoder_expand,
    decoder_expand_bias,
    decoder_shrink,
    decoder_shrink_bias,
):
    x = encoder_input[0]
    half_way = lax.axis_size("section") // 2
    queries = decoder_input.shape[1]
    topk = retrieved.shape[2]
    rows_low = shifted(jnp.concatenate([decoder_input[0], cotangent[0]], 0), "section", -half_way)
    y, grad = rows_low[:queries], rows_low[queries:]
    lengths_row = jnp.pad(decoder_lengths[0], ((0, 0), (0, topk - decoder_lengths.shape[2])))
    integers = shifted(
        jnp.concatenate([retrieved[0], pool_table[0, 0].reshape(-1, topk), lengths_row], 0),
        "section",
        -half_way,
    )
    slots = integers[:queries]
    table = integers[queries:-1].reshape(-1)
    lengths = integers[-1, : decoder_lengths.shape[2]]
    owners = pool_table.shape[2]

    qkv, context, stats, mixed = encoder_attend(
        x, encoder_inward, encoder_outward, encoder_biases
    )
    hidden, slope, summed, states = encoder_feed(
        mixed,
        encoder_norms,
        encoder_expand,
        encoder_expand_bias,
        encoder_shrink,
        encoder_shrink_bias,
    )
    picked = pick_rows(table, states).reshape(owners, -1, WIDTH)
    pooled = lax.all_to_all(picked, "dp", split_axis=0, concat_axis=0, tiled=True)
    pooled = pooled.reshape(-1, WIDTH)

    mask_across, mask_down = slot_mask(slots, pooled.shape[0])
    self_qkv, self_context, self_mixed, cross_q = self_forward(
        lengths, y, self_inward, self_outward, decoder_biases, decoder_norms, cross_inward
    )
    kv, cross_context, cross_stats = cross_forward(
        pooled, cross_q, mask_across, cross_inward, decoder_biases
    )
    (out, joined_back, dc, mid_vec, mid_expand), (d_expand, d_shrink, d_cross_out) = middle(
        self_mixed,
        cross_context,
        cross_outward,
        decoder_biases,
        decoder_norms,
        decoder_expand,
        decoder_expand_bias,
        decoder_shrink,
        decoder_shrink_bias,
        grad,
    )
    dkv, dq, cross_vec, dpool = cross_back(
        kv, cross_q, cross_context, dc, cross_stats, mask_down, cross_inward
    )
    returned = lax.all_to_all(
        dpool.reshape(owners, -1, WIDTH), "dp", split_axis=0, concat_axis=0, tiled=True
    )
    d_cross_in = cross_grads(pooled, dkv, self_mixed, dq, decoder_norms)
    (dy, self_vec), d_self = self_back(
        lengths,
        y,
        self_mixed,
        joined_back,
        dq,
        self_qkv,
        self_context,
        self_inward,
        self_outward,
        cross_inward,
        decoder_norms,
    )
    decoder_out = shifted(out, "section", half_way)
    decoder_grad = shifted(dy, "section", half_way)
    states_back = spread_rows(table, returned.reshape(-1, WIDTH), x.shape[0])

    (dmix, feed_vec, feed_expand), (e_expand, e_shrink, e_out) = encoder_feed_back(
        states_back,
        summed,
        mixed,
        hidden,
        slope,
        context,
        encoder_norms,
        encoder_expand,
        encoder_shrink,
    )
    (dx, attend_vec), e_in = encoder_attend_back(
        dmix, x, qkv, context, stats, encoder_inward, encoder_outward
    )

    shards, vectors = sum_all(
        [d_expand, d_shrink, d_cross_in, d_cross_out, d_self, e_expand, e_shrink, e_in, e_out],
        [
            jnp.concatenate([attend_vec[0:2], feed_vec[5:6]], 0),
            jnp.stack([feed_vec[3:5], feed_vec[0:2]]),
            feed_expand[0],
            feed_vec[2],
            jnp.concatenate([self_vec[3:5], self_vec[2:3], cross_vec[0:2], mid_vec[5:6]], 0),
            jnp.stack([self_vec[0:2], mid_vec[3:5], mid_vec[0:2]]),
            mid_expand[0],
            mid_vec[2],
        ],
    )
    d_expand, d_shrink, d_cross_in, d_cross_out, d_self, e_expand, e_shrink, e_in, e_out = shards
    rows = WIDTH // lax.axis_size("dp")
    return (
        decoder_out[None],
        dx[None],
        decoder_grad[None],
        e_in.reshape(3, rows, WIDTH),
        e_out,
        vectors[0],
        vectors[1],
        beside(e_expand),
        vectors[2],
        e_shrink,
        vectors[3],
        d_self[: 3 * rows].reshape(3, rows, WIDTH),
        d_self[3 * rows :],
        d_cross_in.reshape(3, rows, WIDTH),
        d_cross_out,
        vectors[4],
        vectors[5],
        beside(d_expand),
        vectors[6],
        d_shrink,
        vectors[7],
    )


def solution(mesh):
    in_specs = (
        P("section", "dp", None),
        P("section", "dp", None),
        P("section", "dp", None),
        P("section", "dp", None, None),
        P("section", "dp", None),
        P("section", "dp", None),
        P(),
        P(),
        P(),
        P(),
        P(),
        P(),
        P(),
        P(),
        P(),
        P(),
        P(),
        P(),
        P(),
        P(),
        P(),
        P(),
        P(),
        P(),
    )
    out_specs = (
        P("section", "dp", None),
        P("section", "dp", None),
        P("section", "dp", None),
        P(None, "dp", None),
        P("dp", None),
        P(None, "dp"),
        P(None, None, "dp"),
        P("dp", None),
        P("dp"),
        P("dp", None),
        P("dp"),
        P(None, "dp", None),
        P("dp", None),
        P(None, "dp", None),
        P("dp", None),
        P(None, "dp"),
        P(None, None, "dp"),
        P("dp", None),
        P("dp"),
        P("dp", None),
        P("dp"),
    )
    return jax.shard_map(
        on_device, mesh=mesh, in_specs=in_specs, out_specs=out_specs, check_vma=False
    )
```

time: 1030 us -> 566 us (0.55)
  Pallas kernels: 9.1 us -> 461 us
  matrix products: 371 us -> 0 us
  waiting for transfers between devices: 368 us -> 32.1 us
  other arithmetic: 110 us -> 9.65 us
  local copies, waits for them, and re-layouts: 131 us -> 36.6 us
  between operations: 18.1 us -> 1.47 us
    pallas_call x1 -> x14, Pallas kernels: 9.1 us -> 461 us  [the longest x1 201 us: sum_pairs(): pl.pallas_call(functools.partial(sum_kernel, sources), in_specs=[anywhere...]
    dot_general x73 -> x0, matrix products: 371 us -> none  [the longest x16 90.1 us: project(): return jnp.dot(left, right, preferred_element_type=wide_type)]
    reduce_scatter x3 -> x0, waiting for transfers between devices: 149 us -> none  [sum_matrices(): shard = lax.psum_scatter(packed, 'dp', scatter_dimension=0, tiled=True)[0]]
    psum x2 -> x0, waiting for transfers between devices: 113 us -> none  [the longest x1 113 us: sum_matrices(): total = lax.psum(shard, 'section').astype(wide_type)]
    convert_element_type x8 -> x4, other arithmetic: 52.7 us -> 7.28 us  [wide(): return value.astype(wide_type)]
    all_to_all x2, waiting for transfers between devices: 67.9 us -> 25 us  [the longest x1 25 us: on_device(): lax.all_to_all(picked, 'dp', split_axis=0, concat_axis=0, tiled=True)]
    reduce_sum x22 -> x0, other arithmetic: 40.4 us -> none  [the longest x4 24.8 us: attend_forward(): row_total = jnp.sum(exponent, -1, keepdims=True)]
    convert_element_type x14 -> x0, local copies, waits for them, and re-layouts: 35.2 us -> none  [the longest x7 30.2 us: sum_matrices(): rows_of(m, parts).astype(low_type)]
  transfers between devices with their start and end apart: 11 -> 6, of which waited for: 6 -> 2; matrix products, arithmetic and copies ran while one was open for 28% -> 1% of each run, Pallas kernels for 0% -> 21%
where the time goes in v2:
time: 566 us; the launch traced here: 557 us
  Pallas kernels  461 us (81%)
  local copies, waits for them, and re-layouts  36.6 us (6%)
  waiting for transfers between devices  32.1 us (6%)
  starting transfers between devices  15.7 us (3%)
  other arithmetic  9.65 us (2%)
    pallas_call x1, Pallas kernels, sum_pairs(): pl.pallas_call(functools.partial(sum_kernel, sources), in_specs=[anywhere...  201 us
    pallas_call x1, Pallas kernels, encoder_attend_back(): pl.pallas_call(encoder_attend_back_kernel, grid=(groups,), in_specs=[full...  54.4 us
    pallas_call x1, Pallas kernels, encoder_feed_back(): pl.pallas_call(encoder_feed_back_kernel, grid=(4,), in_specs=[full(tokens...  41.6 us
    pallas_call x1, Pallas kernels, encoder_attend(): pl.pallas_call(encoder_attend_kernel, grid=(groups,), in_specs=[full(toke...  34.3 us
    pallas_call x1, Pallas kernels, encoder_feed(): pl.pallas_call(encoder_feed_kernel, grid=(4,), in_specs=[full(tokens, wid...  27.4 us
    all_to_all x1, waiting for transfers between devices, on_device(): lax.all_to_all(picked, 'dp', split_axis=0, concat_axis=0, tiled=True)  25 us
    pallas_call x1, Pallas kernels, cross_back(): pl.pallas_call(cross_back_kernel, grid=(groups,), in_specs=[pl.BlockSpec(...  24.3 us
    unnamed x75, local copies, waits for them, and re-layouts  19.6 us
  transfers between devices with their start and end apart: 6, of which 2 were waited for; matrix products, arithmetic and copies ran while one was open for 1% of the time, Pallas kernels for 21%

profile of v2, /device:TPU:0, one launch (start us, length us, event | category | flops | bytes accessed | tf_op | source)
XLA Modules:
  0.0 556.5 jit_solution(6304805101708591508)
XLA Ops:
  2.5 4.1 collective-permute-start
  9.0 34.3 %encoder_attend.1 = (bf16[3,1024,768]{2,1,0:T(8,128)(2,1)}, f32[1024,768]{1,0:T(8,128)}, f32[3,8,1024]{2,1,0:T(8,128)}, f32[1024,768]{1,0:T(8,128)}) custom-call(bf16[1024,768]{1,0:T(8,128)(2,1)} %bitcast.93, bf16[3,768,768]{2,1,0:T(8,128)(2,1)} %w_ref.10, bf16[768,768]{1,0:T(8,128)(2,1)} %wo_ref.6, f32[3,768]{1,0:T(4,128)} %b_ref.4, f32[3,768]{1,0:T(4,128)} %b_ref.4), custom_call_target="tpu_custom_call" | custom-call | flops 30000001024 | bytes 20000000 | tf_op jit(solution)/shard_map/encoder_attend/pallas_call | solution.py:189
  43.2 27.4 %encoder_feed.1 = (bf16[1024,3072]{1,0:T(8,128)(2,1)}, bf16[1024,3072]{1,0:T(8,128)(2,1)}, f32[1024,768]{1,0:T(8,128)}, bf16[1024,768]{1,0:T(8,128)(2,1)}) custom-call(f32[1024,768]{1,0:T(8,128)} %get-tuple-element.75.mixed_ref, f32[2,2,768]{2,1,0:T(2,128)} %n_ref.9, bf16[768,3072]{1,0:T(8,128)(2,1)} %e_ref.5, f32[1,3072]{1,0:T(1,128)} %bitcast.95, ...), custom_call_target="tpu_custom_call" | custom-call | flops 20000000000 | bytes 30000000 | tf_op jit(solution)/shard_map/encoder_feed/pallas_call | solution.py:247
  73.8 6.4 %pick_rows.1 = bf16[2048,768]{1,0:T(8,128)(2,1)} custom-call(s32[2048,1]{1,0:T(8,128)S(1)} %bitcast.75, bf16[1024,768]{1,0:T(8,128)(2,1)S(1)} %copy-done.10), custom_call_target="tpu_custom_call" | custom-call | flops 4000000000 | bytes 5000000 | tf_op jit(solution)/shard_map/pick_rows/pallas_call | solution.py:527
  80.1 4.7 all-to-all-start
  85.1 6.5 %slot_mask.1 = (f32[128,2048]{1,0:T(8,128)S(1)}, f32[2048,128]{1,0:T(8,128)S(1)}) custom-call(s32[1024,128]{1,0:T(8,128)S(1)} %bitcast.76), custom_call_target="tpu_custom_call" | custom-call | flops 10000000000 | bytes 1000000 | tf_op jit(solution)/shard_map/slot_mask/pallas_call | solution.py:508
  91.7 3.1 self_forward.1
  97.8 25.0 %all-to-all-done = bf16[8,256,768]{2,1,0:T(8,128)(2,1)} async-done(((bf16[8,256,768]{2,1,0:T(8,128)(2,1)}), bf16[8,256,768]{2,1,0:T(8,128)(2,1)}, u32[]{:S(2)}, u32[]{:S(2)}) %all-to-all-start) | async-done | bytes 3145760 | tf_op jit(solution)/shard_map/all_to_all | solution.py:1333
  122.7 17.6 %cross_forward.1 = (bf16[2,2048,768]{2,1,0:T(8,128)(2,1)}, f32[128,768]{1,0:T(8,128)}, f32[3,8,512]{2,1,0:T(8,128)}) custom-call(bf16[2048,768]{1,0:T(8,128)(2,1)} %bitcast.8.pooled_ref, bf16[128,768]{1,0:T(8,128)(2,1)} %copy-done.24, f32[128,2048]{1,0:T(8,128)} %copy-done.13, bf16[3,768,768]{2,1,0:T(8,128)(2,1)} %cw_ref.3, f32[6,768]{1,0:T(8,128)} %b_ref.5), custom_call_target="tpu_custom_call" | custom-call | flops 20000000000 | bytes 12000000 | tf_op jit(solution)/shard_map/cross_forward/pallas_call | solution.py:690
  140.3 19.6 %middle.1 = (bf16[128,768]{1,0:T(8,128)(2,1)}, f32[128,768]{1,0:T(8,128)}, bf16[128,768]{1,0:T(8,128)(2,1)}, f32[8,768]{1,0:T(8,128)}, f32[1,3072]{1,0:T(1,128)}...) custom-call(f32[128,768]{1,0:T(8,128)} %copy-done.14, ...), custom_call_target="tpu_custom_call" | custom-call | flops 20000000000 | bytes 22000000 | tf_op jit(solution)/shard_map/middle/pallas_call | solution.py:781
  160.0 2.9 collective-permute-start.2
  162.9 24.3 %cross_back.1 = (bf16[2,2048,768]{2,1,0:T(8,128)(2,1)}, bf16[128,768]{1,0:T(8,128)(2,1)}, f32[8,768]{1,0:T(8,128)}, bf16[2048,768]{1,0:T(8,128)(2,1)}) custom-call(bf16[2,2048,768]{2,1,0:T(8,128)(2,1)} %get-tuple-element.81.kv_ref, bf16[128,768]{1,0:T(8,128)(2,1)} %copy-done.24, f32[128,768]{1,0:T(8,128)} %get-tuple-element.79.c_ref, ...), custom_call_target="tpu_custom_call" | custom-call | flops 30000001024 | bytes 22000000 | tf_op jit(solution)/shard_map/cross_back/pallas_call | solution.py:868
  187.3 3.9 all-to-all-start.1
  197.3 9.5 %self_back.1 = (f32[128,768]{1,0:T(8,128)}, f32[8,768]{1,0:T(8,128)S(1)}, bf16[4,384,768]{2,1,0:T(8,128)(2,1)S(1)}, bf16[4,384,768]{2,1,0:T(8,128)(2,1)}) custom-call(s32[4]{0:T(128)S(1)} %slice_bitcast_fusion.7.lengths_ref, bf16[128,768]{1,0:T(8,128)(2,1)S(1)} %get-tuple-element.137.y_ref, f32[128,768]{1,0:T(8,128)S(1)} %copy-done.15, ...), custom_call_target="tpu_custom_call" | custom-call | flops 20000000000 | bytes 15000000 | tf_op jit(solution)/shard_map/self_back/pallas_call | solution.py:986
  209.1 10.6 %cross_grads.1 = (bf16[4,288,768]{2,1,0:T(8,128)(2,1)S(1)}, bf16[4,288,768]{2,1,0:T(8,128)(2,1)S(1)}) custom-call(bf16[2048,768]{1,0:T(8,128)(2,1)} %bitcast.8.pooled_ref, bf16[2,2048,768]{2,1,0:T(8,128)(2,1)} %get-tuple-element.101.dkv_ref, f32[128,768]{1,0:T(8,128)S(1)} %copy-done.16, bf16[128,768]{1,0:T(8,128)(2,1)S(1)} %copy-done.18, ...), custom_call_target="tpu_custom_call" | custom-call | flops 10000000000 | bytes 15000000 | tf_op jit(solution)/shard_map/cross_grads/pallas_call | solution.py:922
  222.2 7.1 %collective-permute-done.3 = f32[128,768]{1,0:T(8,128)} collective-permute-done((f32[128,768]{1,0:T(8,128)}, f32[128,768]{1,0:T(8,128)}, u32[]{:S(2)}, u32[]{:S(2)}) %collective-permute-start.3) | collective-permute-done | bytes 393248 | tf_op jit(solution)/shard_map/ppermute | solution.py:1011
  229.3 5.3 spread_rows.1.g_ref
  235.8 41.6 %encoder_feed_back.1 = (f32[1024,768]{1,0:T(8,128)}, f32[8,768]{1,0:T(8,128)}, f32[1,3072]{1,0:T(1,128)}, bf16[4,384,768]{2,1,0:T(8,128)(2,1)}, bf16[4,384,768]{...) custom-call(bf16[1024,768]{1,0:T(8,128)(2,1)} %copy-done.11, ...), custom_call_target="tpu_custom_call" | custom-call | flops 40000000000 | bytes 50000000 | tf_op jit(solution)/shard_map/encoder_feed_back/pallas_call | solution.py:327
  279.0 54.4 %encoder_attend_back.1 = (f32[1024,768]{1,0:T(8,128)}, f32[8,768]{1,0:T(8,128)}, bf16[4,288,768]{2,1,0:T(8,128)(2,1)}, bf16[4,288,768]{2,1,0:T(8,128)(2,1)}) custom-call(f32[1024,768]{1,0:T(8,128)} %get-tuple-element.90.dmix_ref, bf16[1024,768]{1,0:T(8,128)(2,1)} %bitcast.94, bf16[3,1024,768]{2,1,0:T(8,128)(2,1)} %get-tuple-element.91.qkv_ref, ...), custom_call_target="tpu_custom_call" | custom-call | flops 49999998976 | bytes 40000000 | tf_op jit(solution)/shard_map/encoder_attend_back/pallas_call | solution.py:439
  335.1 200.5 %sum_pairs.1 = (bf16[7,384,768]{2,1,0:T(8,128)(2,1)}, f32[32,768]{1,0:T(8,128)}) custom-call(bf16[4,384,768]{2,1,0:T(8,128)(2,1)} %get-tuple-element.99.refs_0_, bf16[4,384,768]{2,1,0:T(8,128)(2,1)} %get-tuple-element.100.refs_1_, bf16[4,288,768]{2,1,0:T(8,128)(2,1)} %copy-done.1, bf16[4,96,768]{2,1,0:T(8,128)(2,1)} %get-tuple-element.103.refs_3_, ...), custom_call_target="tpu_custom_call" | custom-call | flops 100000000 | bytes 100000000 | tf_op jit(solution)/shard_map/sum_pairs/pallas_call | solution.py:1198
  536.9 1.8 bitcast_convert_fusion.2
  538.7 3.5 bitcast_convert_fusion
  552.9 1.6 copy.78
  554.5 1.8 copy.79
  (131 shorter events, 37.7 us)
Async XLA Ops:
  2.5 69.5 %collective-permute-start = (s32[131,1024]{1,0:T(8,128)S(1)}, s32[131,1024]{1,0:T(8,128)S(1)}, u32[]{:S(2)}, u32[]{:S(2)}) collective-permute-start(s32[131,1024]{1,0:T(8,128)S(1)} %pad_add_fusion), channel_id=1, source_target_pairs={{0,2},{1,3},{2,0},{3,1},{4,6},{5,7},{6,4},{7,5},{8,10},{9,11},{10,... | collective-permute-start | bytes 1609736 | tf_op jit(solution)/shard_map/ppermute | solution.py:1011
  7.6 63.7 %collective-permute-start.1 = (bf16[256,768]{1,0:T(8,128)(2,1)S(1)}, bf16[256,768]{1,0:T(8,128)(2,1)S(1)}, u32[]{:S(2)}, u32[]{:S(2)}) collective-permute-start(bf16[256,768]{1,0:T(8,128)(2,1)S(1)} %pad_maximum_fusion), channel_id=1, source_target_pairs={{0,2},{1,3},{2,0},{3,1},{4,6},{5,7},{6,4},{7,5},{8,10},{9,11},{10,... | collective-permute-start | bytes 1179656 | tf_op jit(solution)/shard_map/ppermute | solution.py:1011
  43.2 27.5 %copy-start.30 = (f32[768]{0:T(1024)S(1)}, f32[768]{0:T(1024)}, u32[]{:S(2)}) copy-start(f32[768]{0:T(1024)} %param.47) | copy-start | bytes 9220
  72.4 1.4 copy-start.10
  80.1 42.6 %all-to-all-start = ((bf16[8,256,768]{2,1,0:T(8,128)(2,1)}), bf16[8,256,768]{2,1,0:T(8,128)(2,1)}, u32[]{:S(2)}, u32[]{:S(2)}) async-start(bf16[8,256,768]{2,1,0:T(8,128)(2,1)} %bitcast.7), calls=%async_computation | async-start | bytes 6291456 | tf_op jit(solution)/shard_map/all_to_all | solution.py:1333
  85.1 6.6 %copy-start.3 = (bf16[3,768,768]{2,1,0:T(8,128)(2,1)S(1)}, bf16[3,768,768]{2,1,0:T(8,128)(2,1)}, u32[]{:S(2)}) copy-start(bf16[3,768,768]{2,1,0:T(8,128)(2,1)} %w_ref.11) | copy-start | bytes 10616836
  85.1 6.6 %copy-start.4 = (bf16[3,768,768]{2,1,0:T(8,128)(2,1)S(1)}, bf16[3,768,768]{2,1,0:T(8,128)(2,1)}, u32[]{:S(2)}) copy-start(bf16[3,768,768]{2,1,0:T(8,128)(2,1)} %cw_ref.3) | copy-start | bytes 10616836
  85.1 6.6 %copy-start.5 = (bf16[768,768]{1,0:T(8,128)(2,1)S(1)}, bf16[768,768]{1,0:T(8,128)(2,1)}, u32[]{:S(2)}) copy-start(bf16[768,768]{1,0:T(8,128)(2,1)} %wo_ref.7) | copy-start | bytes 3538948
  85.1 6.6 %copy-start.7 = (f32[6,768]{1,0:T(8,128)S(1)}, f32[6,768]{1,0:T(8,128)}, u32[]{:S(2)}) copy-start(f32[6,768]{1,0:T(8,128)} %b_ref.5) | copy-start | bytes 55300
  85.1 6.6 %copy-start.8 = (f32[3,2,768]{2,1,0:T(2,128)S(1)}, f32[3,2,768]{2,1,0:T(2,128)}, u32[]{:S(2)}) copy-start(f32[3,2,768]{2,1,0:T(2,128)} %n_ref.11) | copy-start | bytes 55300
  91.6 3.2 copy-start.12
  91.7 3.2 copy-start.13
  160.0 62.3 %collective-permute-start.2 = (bf16[128,768]{1,0:T(8,128)(2,1)}, bf16[128,768]{1,0:T(8,128)(2,1)}, u32[]{:S(2)}, u32[]{:S(2)}) collective-permute-start(bf16[128,768]{1,0:T(8,128)(2,1)} %get-tuple-element.80), channel_id=1, source_target_pairs={{0,2},{1,3},{2,0},{3,1},{4,6},{5,7},{6,4},{7,5},{8,10},{9,11},{10,... | collective-permute-start | bytes 589832 | tf_op jit(solution)/shard_map/ppermute | solution.py:1011
  187.2 3.9 copy-start.9
  187.3 42.1 %all-to-all-start.1 = ((bf16[8,256,768]{2,1,0:T(8,128)(2,1)}), bf16[8,256,768]{2,1,0:T(8,128)(2,1)S(1)}, u32[]{:S(2)}, u32[]{:S(2)}) async-start(bf16[8,256,768]{2,1,0:T(8,128)(2,1)} %bitcast.79), calls=%async_computation.1 | async-start | bytes 6291456 | tf_op jit(solution)/shard_map/all_to_all | solution.py:1358
  197.3 11.7 %copy-start.27 = (f32[8,768]{1,0:T(8,128)S(1)}, f32[8,768]{1,0:T(8,128)}, u32[]{:S(2)}) copy-start(f32[8,768]{1,0:T(8,128)} %get-tuple-element.123) | copy-start | bytes 73732
  197.3 11.7 %copy-start.16 = (f32[128,768]{1,0:T(8,128)S(1)}, f32[128,768]{1,0:T(8,128)}, u32[]{:S(2)}) copy-start(f32[128,768]{1,0:T(8,128)} %copy-done.14) | copy-start | bytes 1179652
  197.3 11.7 %copy-start.18 = (bf16[128,768]{1,0:T(8,128)(2,1)S(1)}, bf16[128,768]{1,0:T(8,128)(2,1)}, u32[]{:S(2)}) copy-start(bf16[128,768]{1,0:T(8,128)(2,1)} %get-tuple-element.95.cdq_ref.dq_ref) | copy-start | bytes 589828
  206.8 1.4 copy-start
  208.2 21.1 %collective-permute-start.3 = (f32[128,768]{1,0:T(8,128)}, f32[128,768]{1,0:T(8,128)}, u32[]{:S(2)}, u32[]{:S(2)}) collective-permute-start(f32[128,768]{1,0:T(8,128)} %get-tuple-element.98), channel_id=1, source_target_pairs={{0,2},{1,3},{2,0},{3,1},{4,6},{5,7},{6,4},{7,5},{8,10},{9,11},{10,... | collective-permute-start | bytes 1179656 | tf_op jit(solution)/shard_map/ppermute | solution.py:1011
  279.0 55.3 %copy-start.26 = (f32[22272]{0:T(1024)S(1)}, f32[22272]{0:T(1024)}, u32[]{:S(2)}) copy-start(f32[22272]{0:T(1024)} %custom-call) | copy-start | bytes 267268
  279.0 55.3 %copy-start.29 = (f32[1,3072]{1,0:T(1,128)S(1)}, f32[1,3072]{1,0:T(1,128)}, u32[]{:S(2)}) copy-start(f32[1,3072]{1,0:T(1,128)} %get-tuple-element.120) | copy-start | bytes 36868
  279.0 55.3 %copy-start.28 = (f32[1,3072]{1,0:T(1,128)S(1)}, f32[1,3072]{1,0:T(1,128)}, u32[]{:S(2)}) copy-start(f32[1,3072]{1,0:T(1,128)} %get-tuple-element.124) | copy-start | bytes 36868
  535.6 3.1 copy-start.25
  (13 other events, 12.7 us)

commit v3 on v2

--- a/solution.py
+++ b/solution.py
@@ -81,12 +81,22 @@
     return pltpu.CompilerParams(vmem_limit_bytes=limit * 2**20, **rest)
 
 
+def host_params(plan):
+    if plan:
+        return params(62, collective_id=plan.collective_id, has_side_effects=True)
+    return params()
+
+
 def cost(flops, size, exps=0):
     return pl.CostEstimate(flops=int(flops), bytes_accessed=int(size), transcendentals=int(exps))
 
 
 def full(*shape):
     return pl.BlockSpec(shape, lambda *_: (0,) * len(shape))
+
+
+def once(*shape):
+    return pl.BlockSpec(shape, lambda *_: (0,) * len(shape), pipeline_mode=pl.Buffered(1))
 
 
 def like(shape, dtype):
@@ -146,7 +156,7 @@
 
 
 def encoder_attend_kernel(
-    x_ref, w_ref, wo_ref, bg_ref, b_ref, qkv_ref, c_ref, stat_ref, mixed_ref, stats
+    x_ref, w_ref, wo_ref, bg_ref, b_ref, qkv_ref, c_ref, cl_ref, stat_ref, mixed_ref, stats
 ):
     group = pl.program_id(0)
     tokens = x_ref.shape[0]
@@ -175,6 +185,7 @@
             context += dot(low(weights), qkv_ref[2]) * (lanes[h] * (1.0 / total))
             stat = jnp.where(lane == h, top + jnp.log(total), stat)
         c_ref[rows, :] = context
+        cl_ref[rows, :] = low(context)
         stats[rows, :] = stat
         mixed_ref[rows, :] += dot(low(context), wo_ref[...])
         return carry
@@ -199,12 +210,14 @@
         out_specs=[
             pl.BlockSpec((3, tokens, GROUP), lambda g: (0, 0, g)),
             pl.BlockSpec((tokens, GROUP), lambda g: (0, g)),
+            pl.BlockSpec((tokens, GROUP), lambda g: (0, g)),
             pl.BlockSpec((1, 8, tokens), lambda g: (g, 0, 0)),
             full(tokens, width),
         ],
         out_shape=[
             like((3, tokens, width), low_type),
             like((tokens, width), wide_type),
+            like((tokens, width), low_type),
             like((groups, 8, tokens), wide_type),
             like((tokens, width), wide_type),
         ],
@@ -224,9 +237,14 @@
 
     @pl.when(step == 0)
     def _():
-        first = norm_rows(mixed_ref[...], n_ref[0, 0:1], n_ref[0, 1:2])
-        a_low[...] = low(first)
-        sum_ref[...] = first + sb_ref[...]
+        def rows_step(i, carry):
+            rows = pl.ds(pl.multiple_of(i * 128, 128), 128)
+            first = norm_rows(mixed_ref[rows, :], n_ref[0, 0:1], n_ref[0, 1:2])
+            a_low[rows, :] = low(first)
+            sum_ref[rows, :] = first + sb_ref[...]
+            return carry
+
+        lax.fori_loop(0, tokens // 128, rows_step, 0)
 
     for i in range(tokens // block):
         rows = slice(i * block, (i + 1) * block)
@@ -237,7 +255,12 @@
 
     @pl.when(step == pl.num_programs(0) - 1)
     def _():
-        out_ref[...] = low(norm_rows(sum_ref[...], n_ref[1, 0:1], n_ref[1, 1:2]))
+        def rows_step(i, carry):
+            rows = pl.ds(pl.multiple_of(i * 128, 128), 128)
+            out_ref[rows, :] = low(norm_rows(sum_ref[rows, :], n_ref[1, 0:1], n_ref[1, 1:2]))
+            return carry
+
+        lax.fori_loop(0, tokens // 128, rows_step, 0)
 
 
 def encoder_feed(mixed, norms, expand, expand_bias, shrink, shrink_bias):
@@ -274,26 +297,58 @@
     )(mixed, norms, expand, expand_bias[None], shrink, shrink_bias[None])
 
 
-def encoder_feed_back_kernel(
-    g_ref, sum_ref, mixed_ref, h_ref, d_ref, c_ref, n_ref, e_ref, s_ref, *rest
-):
-    dmix_ref, vec_ref, eb_ref = rest[:3]
-    back_low, a_turned, between, hold = rest[-4:]
-    wide_outs, tall_outs, out_outs = thirds(rest[3:-4])
+def split_refs(refs, *counts):
+    out, at = [], 0
+    for count in counts:
+        out.append(refs[at : at + count])
+        at += count
+    return out + [refs[at:]]
+
+
+def hosting(plan):
+    return (plan.ins, len(plan.outs())) if plan else (0, 0)
+
+
+def encoder_feed_back_kernel(plan, *refs):
+    grads = 6 if paired() else 3
+    host_ins, host_outs = hosting(plan)
+    main, guests, outs, guest_outs, scratch, guest_scratch = split_refs(
+        refs, 9, host_ins, 3 + grads, host_outs, 4
+    )
+    g_ref, sum_ref, mixed_ref, h_ref, d_ref, c_ref, n_ref, e_ref, s_ref = main
+    dmix_ref, vec_ref, eb_ref = outs[:3]
+    wide_outs, tall_outs, out_outs = thirds(outs[3:])
+    back_low, a_turned, between, hold = scratch
     step = pl.program_id(0)
+    sums = plan.open(guests, guest_outs, guest_scratch) if plan else None
+
+    def place(n):
+        if sums:
+            sums.slot(step, 4, 3, n)
+
+    place(0)
     tokens = sum_ref.shape[0]
     block = 256
 
     @pl.when(step == 0)
     def _():
-        grad, gain, offset = norm_rows_back(sum_ref[...], n_ref[1, 0:1], wide(g_ref[...]))
-        dmix_ref[...] = grad
-        back_low[...] = low(grad)
         vec_ref[...] = jnp.zeros(vec_ref.shape, wide_type)
-        vec_ref[0:1] = gain
-        vec_ref[1:2] = offset
-        vec_ref[2:3] = jnp.sum(wide(back_low[...]), 0, keepdims=True)
-        a_turned[...] = low(norm_rows(mixed_ref[...], n_ref[0, 0:1], n_ref[0, 1:2])).T
+
+        def rows_step(i, carry):
+            rows = pl.ds(pl.multiple_of(i * 128, 128), 128)
+            grad, gain, offset = norm_rows_back(
+                sum_ref[rows, :], n_ref[1, 0:1], wide(g_ref[rows, :])
+            )
+            dmix_ref[rows, :] = grad
+            back_low[rows, :] = low(grad)
+            vec_ref[0:1] += gain
+            vec_ref[1:2] += offset
+            vec_ref[2:3] += jnp.sum(wide(low(grad)), 0, keepdims=True)
+            first = norm_rows(mixed_ref[rows, :], n_ref[0, 0:1], n_ref[0, 1:2])
+            a_turned[:, rows] = low(first).T
+            return carry
+
+        lax.fori_loop(0, tokens // 128, rows_step, 0)
 
     column = jnp.zeros(eb_ref.shape, wide_type)
     for i in range(tokens // block):
@@ -302,6 +357,8 @@
         between[rows, :] = before
         column += jnp.sum(wide(before), 0, keepdims=True)
         dmix_ref[rows, :] += dot(before, e_ref[...], NT)
+        if i == 1:
+            place(1)
     eb_ref[...] = column
     hold[...] = dot(a_turned[...], between[...])
     emit(wide_outs, step, hold)
@@ -310,33 +367,47 @@
 
     @pl.when(step == pl.num_programs(0) - 1)
     def _():
-        grad, gain, offset = norm_rows_back(mixed_ref[...], n_ref[0, 0:1], dmix_ref[...])
-        dmix_ref[...] = grad
-        back_low[...] = low(grad)
-        vec_ref[3:4] = gain
-        vec_ref[4:5] = offset
-        vec_ref[5:6] = jnp.sum(wide(back_low[...]), 0, keepdims=True)
-        hold[...] = dot(low(c_ref[...]), back_low[...], TN)
+
+        def rows_step(i, carry):
+            rows = pl.ds(pl.multiple_of(i * 128, 128), 128)
+            grad, gain, offset = norm_rows_back(
+                mixed_ref[rows, :], n_ref[0, 0:1], dmix_ref[rows, :]
+            )
+            dmix_ref[rows, :] = grad
+            back_low[rows, :] = low(grad)
+            vec_ref[3:4] += gain
+            vec_ref[4:5] += offset
+            vec_ref[5:6] += jnp.sum(wide(low(grad)), 0, keepdims=True)
+            return carry
+
+        lax.fori_loop(0, tokens // 128, rows_step, 0)
+        hold[...] = dot(c_ref[...], back_low[...], TN)
         emit(out_outs, 0, hold)
 
-
-def encoder_feed_back(grad, summed, mixed, hidden, slope, context, norms, expand, shrink):
+    place(2)
+
+
+def encoder_feed_back(
+    grad, summed, mixed, hidden, slope, context, norms, expand, shrink, plan=None, guests=()
+):
     tokens, width = mixed.shape
     total = expand.shape[1]
     cut = total // 4
+    guest_outs = plan.outs() if plan else []
     outs = pl.pallas_call(
-        encoder_feed_back_kernel,
+        functools.partial(encoder_feed_back_kernel, plan),
         grid=(4,),
         in_specs=[
-            full(tokens, width),
-            full(tokens, width),
-            full(tokens, width),
+            once(tokens, width),
+            once(tokens, width),
+            once(tokens, width),
             pl.BlockSpec((tokens, cut), lambda i: (0, i)),
             pl.BlockSpec((tokens, cut), lambda i: (0, i)),
-            full(tokens, width),
+            once(tokens, width),
             full(2, 2, width),
             pl.BlockSpec((width, cut), lambda i: (0, i)),
             pl.BlockSpec((cut, width), lambda i: (i, 0)),
+            *(plan.in_specs() if plan else []),
         ],
         out_specs=[
             full(tokens, width),
@@ -345,6 +416,7 @@
             *grad_specs(4, width, width),
             *grad_specs(1, total, width),
             *grad_specs(1, width, width),
+            *[spec for spec, _ in guest_outs],
         ],
         out_shape=[
             like((tokens, width), wide_type),
@@ -353,29 +425,38 @@
             *grad_shapes(4, width, width),
             *grad_shapes(1, total, width),
             *grad_shapes(1, width, width),
+            *[shape for _, shape in guest_outs],
         ],
         scratch_shapes=[
             VMEM((tokens, width), low_type),
             VMEM((width, tokens), low_type),
             VMEM((tokens, cut), low_type),
             VMEM((width, width), wide_type),
-        ],
-        compiler_params=params(),
+            *(plan.scratch() if plan else []),
+        ],
+        compiler_params=host_params(plan),
         cost_estimate=cost(4e10, 5e7),
         name="encoder_feed_back",
-    )(grad, summed, mixed, hidden, slope, context, norms, expand, shrink)
-    return outs[:3], thirds(outs[3:])
-
-
-def encoder_attend_back_kernel(
-    dmix_ref, x_ref, qkv_ref, c_ref, stat_ref, w_ref, wo_ref, *rest
-):
-    dx_ref, vec_ref = rest[:2]
-    outs, (dmix_low, x_turned, dc, weights, scores_back, dk, dv, dq_turned, hold) = (
-        rest[2:-9],
-        rest[-9:],
-    )
+    )(grad, summed, mixed, hidden, slope, context, norms, expand, shrink, *guests)
+    main = len(outs) - len(guest_outs)
+    return outs[:3], thirds(outs[3:main]), outs[main:]
+
+
+def encoder_attend_back_kernel(plan, *refs):
+    host_ins, host_outs = hosting(plan)
+    main, guests, (dx_ref, vec_ref), outs, guest_outs, scratch, guest_scratch = split_refs(
+        refs, 7, host_ins, 2, 2 if paired() else 1, host_outs, 9
+    )
+    dmix_ref, x_ref, qkv_ref, c_ref, stat_ref, w_ref, wo_ref = main
+    dmix_low, x_turned, dc, weights, scores_back, dk, dv, dq_turned, hold = scratch
     group = pl.program_id(0)
+    sums = plan.open(guests, guest_outs, guest_scratch) if plan else None
+
+    def place(n):
+        if sums:
+            sums.slot(group, 3, 3, n)
+
+    place(0)
     tokens = x_ref.shape[0]
     block = 256
     heads = GROUP // HEAD
@@ -419,6 +500,8 @@
             )
         dv[...] += dot(weights[...], dc_heads)
         dk[...] += dot(scores_back[...], q_heads)
+        if i == 1:
+            place(1)
     dq = low(dq_turned[...].T * scale_scores)
     dk_low, dv_low = low(dk[...]), low(dv[...])
     vec_ref[...] = jnp.zeros(vec_ref.shape, wide_type)
@@ -430,33 +513,40 @@
     for part, grad in enumerate((dq, dk_low, dv_low)):
         hold[...] = dot(x_turned[...], grad)
         emit(outs, part, hold)
-
-
-def encoder_attend_back(dmix, x, qkv, context, stats, inward, outward):
+    place(2)
+
+
+def encoder_attend_back(
+    dmix, x, qkv, context, stats, inward, outward, plan=None, guests=()
+):
     tokens, width = x.shape
     groups = width // GROUP
     specs = grad_specs(3, width, GROUP, lambda g: (0, 0, g))
+    guest_outs = plan.outs() if plan else []
     outs = pl.pallas_call(
-        encoder_attend_back_kernel,
+        functools.partial(encoder_attend_back_kernel, plan),
         grid=(groups,),
         in_specs=[
-            full(tokens, width),
-            full(tokens, width),
+            once(tokens, width),
+            once(tokens, width),
             pl.BlockSpec((3, tokens, GROUP), lambda g: (0, 0, g)),
             pl.BlockSpec((tokens, GROUP), lambda g: (0, g)),
             pl.BlockSpec((1, 8, tokens), lambda g: (g, 0, 0)),
             pl.BlockSpec((3, width, GROUP), lambda g: (0, 0, g)),
             pl.BlockSpec((GROUP, width), lambda g: (g, 0)),
+            *(plan.in_specs() if plan else []),
         ],
         out_specs=[
             full(tokens, width),
             pl.BlockSpec((8, GROUP), lambda g: (0, g)),
             *specs,
+            *[spec for spec, _ in guest_outs],
         ],
         out_shape=[
             like((tokens, width), wide_type),
             like((8, width), wide_type),
             *grad_shapes(3, width, width),
+            *[shape for _, shape in guest_outs],
         ],
         scratch_shapes=[
             VMEM((tokens, width), low_type),
@@ -468,12 +558,14 @@
             VMEM((tokens, GROUP), wide_type),
             VMEM((GROUP, tokens), wide_type),
             VMEM((width, GROUP), wide_type),
-        ],
-        compiler_params=params(),
+            *(plan.scratch() if plan else []),
+        ],
+        compiler_params=host_params(plan),
         cost_estimate=cost(5e10, 4e7, 1.3e7),
         name="encoder_attend_back",
-    )(dmix, x, qkv, context, stats, inward, outward)
-    return outs[:2], outs[2:]
+    )(dmix, x, qkv, context, stats, inward, outward, *guests)
+    main = len(outs) - len(guest_outs)
+    return outs[:2], outs[2:main], outs[main:]
 
 
 def mask_kernel(slots_ref, across_ref, down_ref):
@@ -719,7 +811,8 @@
 ):
     out_ref, joined_back_ref, dc_ref, vec_ref, deb_ref = rest[:5]
     hidden, slope, between, hold = rest[-4:]
-    wide_outs, tall_outs, out_outs = thirds(rest[5:-4])
+    feed_ref, out_outs = rest[5], rest[6:-4]
+    parts = feed_ref.shape[0]
     width = mixed_ref.shape[1]
     blocks = [slice(i * width, (i + 1) * width) for i in range(e_ref.shape[1] // width)]
     first = norm_rows(mixed_ref[...], n_ref[0, 0:1], n_ref[0, 1:2])
@@ -755,10 +848,14 @@
     vec_ref[5:6] = jnp.sum(wide(joined_low), 0, keepdims=True)
     dc_ref[...] = low(dot(joined_low, co_ref[...], NT))
     for i, part in enumerate(blocks):
-        hold[...] = dot(second_low, between[:, part], TN)
-        emit(wide_outs, i, hold)
-        hold[...] = dot(hidden[:, part], summed_low, TN)
-        emit_tall(tall_outs, i, hold)
+        rows = width // parts
+        grad = low(dot(second_low, between[:, part], TN))
+        for n in range(parts):
+            feed_ref[n, i * rows : (i + 1) * rows, :] = grad[n * rows : (n + 1) * rows]
+        grad = low(dot(hidden[:, part], summed_low, TN))
+        rows, first = 4 * rows, i * parts // 4
+        for n in range(parts // 4):
+            feed_ref[first + n, rows:, :] = grad[n * rows : (n + 1) * rows]
     hold[...] = dot(context, joined_low, TN)
     emit(out_outs, 0, hold)
 
@@ -766,6 +863,7 @@
 def middle(mixed, context, outward, biases, norms, expand, expand_bias, shrink, shrink_bias, grad):
     rows, width = mixed.shape
     total = expand.shape[1]
+    parts = lax.axis_size("dp")
     ins = (
         mixed,
         context,
@@ -788,8 +886,7 @@
             full(rows, width),
             full(8, width),
             full(1, total),
-            *grad_specs(4, width, width),
-            *grad_specs(1, total, width),
+            full(parts, 2 * total // parts, width),
             *grad_specs(1, width, width),
         ],
         out_shape=[
@@ -798,8 +895,7 @@
             like((rows, width), low_type),
             like((8, width), wide_type),
             like((1, total), wide_type),
-            *grad_shapes(4, width, width),
-            *grad_shapes(1, total, width),
+            like((parts, 2 * total // parts, width), low_type),
             *grad_shapes(1, width, width),
         ],
         scratch_shapes=[
@@ -812,7 +908,7 @@
         cost_estimate=cost(2e10, 2.2e7),
         name="middle",
     )(*ins)
-    return outs[:5], thirds(outs[5:])
+    return outs[:5], outs[5], outs[6:]
 
 
 def cross_back_kernel(
@@ -1006,16 +1102,16 @@
     return outs[:2], outs[2:]
 
 
+CUT = 192
+HALF = CUT // 2
+QUARTER = CUT // 4
+VEC_ROWS = 32
+MESH = pl.DeviceIdType.MESH
+
+
 def shifted(value, axis, by):
     length = lax.axis_size(axis)
     return lax.ppermute(value, axis, [(i, (i + by) % length) for i in range(length)])
-
-
-COUNT = 7
-ROWS = 384
-HALF = ROWS // 2
-QUARTER = ROWS // 4
-VEC_ROWS = 32
 
 
 def add_rows(to, other, rows):
@@ -1041,190 +1137,480 @@
 def greet():
     barrier = pltpu.get_barrier_semaphore()
     for partner in partners():
-        pl.semaphore_signal(barrier, 1, device_id=partner, device_id_type=pl.DeviceIdType.MESH)
+        pl.semaphore_signal(barrier, 1, device_id=partner, device_id_type=MESH)
     pl.semaphore_wait(barrier, 5)
 
 
-def sum_kernel(sources, *refs):
-    count = len(sources)
-    keeps, sends, vec_ref = refs[:count], refs[count : 2 * count], refs[2 * count]
-    out_ref, vec_out = refs[2 * count + 1 : 2 * count + 3]
-    own, from_core, from_one, from_two, from_three, from_four, whole, vec_in = refs[
-        2 * count + 3 : 2 * count + 11
-    ]
-    load_sems, core_send, core_recv, send_sems, recv_sems, vec_send, vec_recv, out_sems = refs[
-        2 * count + 11 :
-    ]
-    core, over_x, over_y, near, far = partners()
-    section = lax.axis_index("section")
-    side = section % 2
-    far_side = section // 2
-    half_at = pl.multiple_of(side * HALF, HALF)
-    half_other = pl.multiple_of((1 - side) * HALF, HALF)
-    quarter_at = pl.multiple_of(side * HALF + far_side * QUARTER, QUARTER)
-    quarter_other = pl.multiple_of(side * HALF + (1 - far_side) * QUARTER, QUARTER)
-    upper, lower = pl.ds(0, HALF), pl.ds(HALF, HALF)
-
-    def remote(source, to, send, recv, partner):
+def laid_out(pieces):
+    out, at = [], 0
+    for n, first, size in pieces:
+        row = first
+        while row < first + size:
+            rows = min(CUT - at % CUT, first + size - row)
+            out.append((n, row, rows, at // CUT, at % CUT))
+            row, at = row + rows, at + rows
+    return tuple(out), at // CUT
+
+
+class Plan:
+    def __init__(self, pieces, arrived, schedule, collective_id, onward=False, vector=False):
+        self.arrays = 1 + max(piece[0] for piece in pieces)
+        self.schedule, self.collective_id = schedule, collective_id
+        self.sources, self.fresh = laid_out(pieces)
+        self.from_kernels = tuple(arrived)
+        arrived = sum(self.from_kernels)
+        self.arrived, self.onward, self.vector = arrived, onward, vector
+        self.late = arrived + (self.fresh if onward else 0)
+        self.ins = 2 * self.arrays + len(self.from_kernels) + (1 if vector else 0)
+
+    def in_specs(self):
+        anywhere = pl.BlockSpec(memory_space=pl.ANY)
+        count = self.ins - (1 if self.vector else 0)
+        return [anywhere] * count + ([pl.BlockSpec(memory_space=VMEM)] if self.vector else [])
+
+    def outs(self):
+        out = []
+        if not self.onward:
+            out.append((pl.BlockSpec(memory_space=pl.ANY), like((self.fresh * CUT, WIDTH), low_type)))
+        if self.late:
+            out.append((pl.BlockSpec(memory_space=pl.ANY), like((self.late * CUT, WIDTH), low_type)))
+        if self.vector:
+            out.append((pl.BlockSpec(memory_space=VMEM), like((VEC_ROWS, WIDTH), wide_type)))
+        return out
+
+    def scratch(self):
+        dma = pltpu.SemaphoreType.DMA
+        fresh, late, arrived = self.fresh, max(self.late, 1), max(self.arrived, 1)
+        most = max(fresh, late)
+        count = len(self.sources)
+        return [
+            VMEM((fresh, 4, CUT, WIDTH), low_type),
+            VMEM((fresh, 4, CUT, WIDTH), low_type),
+            VMEM((fresh, 2, 2, HALF, WIDTH), low_type),
+            VMEM((fresh, 2, HALF, WIDTH), low_type),
+            VMEM((arrived, CUT, WIDTH if self.late else 128), low_type),
+            VMEM((late, HALF, WIDTH if self.late else 128), low_type),
+            VMEM((late, QUARTER, WIDTH if self.late else 128), low_type),
+            VMEM((late, CUT, WIDTH if self.late else 128), low_type),
+            VMEM((5, VEC_ROWS if self.vector else 8, WIDTH), wide_type),
+            dma((count,)),
+            dma((count,)),
+            dma((count,)),
+            dma((3, fresh, 3)),
+            dma((3, fresh, 3)),
+            dma((late, 4)),
+            dma((late, 4)),
+            dma((arrived,)),
+            dma((2, most)),
+            dma((5,)),
+            dma((5,)),
+        ]
+
+    def open(self, ins, outs, scratch):
+        return Sums(self, ins, outs, scratch)
+
+
+class Sums:
+    def __init__(self, plan, ins, outs, scratch):
+        count = plan.arrays
+        outs, ins = list(outs), list(ins)
+        self.plan = plan
+        self.keeps, self.sends = ins[:count], ins[count : 2 * count]
+        ins = ins[2 * count :]
+        self.arrived = [ins.pop(0) for _ in plan.from_kernels]
+        self.vec_ref = ins.pop(0) if plan.vector else None
+        self.shard_out = None if plan.onward else outs.pop(0)
+        self.late_out = outs.pop(0) if plan.late else None
+        self.vec_out = outs.pop(0) if plan.vector else None
+        (
+            self.own,
+            self.from_core,
+            self.from_one,
+            self.from_two,
+            self.waiting,
+            self.from_three,
+            self.from_four,
+            self.whole,
+            self.vec_in,
+            self.load_sems,
+            self.core_send,
+            self.core_recv,
+            self.send_sems,
+            self.recv_sems,
+            self.line_send,
+            self.line_recv,
+            self.arrive_sems,
+            self.out_sems,
+            self.vec_send,
+            self.vec_recv,
+        ) = scratch
+        self.core, self.over_x, self.over_y, self.near, self.far = partners()
+        section = lax.axis_index("section")
+        side, far_side = section % 2, section // 2
+        self.half_at = pl.multiple_of(side * HALF, HALF)
+        self.half_other = pl.multiple_of((1 - side) * HALF, HALF)
+        self.quarter_at = pl.multiple_of(side * HALF + far_side * QUARTER, QUARTER)
+        self.quarter_other = pl.multiple_of(side * HALF + (1 - far_side) * QUARTER, QUARTER)
+
+    def remote(self, source, to, send, recv, partner):
         return pltpu.make_async_remote_copy(
             src_ref=source,
             dst_ref=to,
             send_sem=send,
             recv_sem=recv,
             device_id=partner,
-            device_id_type=pl.DeviceIdType.MESH,
+            device_id_type=MESH,
         )
 
-    loads, first = [], []
-    for n, (chunk, row) in enumerate(sources):
-        rows = pl.ds(row, keeps[n].shape[1])
-        loads.append(
-            pltpu.make_async_copy(
-                keeps[n], own.at[chunk, :, rows], load_sems.at[n]
-            )
+    def load(self, s):
+        n, row, rows, chunk, at = self.plan.sources[s]
+        return pltpu.make_async_copy(
+            self.keeps[n].at[:, pl.ds(row, rows)],
+            self.own.at[chunk, :, pl.ds(at, rows)],
+            self.load_sems.at[s],
         )
-        first.append(
-            remote(sends[n], from_core.at[chunk, :, rows], core_send.at[n], core_recv.at[n], core)
+
+    def cross(self, s):
+        n, row, rows, chunk, at = self.plan.sources[s]
+        return self.remote(
+            self.sends[n].at[:, pl.ds(row, rows)],
+            self.from_core.at[chunk, :, pl.ds(at, rows)],
+            self.core_send.at[s],
+            self.core_recv.at[s],
+            self.core,
         )
 
-    def pairs(stage, c):
-        total = own.at[c, 0]
+    def arrive(self, k):
+        at, source = k, 0
+        while at >= self.plan.from_kernels[source]:
+            at, source = at - self.plan.from_kernels[source], source + 1
+        return pltpu.make_async_copy(
+            self.arrived[source].at[pl.ds(at * CUT, CUT)],
+            self.waiting.at[k],
+            self.arrive_sems.at[k],
+        )
+
+    def summed(self, k):
+        if k < self.plan.arrived:
+            return self.waiting.at[k]
+        return self.own.at[k - self.plan.arrived, 0]
+
+    def pairs(self, stage, c):
+        own, upper, lower = self.own, pl.ds(0, HALF), pl.ds(HALF, HALF)
         if stage == 1:
             return (
-                (own.at[c, pl.ds(1, 1), upper], from_one.at[c, 0, pl.ds(0, 1)], over_x),
-                (own.at[c, pl.ds(3, 1), upper], from_one.at[c, 0, pl.ds(1, 1)], over_x),
-                (own.at[c, pl.ds(2, 2), lower], from_one.at[c, 1], over_y),
+                (own.at[c, 1, upper], self.from_one.at[c, 0, 0], self.over_x),
+                (own.at[c, 3, upper], self.from_one.at[c, 0, 1], self.over_x),
+                (own.at[c, pl.ds(2, 2), lower], self.from_one.at[c, 1], self.over_y),
             )
-        if stage == 2:
-            return (
-                (own.at[c, 2, upper], from_two.at[c, 0], over_y),
-                (own.at[c, 1, lower], from_two.at[c, 1], over_x),
+        return (
+            (own.at[c, 2, upper], self.from_two.at[c, 0], self.over_y),
+            (own.at[c, 1, lower], self.from_two.at[c, 1], self.over_x),
+        )
+
+    def copies(self, stage, c):
+        return [
+            self.remote(
+                source, to, self.send_sems.at[stage, c, k], self.recv_sems.at[stage, c, k], partner
             )
+            for k, (source, to, partner) in enumerate(self.pairs(stage, c))
+        ]
+
+    def start(self, stage, c):
+        for copy in self.copies(stage, c):
+            copy.start()
+
+    def across(self, stage, k):
+        half = self.summed(k).at[pl.ds(self.half_other, HALF)]
+        quarter = self.summed(k).at[pl.ds(self.quarter_other, QUARTER)]
+        mine = self.whole.at[k, pl.ds(self.quarter_at, QUARTER)]
+        ours = self.whole.at[k, pl.ds(self.half_at, HALF)]
+        source, to, partner = (
+            (half, self.from_three.at[k], self.near),
+            (quarter, self.from_four.at[k], self.far),
+            (mine, mine, self.far),
+            (ours, ours, self.near),
+        )[stage - 3]
+        n = stage - 3
+        return self.remote(source, to, self.line_send.at[k, n], self.line_recv.at[k, n], partner)
+
+    def line(self, stage, k):
+        if stage == "go":
+            self.across(3, k).start()
+            return
+        self.across(stage, k).wait_recv()
         if stage == 3:
-            return ((total.at[pl.ds(half_other, HALF)], from_three.at[c], near),)
-        if stage == 4:
-            return ((total.at[pl.ds(quarter_other, QUARTER)], from_four.at[c], far),)
-        if stage == 5:
-            rows = pl.ds(quarter_at, QUARTER)
-            return ((whole.at[c, rows], whole.at[c, rows], far),)
-        rows = pl.ds(half_at, HALF)
-        return ((whole.at[c, rows], whole.at[c, rows], near),)
-
-    def copies(stage, c):
-        return [
-            remote(source, to, send_sems.at[stage, c, k], recv_sems.at[stage, c, k], partner)
-            for k, (source, to, partner) in enumerate(pairs(stage, c))
-        ]
-
-    def start(stage, c):
-        for copy in copies(stage, c):
-            copy.start()
-
-    def land(stage, c):
-        for copy in copies(stage, c):
+            add_rows(self.summed(k).at[pl.ds(self.half_at, HALF)], self.from_three.at[k], HALF)
+        elif stage == 4:
+            rows = pl.ds(self.quarter_at, QUARTER)
+            self.whole[k, rows, :] = low(wide(self.summed(k)[rows, :]) + wide(self.from_four[k]))
+        if stage < 6:
+            self.across(stage + 1, k).start()
+        else:
+            self.late_copy(k).start()
+
+    def shard_copy(self, c):
+        return pltpu.make_async_copy(
+            self.own.at[c, 0], self.shard_out.at[pl.ds(c * CUT, CUT)], self.out_sems.at[0, c]
+        )
+
+    def late_copy(self, k):
+        return pltpu.make_async_copy(
+            self.whole.at[k], self.late_out.at[pl.ds(k * CUT, CUT)], self.out_sems.at[1, k]
+        )
+
+    def vec_copy(self, stage):
+        return self.remote(
+            self.vec_out,
+            self.vec_in.at[stage],
+            self.vec_send.at[stage],
+            self.vec_recv.at[stage],
+            partners()[stage],
+        )
+
+    def vec_step(self, stage):
+        if stage:
+            self.vec_copy(stage - 1).wait()
+            self.vec_out[...] += self.vec_in[stage - 1]
+        else:
+            self.vec_out[...] = self.vec_ref[...]
+        if stage < 5:
+            self.vec_copy(stage).start()
+
+    def begin(self):
+        greet()
+        for s in range(len(self.plan.sources)):
+            self.cross(s).start()
+            self.load(s).start()
+        for k in range(self.plan.arrived):
+            self.arrive(k).start()
+
+    def step(self, stage, c):
+        if stage == "vec":
+            self.vec_step(c)
+            return
+        if stage == "go":
+            self.arrive(c).wait()
+            self.line("go", c)
+            return
+        if stage > 2:
+            self.line(stage, c)
+            return
+        if stage == 0:
+            for s, source in enumerate(self.plan.sources):
+                if source[3] == c:
+                    self.load(s).wait()
+                    self.cross(s).wait_recv()
+            for at in range(4):
+                add_rows(self.own.at[c, at], self.from_core.at[c, at], CUT)
+            self.start(1, c)
+            return
+        for copy in self.copies(stage, c):
             copy.wait_recv()
-
-    def out_copy(c):
-        return pltpu.make_async_copy(whole.at[c], out_ref.at[c], out_sems.at[c])
-
-    def vec_copy(stage):
-        return remote(
-            vec_out, vec_in.at[stage], vec_send.at[stage], vec_recv.at[stage], partners()[stage]
-        )
-
-    def vec_step(stage):
-        if stage:
-            vec_copy(stage - 1).wait()
-            vec_out[...] += vec_in[stage - 1]
-        else:
-            vec_out[...] = vec_ref[...]
-        if stage < 5:
-            vec_copy(stage).start()
-
-    def step(stage, c):
-        if stage == 0:
-            for n, (chunk, _) in enumerate(sources):
-                if chunk == c:
-                    loads[n].wait()
-                    first[n].wait_recv()
-            for at in range(4):
-                add_rows(own.at[c, at], from_core.at[c, at], ROWS)
-            start(1, c)
-            return
-        land(stage, c)
+        upper, lower = pl.ds(0, HALF), pl.ds(HALF, HALF)
         if stage == 1:
             for k in range(2):
-                add_rows(own.at[c, 2 * k, upper], from_one.at[c, 0, k], HALF)
-                add_rows(own.at[c, k, lower], from_one.at[c, 1, k], HALF)
-        elif stage == 2:
-            add_rows(own.at[c, 0, upper], from_two.at[c, 0], HALF)
-            add_rows(own.at[c, 0, lower], from_two.at[c, 1], HALF)
+                add_rows(self.own.at[c, 2 * k, upper], self.from_one.at[c, 0, k], HALF)
+                add_rows(self.own.at[c, k, lower], self.from_one.at[c, 1, k], HALF)
+            self.start(2, c)
+        else:
+            add_rows(self.own.at[c, 0, upper], self.from_two.at[c, 0], HALF)
+            add_rows(self.own.at[c, 0, lower], self.from_two.at[c, 1], HALF)
+            if self.plan.onward:
+                self.line("go", self.plan.arrived + c)
+            else:
+                self.shard_copy(c).start()
+
+    def finish(self):
+        for s in range(len(self.plan.sources)):
+            self.cross(s).wait_send()
+        for c in range(self.plan.fresh):
+            for stage in (1, 2):
+                for copy in self.copies(stage, c):
+                    copy.wait_send()
+            if not self.plan.onward:
+                self.shard_copy(c).wait()
+        for k in range(self.plan.late):
+            for stage in (3, 4, 5, 6):
+                self.across(stage, k).wait_send()
+            self.late_copy(k).wait()
+
+    def slot(self, grid_step, steps, slots, slot):
+        for n in range(steps):
+            wanted = self.plan.schedule.get(n * slots + slot, ())
+            if not wanted:
+                continue
+
+            @pl.when(grid_step == n)
+            def _(wanted=wanted):
+                for stage, c in wanted:
+                    if stage == "begin":
+                        self.begin()
+                    elif stage == "finish":
+                        self.finish()
+                    else:
+                        self.step(stage, c)
+
+
+def last_sums_kernel(plan, *refs):
+    ins, rest = refs[: plan.ins], refs[plan.ins :]
+    count = len(plan.outs())
+    sums = plan.open(ins, rest[:count], rest[count:])
+    sums.begin()
+    for stage, c in plan.schedule:
+        sums.step(stage, c)
+    sums.finish()
+
+
+def last_sums(plan, pairs, arrived, vector):
+    outs = plan.outs()
+    return pl.pallas_call(
+        functools.partial(last_sums_kernel, plan),
+        in_specs=plan.in_specs(),
+        out_specs=[spec for spec, _ in outs],
+        out_shape=[shape for _, shape in outs],
+        scratch_shapes=plan.scratch(),
+        compiler_params=params(60, collective_id=plan.collective_id, has_side_effects=True),
+        cost_estimate=cost(1e8, 1e8),
+        name="last_sums",
+    )(*[p[0] for p in pairs], *[p[1] for p in pairs], *arrived, vector)
+
+
+def landing_order(fresh, arrived, onward, vector=False, first=0.0):
+    free = {}
+    events, steps = [], []
+
+    def send(time, takes, *links):
+        begin = max([time] + [free.get(link, 0.0) for link in links])
+        for link in links:
+            free[link] = begin + takes
+        return begin + takes + 1.5
+
+    def push(time, stage, c):
+        events.append((time, len(steps) + len(events), stage, c))
+
+    for c in range(fresh):
+        push(first + 4.0 + 2.2 * c, 0, c)
+    for k in range(arrived):
+        push(first + 3.0 + 0.3 * k, "go", k)
+    if vector:
+        push(first, "vec", 0)
+    while events:
+        event = min(events)
+        events.remove(event)
+        time, _, stage, c = event
+        steps.append((time, stage, c))
+        if stage == "vec":
+            if c < 5:
+                push(time + 5.0, "vec", c + 1)
+        elif stage == 0:
+            if free.get("xy", 0.0) > time + 2.5:
+                steps.pop()
+                push(free["xy"] - 2.0, 0, c)
+            else:
+                push(send(time, 6.6, "xy"), 1, c)
+        elif stage == 1:
+            push(send(time, 3.3, "xy"), 2, c)
+        elif stage == 2 and not onward:
+            pass
+        elif stage in ("go", 2):
+            push(send(time, 3.3, "out"), 3, c + (arrived if stage == 2 else 0))
         elif stage == 3:
-            add_rows(own.at[c, 0, pl.ds(half_at, HALF)], from_three.at[c], HALF)
+            push(send(time, 3.3, "mid", "out"), 4, c)
         elif stage == 4:
-            rows = pl.ds(quarter_at, QUARTER)
-            whole[c, rows, :] = low(wide(own[c, 0, rows, :]) + wide(from_four[c]))
-        if stage < 6:
-            start(stage + 1, c)
-        else:
-            out_copy(c).start()
-
-    greet()
-    for n in range(count):
-        first[n].start()
-        loads[n].start()
-    vec_step(0)
-    for time in range(COUNT + 6):
-        for stage in reversed(range(7)):
-            if 0 <= time - stage < COUNT:
-                step(stage, time - stage)
-        if 1 <= time + 1 <= 5:
-            vec_step(time + 1)
-    for n in range(count):
-        first[n].wait_send()
-    for c in range(COUNT):
-        for stage in range(1, 7):
-            for copy in copies(stage, c):
-                copy.wait_send()
-        out_copy(c).wait()
-
-
-def sum_pairs(pairs, sources, vector):
-    count = len(pairs)
-    width = pairs[0][0].shape[2]
-    anywhere = pl.BlockSpec(memory_space=pl.ANY)
+            push(send(time, 3.3, "mid", "out"), 5, c)
+        elif stage == 5:
+            push(send(time, 3.3, "out"), 6, c)
+    return steps
+
+
+def feed_plan():
+    schedule = {
+        0: [("begin", 0)],
+        1: [(0, 0), (0, 1), (0, 2)],
+        9: [(1, 0), (1, 1), (1, 2)],
+        11: [(2, 0), (2, 1), (2, 2), ("finish", 0)],
+    }
+    return Plan(((0, 0, 288), (1, 0, 96), (2, 0, 192)), (), schedule, 1)
+
+
+def attend_plan():
+    schedule = {
+        0: [("begin", 0)],
+        1: [(0, 0), (0, 1), (0, 2), (0, 3), (0, 4)],
+        6: [(1, 0), (1, 1), (1, 2)],
+        7: [(1, 3), (1, 4), (2, 0), (2, 1)],
+        8: [(2, 2), (2, 3), (2, 4), ("finish", 0)],
+    }
+    return Plan(((0, 192, 192), (1, 0, 384), (2, 0, 384)), (), schedule, 2)
+
+
+def last_plan():
+    order = [step[1:] for step in landing_order(2, 5, True, True)]
+    return Plan(((0, 0, 288), (1, 0, 96)), (5,), order, 3, onward=True, vector=True)
+
+
+def unpack_kernel(first_ref, last_ref, vec_ref, *outs):
+    (
+        e_in, e_out, e_bias, e_norm, e_expand, e_expand_bias, e_shrink, e_shrink_bias,
+        s_in, s_out, c_in, c_out, d_bias, d_norm, d_expand, d_expand_bias, d_shrink, d_shrink_bias,
+    ) = outs
+    rows = e_out.shape[0]
+
+    def rows_of(ref, at, count=1):
+        return wide(ref[at * rows : (at + count) * rows, :])
+
+    for i in range(4):
+        part = slice(i * WIDTH, (i + 1) * WIDTH)
+        d_expand[:, part] = rows_of(first_ref, i)
+        e_expand[:, part] = rows_of(last_ref, 2 + i)
+    d_shrink[...] = rows_of(first_ref, 4, 4)
+    for i in range(3):
+        c_in[i] = rows_of(first_ref, 8 + i)
+        e_in[i] = rows_of(last_ref, 10 + i)
+    c_out[...] = rows_of(first_ref, 11)
+    s_in[0] = rows_of(first_ref, 12)
+    s_in[1] = rows_of(first_ref, 13)
+    s_in[2] = rows_of(last_ref, 0)
+    s_out[...] = rows_of(last_ref, 1)
+    e_shrink[...] = rows_of(last_ref, 6, 4)
+    e_out[...] = rows_of(last_ref, 13)
+    me = lax.axis_index("dp")
+    mine = pltpu.roll(vec_ref[...], WIDTH - me * rows, 1)
+    e_bias[...] = mine[0:3, 0:rows]
+    e_norm[0] = mine[3:5, 0:rows]
+    e_norm[1] = mine[5:7, 0:rows]
+    e_shrink_bias[...] = mine[11:12, 0:rows]
+    d_bias[...] = mine[12:18, 0:rows]
+    for i in range(3):
+        d_norm[i] = mine[18 + 2 * i : 20 + 2 * i, 0:rows]
+    d_shrink_bias[...] = mine[28:29, 0:rows]
+    for at, to in ((7, e_expand_bias), (24, d_expand_bias)):
+        row = jnp.zeros((1, WIDTH), wide_type)
+        for i in range(4):
+            row = jnp.where(me // 2 == i, vec_ref[at + i : at + i + 1, :], row)
+        to[...] = jnp.where(me % 2 == 0, row[:, : WIDTH // 2], row[:, WIDTH // 2 :])
+
+
+def unpack(first, last, vector):
+    rows, width = WIDTH // 8, WIDTH
+    square, cube = (rows, width), (3, rows, width)
+    wide_one, tall_one = (rows, 4 * width), (4 * rows, width)
+    shapes = [
+        cube, square, (3, rows), (2, 2, rows), wide_one, (1, 4 * rows), tall_one, (1, rows),
+        cube, square, cube, square, (6, rows), (3, 2, rows), wide_one, (1, 4 * rows), tall_one,
+        (1, rows),
+    ]
     here = pl.BlockSpec(memory_space=VMEM)
-    dma = pltpu.SemaphoreType.DMA
     return pl.pallas_call(
-        functools.partial(sum_kernel, sources),
-        in_specs=[anywhere] * (2 * count) + [here],
-        out_specs=[anywhere, here],
-        out_shape=[
-            like((COUNT, ROWS, width), low_type),
-            like((VEC_ROWS, width), wide_type),
-        ],
-        scratch_shapes=[
-            VMEM((COUNT, 4, ROWS, width), low_type),
-            VMEM((COUNT, 4, ROWS, width), low_type),
-            VMEM((COUNT, 2, 2, HALF, width), low_type),
-            VMEM((COUNT, 2, HALF, width), low_type),
-            VMEM((COUNT, HALF, width), low_type),
-            VMEM((COUNT, QUARTER, width), low_type),
-            VMEM((COUNT, ROWS, width), low_type),
-            VMEM((5, VEC_ROWS, width), wide_type),
-            dma((count,)),
-            dma((count,)),
-            dma((count,)),
-            dma((7, COUNT, 3)),
-            dma((7, COUNT, 3)),
-            dma((5,)),
-            dma((5,)),
-            dma((COUNT,)),
-        ],
-        compiler_params=params(60, collective_id=1, has_side_effects=True),
-        cost_estimate=cost(1e8, 1e8),
-        name="sum_pairs",
-    )(*[p[0] for p in pairs], *[p[1] for p in pairs], vector)
+        unpack_kernel,
+        in_specs=[here] * 3,
+        out_specs=[here] * len(shapes),
+        out_shape=[like(shape, wide_type) for shape in shapes],
+        compiler_params=params(40),
+        cost_estimate=cost(1e7, 1.3e7),
+        name="unpack",
+    )(first, last, vector)
 
 
 def sum_whole(grads):
@@ -1246,20 +1632,16 @@
     return outs
 
 
-def sum_all(grads, vectors):
-    flat = jnp.concatenate([v.reshape(-1) for v in vectors])
-    if paired():
-        sources = ((0, 0), (1, 0), (2, 0), (2, 288), (3, 0), (4, 0), (5, 0), (6, 0), (6, 288))
-        rows = [grad[0].shape[1] for grad in grads]
-        padded = jnp.pad(flat, (0, VEC_ROWS * WIDTH - flat.size)).reshape(VEC_ROWS, WIDTH)
-        total, flat = sum_pairs(grads, sources, padded)
-        flat = flat.reshape(-1)
-        shards = [
-            wide(total[chunk, row : row + size]) for (chunk, row), size in zip(sources, rows)
-        ]
-    else:
-        shards = sum_whole([grad[0] for grad in grads])
-        flat = lax.psum(flat, ("dp", "section"))
+def beside(shard):
+    rows = shard.shape[0] // 4
+    return shard.reshape(4, rows, WIDTH).transpose(1, 0, 2).reshape(rows, 4 * WIDTH)
+
+
+def sum_any(grads, d_feed, vectors):
+    e_in, e_out, e_expand, e_shrink, s_all, c_in, c_out = sum_whole([grad[0] for grad in grads])
+    d_feed = wide(lax.psum(d_feed, "section"))
+    d_expand, d_shrink = d_feed[: d_feed.shape[0] // 2], d_feed[d_feed.shape[0] // 2 :]
+    flat = lax.psum(jnp.concatenate([v.reshape(-1) for v in vectors]), ("dp", "section"))
     parts, mine = lax.axis_size("dp"), lax.axis_index("dp")
     outs, at = [], 0
     for v in vectors:
@@ -1267,12 +1649,27 @@
         at += v.size
         size = v.shape[-1] // parts
         outs.append(lax.dynamic_slice_in_dim(whole, mine * size, size, v.ndim - 1))
-    return shards, outs
-
-
-def beside(shard):
-    rows = shard.shape[0] // 4
-    return shard.reshape(4, rows, WIDTH).transpose(1, 0, 2).reshape(rows, 4 * WIDTH)
+    rows = WIDTH // parts
+    return (
+        e_in.reshape(3, rows, WIDTH),
+        e_out,
+        outs[0],
+        outs[1],
+        beside(e_expand),
+        outs[2],
+        e_shrink,
+        outs[3],
+        s_all[: 3 * rows].reshape(3, rows, WIDTH),
+        s_all[3 * rows :],
+        c_in.reshape(3, rows, WIDTH),
+        c_out,
+        outs[4],
+        outs[5],
+        beside(d_expand),
+        outs[6],
+        d_shrink,
+        outs[7],
+    )
 
 
 def on_device(
@@ -1318,7 +1715,7 @@
     lengths = integers[-1, : decoder_lengths.shape[2]]
     owners = pool_table.shape[2]
 
-    qkv, context, stats, mixed = encoder_attend(
+    qkv, context, context_low, stats, mixed = encoder_attend(
         x, encoder_inward, encoder_outward, encoder_biases
     )
     hidden, slope, summed, states = encoder_feed(
@@ -1340,7 +1737,7 @@
     kv, cross_context, cross_stats = cross_forward(
         pooled, cross_q, mask_across, cross_inward, decoder_biases
     )
-    (out, joined_back, dc, mid_vec, mid_expand), (d_expand, d_shrink, d_cross_out) = middle(
+    (out, joined_back, dc, mid_vec, mid_expand), d_feed, d_cross_out = middle(
         self_mixed,
         cross_context,
         cross_outward,
@@ -1352,6 +1749,7 @@
         decoder_shrink_bias,
         grad,
     )
+    d_feed = lax.psum_scatter(d_feed, "dp", scatter_dimension=0, tiled=True)[0]
     dkv, dq, cross_vec, dpool = cross_back(
         kv, cross_q, cross_context, dc, cross_stats, mask_down, cross_inward
     )
@@ -1376,59 +1774,52 @@
     decoder_grad = shifted(dy, "section", half_way)
     states_back = spread_rows(table, returned.reshape(-1, WIDTH), x.shape[0])
 
-    (dmix, feed_vec, feed_expand), (e_expand, e_shrink, e_out) = encoder_feed_back(
+    hosts = paired()
+    plan = feed_plan() if hosts else None
+    guests = [pair[k] for k in range(2) for pair in (d_cross_in, d_cross_out, d_self)] if hosts else []
+    (dmix, feed_vec, feed_expand), (e_expand, e_shrink, e_out), from_feed = encoder_feed_back(
         states_back,
         summed,
         mixed,
         hidden,
         slope,
-        context,
+        context_low,
         encoder_norms,
         encoder_expand,
         encoder_shrink,
-    )
-    (dx, attend_vec), e_in = encoder_attend_back(
-        dmix, x, qkv, context, stats, encoder_inward, encoder_outward
-    )
-
-    shards, vectors = sum_all(
-        [d_expand, d_shrink, d_cross_in, d_cross_out, d_self, e_expand, e_shrink, e_in, e_out],
-        [
-            jnp.concatenate([attend_vec[0:2], feed_vec[5:6]], 0),
-            jnp.stack([feed_vec[3:5], feed_vec[0:2]]),
-            feed_expand[0],
-            feed_vec[2],
-            jnp.concatenate([self_vec[3:5], self_vec[2:3], cross_vec[0:2], mid_vec[5:6]], 0),
-            jnp.stack([self_vec[0:2], mid_vec[3:5], mid_vec[0:2]]),
-            mid_expand[0],
-            mid_vec[2],
-        ],
-    )
-    d_expand, d_shrink, d_cross_in, d_cross_out, d_self, e_expand, e_shrink, e_in, e_out = shards
-    rows = WIDTH // lax.axis_size("dp")
-    return (
-        decoder_out[None],
-        dx[None],
-        decoder_grad[None],
-        e_in.reshape(3, rows, WIDTH),
-        e_out,
-        vectors[0],
-        vectors[1],
-        beside(e_expand),
-        vectors[2],
-        e_shrink,
-        vectors[3],
-        d_self[: 3 * rows].reshape(3, rows, WIDTH),
-        d_self[3 * rows :],
-        d_cross_in.reshape(3, rows, WIDTH),
-        d_cross_out,
-        vectors[4],
-        vectors[5],
-        beside(d_expand),
-        vectors[6],
-        d_shrink,
-        vectors[7],
-    )
+        plan,
+        guests,
+    )
+    plan = attend_plan() if hosts else None
+    if hosts:
+        guests = [pair[k] for k in range(2) for pair in (d_self, e_expand, e_shrink)]
+        early = jnp.concatenate([d_feed, from_feed[0]], 0)
+        early, dmix = lax.optimization_barrier((early, dmix))
+        early = lax.psum(early, "section")
+    (dx, attend_vec), e_in, from_attend = encoder_attend_back(
+        dmix, x, qkv, context, stats, encoder_inward, encoder_outward, plan, guests
+    )
+    vectors = [
+        jnp.concatenate([attend_vec[0:2], feed_vec[5:6]], 0),
+        jnp.stack([feed_vec[3:5], feed_vec[0:2]]),
+        feed_expand[0],
+        feed_vec[2],
+        jnp.concatenate([self_vec[3:5], self_vec[2:3], cross_vec[0:2], mid_vec[5:6]], 0),
+        jnp.stack([self_vec[0:2], mid_vec[3:5], mid_vec[0:2]]),
+        mid_expand[0],
+        mid_vec[2],
+    ]
+    if hosts:
+        flat = jnp.concatenate([v.reshape(-1) for v in vectors])
+        flat = jnp.pad(flat, (0, VEC_ROWS * WIDTH - flat.size)).reshape(VEC_ROWS, WIDTH)
+        last, vector = last_sums(last_plan(), (e_in, e_out), from_attend, flat)
+        results = unpack(early, last, vector)
+        results = [r[0] if n in (5, 7, 15, 17) else r for n, r in enumerate(results)]
+    else:
+        results = sum_any(
+            [e_in, e_out, e_expand, e_shrink, d_self, d_cross_in, d_cross_out], d_feed, vectors
+        )
+    return (decoder_out[None], dx[None], decoder_grad[None], *results)
 
 
 def solution(mesh):

time: 566 us -> 503 us (0.89)
  Pallas kernels: 461 us -> 377 us
  waiting for transfers between devices: 32.1 us -> 47.2 us
  between operations: 1.47 us -> 14.8 us
    pallas_call x3 -> x4, Pallas kernels: 297 us -> 212 us  [the longest x1 87.6 us: last_sums(): pl.pallas_call(functools.partial(last_sums_kernel, plan), in_specs=plan.i...]
    all_to_all x1, waiting for transfers between devices: 0.01 us -> 16.7 us  [on_device(): lax.all_to_all(dpool.reshape(owners, -1, WIDTH), 'dp', split_axis=0, conc...]
    convert_element_type x4 -> x0, other arithmetic: 7.28 us -> none  [wide(): return value.astype(wide_type)]
    unnamed x75 -> x84, local copies, waits for them, and re-layouts: 19.6 us -> 25.6 us
  transfers between devices with their start and end apart: 6 -> 8, of which waited for: 2 -> 3; matrix products, arithmetic and copies ran while one was open for 1% -> 2% of each run, Pallas kernels for 21% -> 67%
where the time goes in v3:
time: 503 us; the launch traced here: 495 us
  Pallas kernels  377 us (75%)
  waiting for transfers between devices  47.2 us (9%)
  local copies, waits for them, and re-layouts  33.5 us (7%)
  starting transfers between devices  15.9 us (3%)
  between operations  14.8 us (3%)
  other arithmetic  6.39 us (1%)
    pallas_call x1, Pallas kernels, last_sums(): pl.pallas_call(functools.partial(last_sums_kernel, plan), in_specs=plan.i...  87.6 us
    pallas_call x1, Pallas kernels, encoder_attend_back(): pl.pallas_call(functools.partial(encoder_attend_back_kernel, plan), grid=...  70.4 us
    pallas_call x1, Pallas kernels, encoder_feed_back(): pl.pallas_call(functools.partial(encoder_feed_back_kernel, plan), grid=(4...  50.9 us
    pallas_call x1, Pallas kernels, encoder_attend(): pl.pallas_call(encoder_attend_kernel, grid=(groups,), in_specs=[full(toke...  34.3 us
    pallas_call x1, Pallas kernels, encoder_feed(): pl.pallas_call(encoder_feed_kernel, grid=(4,), in_specs=[full(tokens, wid...  29 us
    unnamed x84, local copies, waits for them, and re-layouts  25.6 us
    pallas_call x1, Pallas kernels, cross_back(): pl.pallas_call(cross_back_kernel, grid=(groups,), in_specs=[pl.BlockSpec(...  25.2 us
    all_to_all x1, waiting for transfers between devices, on_device(): lax.all_to_all(picked, 'dp', split_axis=0, concat_axis=0, tiled=True)  23.1 us
  transfers between devices with their start and end apart: 8, of which 3 were waited for; matrix products, arithmetic and copies ran while one was open for 2% of the time, Pallas kernels for 67%

profile of v3, /device:TPU:0, one launch (start us, length us, event | category | flops | bytes accessed | tf_op | source)
XLA Modules:
  0.0 495.1 jit_solution(792893932316556614)
XLA Ops:
  8.2 4.1 collective-permute-start.1
  15.5 34.3 %encoder_attend.1 = (bf16[3,1024,768]{2,1,0:T(8,128)(2,1)}, f32[1024,768]{1,0:T(8,128)}, bf16[1024,768]{1,0:T(8,128)(2,1)}, f32[3,8,1024]{2,1,0:T(8,128)}, f32[1024,768]{1,0:T(8,128)}) custom-call(bf16[1024,768]{1,0:T(8,128)(2,1)} %bitcast.56, bf16[3,768,768]{2,1,0:T(8,128)(2,1)} %refs_5_.1, bf16[768,768]{1,0:T(8,128)(2,1)} %refs_6_.3, f32[3,768]{1,0:T(4,128)} %b_ref.4, ...), custom_call_target="tpu_custom_call" | custom-call | flops 30000001024 | bytes 20000000 | tf_op jit(solution)/shard_map/encoder_attend/pallas_call | solution.py:200
  49.8 29.0 %encoder_feed.1 = (bf16[1024,3072]{1,0:T(8,128)(2,1)}, bf16[1024,3072]{1,0:T(8,128)(2,1)}, f32[1024,768]{1,0:T(8,128)}, bf16[1024,768]{1,0:T(8,128)(2,1)}) custom-call(f32[1024,768]{1,0:T(8,128)} %get-tuple-element.95.mixed_ref.refs_2_, f32[2,2,768]{2,1,0:T(2,128)} %refs_6_.2, bf16[768,3072]{1,0:T(8,128)(2,1)} %refs_7_.1, f32[1,3072]{1,0:T(1,128)} %bitcast.58, ...), custom_call_target="tpu_custom_call" | custom-call | flops 20000000000 | bytes 30000000 | tf_op jit(solution)/shard_map/encoder_feed/pallas_call | solution.py:270
  81.3 6.4 %pick_rows.1 = bf16[2048,768]{1,0:T(8,128)(2,1)} custom-call(s32[2048,1]{1,0:T(8,128)S(1)} %bitcast.43, bf16[1024,768]{1,0:T(8,128)(2,1)S(1)} %copy-done.10), custom_call_target="tpu_custom_call" | custom-call | flops 4000000000 | bytes 5000000 | tf_op jit(solution)/shard_map/pick_rows/pallas_call | solution.py:619
  87.7 4.5 all-to-all-start
  93.5 6.5 %slot_mask.1 = (f32[128,2048]{1,0:T(8,128)S(1)}, f32[2048,128]{1,0:T(8,128)S(1)}) custom-call(s32[1024,128]{1,0:T(8,128)S(1)} %bitcast.44), custom_call_target="tpu_custom_call" | custom-call | flops 10000000000 | bytes 1000000 | tf_op jit(solution)/shard_map/slot_mask/pallas_call | solution.py:600
  101.0 3.1 self_forward.1
  107.0 23.1 %all-to-all-done = bf16[8,256,768]{2,1,0:T(8,128)(2,1)} async-done(((bf16[8,256,768]{2,1,0:T(8,128)(2,1)}), bf16[8,256,768]{2,1,0:T(8,128)(2,1)}, u32[]{:S(2)}, u32[]{:S(2)}) %all-to-all-start) | async-done | bytes 3145760 | tf_op jit(solution)/shard_map/all_to_all | solution.py:1730
  130.1 17.4 %cross_forward.1 = (bf16[2,2048,768]{2,1,0:T(8,128)(2,1)}, f32[128,768]{1,0:T(8,128)}, f32[3,8,512]{2,1,0:T(8,128)}) custom-call(bf16[2048,768]{1,0:T(8,128)(2,1)} %bitcast.8.pooled_ref, bf16[128,768]{1,0:T(8,128)(2,1)} %copy-done.27, f32[128,2048]{1,0:T(8,128)} %copy-done.15, bf16[3,768,768]{2,1,0:T(8,128)(2,1)} %cw_ref.3, f32[6,768]{1,0:T(8,128)} %b_ref.5), custom_call_target="tpu_custom_call" | custom-call | flops 20000000000 | bytes 12000000 | tf_op jit(solution)/shard_map/cross_forward/pallas_call | solution.py:782
  147.4 17.6 %middle.1 = (bf16[128,768]{1,0:T(8,128)(2,1)}, f32[128,768]{1,0:T(8,128)}, bf16[128,768]{1,0:T(8,128)(2,1)}, f32[8,768]{1,0:T(8,128)}, f32[1,3072]{1,0:T(1,128)}...) custom-call(f32[128,768]{1,0:T(8,128)} %copy-done.17, ...), custom_call_target="tpu_custom_call" | custom-call | flops 20000000000 | bytes 22000000 | tf_op jit(solution)/shard_map/middle/pallas_call | solution.py:879
  165.0 3.0 collective-permute-start.2
  168.0 25.2 %cross_back.1 = (bf16[2,2048,768]{2,1,0:T(8,128)(2,1)}, bf16[128,768]{1,0:T(8,128)(2,1)}, f32[8,768]{1,0:T(8,128)}, bf16[2048,768]{1,0:T(8,128)(2,1)}) custom-call(bf16[2,2048,768]{2,1,0:T(8,128)(2,1)} %get-tuple-element.102.kv_ref, bf16[128,768]{1,0:T(8,128)(2,1)} %copy-done.27, f32[128,768]{1,0:T(8,128)} %get-tuple-element.99.c_ref, ...), custom_call_target="tpu_custom_call" | custom-call | flops 30000001024 | bytes 22000000 | tf_op jit(solution)/shard_map/cross_back/pallas_call | solution.py:964
  193.3 3.7 all-to-all-start.1
  203.5 9.4 %self_back.1 = (f32[128,768]{1,0:T(8,128)}, f32[8,768]{1,0:T(8,128)S(1)}, bf16[4,384,768]{2,1,0:T(8,128)(2,1)S(1)}, bf16[4,384,768]{2,1,0:T(8,128)(2,1)}) custom-call(s32[4]{0:T(128)S(1)} %slice_bitcast_fusion.6.lengths_ref, bf16[128,768]{1,0:T(8,128)(2,1)S(1)} %get-tuple-element.168.y_ref, f32[128,768]{1,0:T(8,128)S(1)} %copy-done.18, ...), custom_call_target="tpu_custom_call" | custom-call | flops 20000000000 | bytes 15000000 | tf_op jit(solution)/shard_map/self_back/pallas_call | solution.py:1082
  215.1 11.0 %cross_grads.1 = (bf16[4,288,768]{2,1,0:T(8,128)(2,1)S(1)}, bf16[4,288,768]{2,1,0:T(8,128)(2,1)S(1)}) custom-call(bf16[2048,768]{1,0:T(8,128)(2,1)} %bitcast.8.pooled_ref, bf16[2,2048,768]{2,1,0:T(8,128)(2,1)} %get-tuple-element.111.dkv_ref, f32[128,768]{1,0:T(8,128)S(1)} %copy-done.19, bf16[128,768]{1,0:T(8,128)(2,1)S(1)} %copy-done.21, ...), custom_call_target="tpu_custom_call" | custom-call | flops 10000000000 | bytes 15000000 | tf_op jit(solution)/shard_map/cross_grads/pallas_call | solution.py:1018
  228.6 7.4 %collective-permute-done.3 = f32[128,768]{1,0:T(8,128)} collective-permute-done((f32[128,768]{1,0:T(8,128)}, f32[128,768]{1,0:T(8,128)}, u32[]{:S(2)}, u32[]{:S(2)}) %collective-permute-start.3) | collective-permute-done | bytes 393248 | tf_op jit(solution)/shard_map/ppermute | solution.py:1114
  236.0 16.7 %all-to-all-done.1 = bf16[8,256,768]{2,1,0:T(8,128)(2,1)S(1)} async-done(((bf16[8,256,768]{2,1,0:T(8,128)(2,1)}), bf16[8,256,768]{2,1,0:T(8,128)(2,1)S(1)}, u32[]{:S(2)}, u32[]{:S(2)}) %all-to-all-start.1) | async-done | bytes 3145760 | tf_op jit(solution)/shard_map/all_to_all | solution.py:1756
  252.7 5.3 %spread_rows.1.refs_0_ = bf16[1024,768]{1,0:T(8,128)(2,1)S(1)} custom-call(s32[1,2048]{1,0:T(1,128)S(1)} %bitcast.46, bf16[2048,768]{1,0:T(8,128)(2,1)S(1)} %bitcast.42), custom_call_target="tpu_custom_call" | custom-call | flops 4000000000 | bytes 5000000 | tf_op jit(solution)/shard_map/spread_rows/pallas_call | solution.py:652
  259.2 50.9 %encoder_feed_back.1 = (f32[1024,768]{1,0:T(8,128)}, f32[8,768]{1,0:T(8,128)}, f32[1,3072]{1,0:T(1,128)}, bf16[4,384,768]{2,1,0:T(8,128)(2,1)}, bf16[4,384,768]{...) custom-call(bf16[1024,768]{1,0:T(8,128)(2,1)} %copy-done.11, ...), custom_call_target="tpu_custom_call" | custom-call | flops 40000000000 | bytes 50000000 | tf_op jit(solution)/shard_map/encoder_feed_back/pallas_call | solution.py:397
  311.8 3.0 pad_maximum_fusion
  314.8 70.4 %encoder_attend_back.1 = (f32[1024,768]{1,0:T(8,128)}, f32[8,768]{1,0:T(8,128)}, bf16[4,288,768]{2,1,0:T(8,128)(2,1)}, bf16[4,288,768]{2,1,0:T(8,128)(2,1)}, bf16[960,768]{1,0:T(8,128)(2,1)}) custom-call(f32[1024,768]{1,0:T(8,128)} %get-tuple-element.124.refs_0_, bf16[1024,768]{1,0:T(8,128)(2,1)} %bitcast.57, ...), custom_call_target="tpu_custom_call" | custom-call | flops 49999998976 | bytes 40000000 | tf_op jit(solution)/shard_map/encoder_attend_back/pallas_call | solution.py:526
  386.8 87.6 %last_sums.1 = (bf16[1344,768]{1,0:T(8,128)(2,1)}, f32[32,768]{1,0:T(8,128)}) custom-call(bf16[4,288,768]{2,1,0:T(8,128)(2,1)} %get-tuple-element.135.refs_0_, bf16[4,96,768]{2,1,0:T(8,128)(2,1)} %get-tuple-element.136.refs_1_, bf16[4,288,768]{2,1,0:T(8,128)(2,1)} %get-tuple-element.137.refs_2_, bf16[4,96,768]{2,1,0:T(8,128)(2,1)} %get-tuple-element.138.refs_3_, ...), custom_call_target="tpu_custom_call" | custom-call | flops 100000000 | bytes 100000000 | tf_op jit(solution)/shard_map/last_sums/pallas_call | solution.py:1467
  478.5 3.3 unpack.1
  486.3 1.8 copy.74
  (124 shorter events, 35.9 us)
Async XLA Ops:
  8.2 71.2 %collective-permute-start.1 = (bf16[256,768]{1,0:T(8,128)(2,1)S(1)}, bf16[256,768]{1,0:T(8,128)(2,1)S(1)}, u32[]{:S(2)}, u32[]{:S(2)}) collective-permute-start(bf16[256,768]{1,0:T(8,128)(2,1)S(1)} %pad_maximum_fusion.1), channel_id=1, source_target_pairs={{0,2},{1,3},{2,0},{3,1},{4,6},{5,7},{6,4},{7,5},{8,10},{9,11},{10,... | collective-permute-start | bytes 1179656 | tf_op jit(solution)/shard_map/ppermute | solution.py:1114
  14.2 66.0 %collective-permute-start = (s32[131,1024]{1,0:T(8,128)S(1)}, s32[131,1024]{1,0:T(8,128)S(1)}, u32[]{:S(2)}, u32[]{:S(2)}) collective-permute-start(s32[131,1024]{1,0:T(8,128)S(1)} %pad_add_fusion), channel_id=1, source_target_pairs={{0,2},{1,3},{2,0},{3,1},{4,6},{5,7},{6,4},{7,5},{8,10},{9,11},{10,... | collective-permute-start | bytes 1609736 | tf_op jit(solution)/shard_map/ppermute | solution.py:1114
  49.8 29.0 %copy-start.34 = (f32[768]{0:T(1024)S(1)}, f32[768]{0:T(1024)}, u32[]{:S(2)}) copy-start(f32[768]{0:T(1024)} %param.47) | copy-start | bytes 9220
  78.9 2.5 copy-start.10
  87.7 42.4 %all-to-all-start = ((bf16[8,256,768]{2,1,0:T(8,128)(2,1)}), bf16[8,256,768]{2,1,0:T(8,128)(2,1)}, u32[]{:S(2)}, u32[]{:S(2)}) async-start(bf16[8,256,768]{2,1,0:T(8,128)(2,1)} %bitcast.7), calls=%async_computation | async-start | bytes 6291456 | tf_op jit(solution)/shard_map/all_to_all | solution.py:1730
  92.2 219.6 %reduce-scatter.2.cloned.1.call-start = ((), (), s32[]{:S(2)}) async-start(), calls=%async_computation.3 | async-start | bytes 10616832 | tf_op jit(solution)/shard_map/reduce_scatter | solution.py:1752
  93.4 7.5 %copy-start.3 = (bf16[3,768,768]{2,1,0:T(8,128)(2,1)S(1)}, bf16[3,768,768]{2,1,0:T(8,128)(2,1)}, u32[]{:S(2)}) copy-start(bf16[3,768,768]{2,1,0:T(8,128)(2,1)} %w_ref.9) | copy-start | bytes 10616836
  93.4 7.5 %copy-start.4 = (bf16[3,768,768]{2,1,0:T(8,128)(2,1)S(1)}, bf16[3,768,768]{2,1,0:T(8,128)(2,1)}, u32[]{:S(2)}) copy-start(bf16[3,768,768]{2,1,0:T(8,128)(2,1)} %cw_ref.3) | copy-start | bytes 10616836
  93.4 7.5 %copy-start.5 = (bf16[768,768]{1,0:T(8,128)(2,1)S(1)}, bf16[768,768]{1,0:T(8,128)(2,1)}, u32[]{:S(2)}) copy-start(bf16[768,768]{1,0:T(8,128)(2,1)} %wo_ref.5) | copy-start | bytes 3538948
  93.4 7.5 %copy-start.7 = (f32[6,768]{1,0:T(8,128)S(1)}, f32[6,768]{1,0:T(8,128)}, u32[]{:S(2)}) copy-start(f32[6,768]{1,0:T(8,128)} %b_ref.5) | copy-start | bytes 55300
  93.5 7.5 %copy-start.8 = (f32[3,2,768]{2,1,0:T(2,128)S(1)}, f32[3,2,768]{2,1,0:T(2,128)}, u32[]{:S(2)}) copy-start(f32[3,2,768]{2,1,0:T(2,128)} %n_ref.9) | copy-start | bytes 55300
  100.9 3.1 copy-start.14
  165.0 63.6 %collective-permute-start.2 = (bf16[128,768]{1,0:T(8,128)(2,1)}, bf16[128,768]{1,0:T(8,128)(2,1)}, u32[]{:S(2)}, u32[]{:S(2)}) collective-permute-start(bf16[128,768]{1,0:T(8,128)(2,1)} %get-tuple-element.100), channel_id=1, source_target_pairs={{0,2},{1,3},{2,0},{3,1},{4,6},{5,7},{6,4},{7,5},{8,10},{9,11},{10,... | collective-permute-start | bytes 589832 | tf_op jit(solution)/shard_map/ppermute | solution.py:1114
  193.2 3.7 copy-start.9
  193.3 59.5 %all-to-all-start.1 = ((bf16[8,256,768]{2,1,0:T(8,128)(2,1)}), bf16[8,256,768]{2,1,0:T(8,128)(2,1)S(1)}, u32[]{:S(2)}, u32[]{:S(2)}) async-start(bf16[8,256,768]{2,1,0:T(8,128)(2,1)} %bitcast.48), calls=%async_computation.2 | async-start | bytes 6291456 | tf_op jit(solution)/shard_map/all_to_all | solution.py:1756
  196.9 277.5 %all-reduce.4.cloned.1.call-start = ((), (), s32[]{:S(2)}) async-start(), calls=%async_computation.4 | async-start | bytes 4128768 | tf_op jit(solution)/shard_map/psum | solution.py:1798
  203.4 11.6 %copy-start.31 = (f32[8,768]{1,0:T(8,128)S(1)}, f32[8,768]{1,0:T(8,128)}, u32[]{:S(2)}) copy-start(f32[8,768]{1,0:T(8,128)} %get-tuple-element.145) | copy-start | bytes 73732
  203.5 11.6 %copy-start.19 = (f32[128,768]{1,0:T(8,128)S(1)}, f32[128,768]{1,0:T(8,128)}, u32[]{:S(2)}) copy-start(f32[128,768]{1,0:T(8,128)} %copy-done.17) | copy-start | bytes 1179652
  203.5 11.6 %copy-start.21 = (bf16[128,768]{1,0:T(8,128)(2,1)S(1)}, bf16[128,768]{1,0:T(8,128)(2,1)}, u32[]{:S(2)}) copy-start(bf16[128,768]{1,0:T(8,128)(2,1)} %get-tuple-element.112.dq_ref.cdq_ref) | copy-start | bytes 589828
  215.0 21.0 %collective-permute-start.3 = (f32[128,768]{1,0:T(8,128)}, f32[128,768]{1,0:T(8,128)}, u32[]{:S(2)}, u32[]{:S(2)}) collective-permute-start(f32[128,768]{1,0:T(8,128)} %get-tuple-element.133), channel_id=1, source_target_pairs={{0,2},{1,3},{2,0},{3,1},{4,6},{5,7},{6,4},{7,5},{8,10},{9,11},{10,... | collective-permute-start | bytes 1179656 | tf_op jit(solution)/shard_map/ppermute | solution.py:1114
  314.8 71.2 %copy-start.30 = (f32[22272]{0:T(1024)S(1)}, f32[22272]{0:T(1024)}, u32[]{:S(2)}) copy-start(f32[22272]{0:T(1024)} %custom-call) | copy-start | bytes 267268
  314.8 71.2 %copy-start.33 = (f32[1,3072]{1,0:T(1,128)S(1)}, f32[1,3072]{1,0:T(1,128)}, u32[]{:S(2)}) copy-start(f32[1,3072]{1,0:T(1,128)} %get-tuple-element.142) | copy-start | bytes 36868
  314.8 71.3 %copy-start.32 = (f32[1,3072]{1,0:T(1,128)S(1)}, f32[1,3072]{1,0:T(1,128)}, u32[]{:S(2)}) copy-start(f32[1,3072]{1,0:T(1,128)} %get-tuple-element.146) | copy-start | bytes 36868
  386.8 97.8 %copy-start.28 = (f32[1024,768]{1,0:T(8,128)S(1)}, f32[1024,768]{1,0:T(8,128)}, u32[]{:S(2)}) copy-start(f32[1024,768]{1,0:T(8,128)} %get-tuple-element.132) | copy-start | bytes 9437188
  (19 other events, 20.2 us)
Sparse Core Ops, SparseCore 0:
  165.2 109.8 reduce-scatter.1
  314.9 89.3 all-reduce.3

commit v4 on v3

--- a/solution.py
+++ b/solution.py
@@ -160,7 +160,7 @@
 ):
     group = pl.program_id(0)
     tokens = x_ref.shape[0]
-    block = 256
+    block = 512
     x = x_ref[...]
     qkv_ref[0] = low(dot(x, w_ref[0]) + bg_ref[0:1])
     qkv_ref[1] = low(dot(x, w_ref[1]))
@@ -238,13 +238,13 @@
     @pl.when(step == 0)
     def _():
         def rows_step(i, carry):
-            rows = pl.ds(pl.multiple_of(i * 128, 128), 128)
+            rows = pl.ds(pl.multiple_of(i * 256, 256), 256)
             first = norm_rows(mixed_ref[rows, :], n_ref[0, 0:1], n_ref[0, 1:2])
             a_low[rows, :] = low(first)
             sum_ref[rows, :] = first + sb_ref[...]
             return carry
 
-        lax.fori_loop(0, tokens // 128, rows_step, 0)
+        lax.fori_loop(0, tokens // 256, rows_step, 0)
 
     for i in range(tokens // block):
         rows = slice(i * block, (i + 1) * block)
@@ -256,11 +256,11 @@
     @pl.when(step == pl.num_programs(0) - 1)
     def _():
         def rows_step(i, carry):
-            rows = pl.ds(pl.multiple_of(i * 128, 128), 128)
+            rows = pl.ds(pl.multiple_of(i * 256, 256), 256)
             out_ref[rows, :] = low(norm_rows(sum_ref[rows, :], n_ref[1, 0:1], n_ref[1, 1:2]))
             return carry
 
-        lax.fori_loop(0, tokens // 128, rows_step, 0)
+        lax.fori_loop(0, tokens // 256, rows_step, 0)
 
 
 def encoder_feed(mixed, norms, expand, expand_bias, shrink, shrink_bias):
@@ -335,7 +335,7 @@
         vec_ref[...] = jnp.zeros(vec_ref.shape, wide_type)
 
         def rows_step(i, carry):
-            rows = pl.ds(pl.multiple_of(i * 128, 128), 128)
+            rows = pl.ds(pl.multiple_of(i * 256, 256), 256)
             grad, gain, offset = norm_rows_back(
                 sum_ref[rows, :], n_ref[1, 0:1], wide(g_ref[rows, :])
             )
@@ -348,7 +348,7 @@
             a_turned[:, rows] = low(first).T
             return carry
 
-        lax.fori_loop(0, tokens // 128, rows_step, 0)
+        lax.fori_loop(0, tokens // 256, rows_step, 0)
 
     column = jnp.zeros(eb_ref.shape, wide_type)
     for i in range(tokens // block):
@@ -369,7 +369,7 @@
     def _():
 
         def rows_step(i, carry):
-            rows = pl.ds(pl.multiple_of(i * 128, 128), 128)
+            rows = pl.ds(pl.multiple_of(i * 256, 256), 256)
             grad, gain, offset = norm_rows_back(
                 mixed_ref[rows, :], n_ref[0, 0:1], dmix_ref[rows, :]
             )
@@ -380,7 +380,7 @@
             vec_ref[5:6] += jnp.sum(wide(low(grad)), 0, keepdims=True)
             return carry
 
-        lax.fori_loop(0, tokens // 128, rows_step, 0)
+        lax.fori_loop(0, tokens // 256, rows_step, 0)
         hold[...] = dot(c_ref[...], back_low[...], TN)
         emit(out_outs, 0, hold)
 
@@ -458,7 +458,7 @@
 
     place(0)
     tokens = x_ref.shape[0]
-    block = 256
+    block = 512
     heads = GROUP // HEAD
 
     @pl.when(group == 0)
@@ -500,7 +500,7 @@
             )
         dv[...] += dot(weights[...], dc_heads)
         dk[...] += dot(scores_back[...], q_heads)
-        if i == 1:
+        if i == 0:
             place(1)
     dq = low(dq_turned[...].T * scale_scores)
     dk_low, dv_low = low(dk[...]), low(dv[...])
@@ -552,8 +552,8 @@
             VMEM((tokens, width), low_type),
             VMEM((width, tokens), low_type),
             VMEM((tokens, GROUP), low_type),
-            VMEM((tokens, 4 * 256), low_type),
-            VMEM((tokens, 4 * 256), low_type),
+            VMEM((tokens, 4 * 512), low_type),
+            VMEM((tokens, 4 * 512), low_type),
             VMEM((tokens, GROUP), wide_type),
             VMEM((tokens, GROUP), wide_type),
             VMEM((GROUP, tokens), wide_type),
@@ -1104,8 +1104,6 @@
 
 CUT = 192
 HALF = CUT // 2
-QUARTER = CUT // 4
-VEC_ROWS = 32
 MESH = pl.DeviceIdType.MESH
 
 
@@ -1134,11 +1132,28 @@
     )
 
 
+def on_section(*sections):
+    section = lax.axis_index("section")
+    wanted = section == sections[0]
+    for other in sections[1:]:
+        wanted = wanted | (section == other)
+    return pl.when(wanted)
+
+
 def greet():
     barrier = pltpu.get_barrier_semaphore()
     for partner in partners():
         pl.semaphore_signal(barrier, 1, device_id=partner, device_id_type=MESH)
-    pl.semaphore_wait(barrier, 5)
+
+    @on_section(1, 2)
+    def _():
+        other = {"section": 3 - lax.axis_index("section")}
+        pl.semaphore_signal(barrier, 1, device_id=other, device_id_type=MESH)
+        pl.semaphore_wait(barrier, 6)
+
+    @on_section(0, 3)
+    def _():
+        pl.semaphore_wait(barrier, 5)
 
 
 def laid_out(pieces):
@@ -1153,15 +1168,20 @@
 
 
 class Plan:
-    def __init__(self, pieces, arrived, schedule, collective_id, onward=False, vector=False):
+    def __init__(
+        self, pieces, arrived, schedule, collective_id, onward=False, vector=0, moved=()
+    ):
         self.arrays = 1 + max(piece[0] for piece in pieces)
         self.schedule, self.collective_id = schedule, collective_id
         self.sources, self.fresh = laid_out(pieces)
         self.from_kernels = tuple(arrived)
         arrived = sum(self.from_kernels)
-        self.arrived, self.onward, self.vector = arrived, onward, vector
+        self.arrived, self.onward = arrived, onward
+        self.vector = vector
+        self.vector_order = (1, 2, 0, 3, 4)
+        self.moved = tuple(moved)
         self.late = arrived + (self.fresh if onward else 0)
-        self.ins = 2 * self.arrays + len(self.from_kernels) + (1 if vector else 0)
+        self.ins = 2 * self.arrays + len(self.from_kernels) + len(self.moved) + (1 if vector else 0)
 
     def in_specs(self):
         anywhere = pl.BlockSpec(memory_space=pl.ANY)
@@ -1174,8 +1194,10 @@
             out.append((pl.BlockSpec(memory_space=pl.ANY), like((self.fresh * CUT, WIDTH), low_type)))
         if self.late:
             out.append((pl.BlockSpec(memory_space=pl.ANY), like((self.late * CUT, WIDTH), low_type)))
+        for value in self.moved:
+            out.append((pl.BlockSpec(memory_space=pl.ANY), value))
         if self.vector:
-            out.append((pl.BlockSpec(memory_space=VMEM), like((VEC_ROWS, WIDTH), wide_type)))
+            out.append((pl.BlockSpec(memory_space=VMEM), like((self.vector, WIDTH), wide_type)))
         return out
 
     def scratch(self):
@@ -1189,21 +1211,23 @@
             VMEM((fresh, 2, 2, HALF, WIDTH), low_type),
             VMEM((fresh, 2, HALF, WIDTH), low_type),
             VMEM((arrived, CUT, WIDTH if self.late else 128), low_type),
+            VMEM((late, CUT, WIDTH if self.late else 128), low_type),
             VMEM((late, HALF, WIDTH if self.late else 128), low_type),
-            VMEM((late, QUARTER, WIDTH if self.late else 128), low_type),
             VMEM((late, CUT, WIDTH if self.late else 128), low_type),
-            VMEM((5, VEC_ROWS if self.vector else 8, WIDTH), wide_type),
+            VMEM((5, self.vector or 8, WIDTH), wide_type),
             dma((count,)),
             dma((count,)),
             dma((count,)),
             dma((3, fresh, 3)),
             dma((3, fresh, 3)),
-            dma((late, 4)),
-            dma((late, 4)),
+            dma((late, 5)),
+            dma((late, 5)),
             dma((arrived,)),
             dma((2, most)),
             dma((5,)),
             dma((5,)),
+            dma((max(len(self.moved), 1),)),
+            dma((max(len(self.moved), 1),)),
         ]
 
     def open(self, ins, outs, scratch):
@@ -1218,9 +1242,11 @@
         self.keeps, self.sends = ins[:count], ins[count : 2 * count]
         ins = ins[2 * count :]
         self.arrived = [ins.pop(0) for _ in plan.from_kernels]
+        self.moved = [ins.pop(0) for _ in plan.moved]
         self.vec_ref = ins.pop(0) if plan.vector else None
         self.shard_out = None if plan.onward else outs.pop(0)
         self.late_out = outs.pop(0) if plan.late else None
+        self.moved_out = [outs.pop(0) for _ in plan.moved]
         self.vec_out = outs.pop(0) if plan.vector else None
         (
             self.own,
@@ -1228,8 +1254,8 @@
             self.from_one,
             self.from_two,
             self.waiting,
-            self.from_three,
-            self.from_four,
+            self.from_outer,
+            self.from_inner,
             self.whole,
             self.vec_in,
             self.load_sems,
@@ -1243,14 +1269,17 @@
             self.out_sems,
             self.vec_send,
             self.vec_recv,
+            self.moved_send,
+            self.moved_recv,
         ) = scratch
-        self.core, self.over_x, self.over_y, self.near, self.far = partners()
+        self.core, self.over_x, self.over_y = partners()[:3]
         section = lax.axis_index("section")
-        side, far_side = section % 2, section // 2
-        self.half_at = pl.multiple_of(side * HALF, HALF)
-        self.half_other = pl.multiple_of((1 - side) * HALF, HALF)
-        self.quarter_at = pl.multiple_of(side * HALF + far_side * QUARTER, QUARTER)
-        self.quarter_other = pl.multiple_of(side * HALF + (1 - far_side) * QUARTER, QUARTER)
+        side = section // 2
+        self.mine = pl.multiple_of(side * HALF, HALF)
+        self.other = pl.multiple_of((1 - side) * HALF, HALF)
+        self.outer = {"section": 3 * side}
+        self.inner = {"section": 2 - side}
+        self.inward = {"section": 1 + side}
 
     def remote(self, source, to, send, recv, partner):
         return pltpu.make_async_remote_copy(
@@ -1320,34 +1349,61 @@
         for copy in self.copies(stage, c):
             copy.start()
 
-    def across(self, stage, k):
-        half = self.summed(k).at[pl.ds(self.half_other, HALF)]
-        quarter = self.summed(k).at[pl.ds(self.quarter_other, QUARTER)]
-        mine = self.whole.at[k, pl.ds(self.quarter_at, QUARTER)]
-        ours = self.whole.at[k, pl.ds(self.half_at, HALF)]
+    def line_copy(self, n, k):
+        mine, other = pl.ds(self.mine, HALF), pl.ds(self.other, HALF)
+        whole = self.whole.at[k]
         source, to, partner = (
-            (half, self.from_three.at[k], self.near),
-            (quarter, self.from_four.at[k], self.far),
-            (mine, mine, self.far),
-            (ours, ours, self.near),
-        )[stage - 3]
-        n = stage - 3
+            (self.summed(k), self.from_outer.at[k], self.inward),
+            (self.summed(k).at[other], self.from_inner.at[k], self.inner),
+            (whole.at[mine], whole.at[mine], self.inner),
+            (whole.at[mine], whole.at[mine], self.outer),
+            (whole.at[other], whole.at[other], self.outer),
+        )[n]
         return self.remote(source, to, self.line_send.at[k, n], self.line_recv.at[k, n], partner)
 
     def line(self, stage, k):
         if stage == "go":
-            self.across(3, k).start()
+
+            @on_section(0, 3)
+            def _():
+                self.line_copy(0, k).start()
+
             return
-        self.across(stage, k).wait_recv()
-        if stage == 3:
-            add_rows(self.summed(k).at[pl.ds(self.half_at, HALF)], self.from_three.at[k], HALF)
-        elif stage == 4:
-            rows = pl.ds(self.quarter_at, QUARTER)
-            self.whole[k, rows, :] = low(wide(self.summed(k)[rows, :]) + wide(self.from_four[k]))
-        if stage < 6:
-            self.across(stage + 1, k).start()
-        else:
+        if stage == 6:
+
+            @on_section(0, 3)
+            def _():
+                self.line_copy(3, k).wait_recv()
+                self.line_copy(4, k).wait_recv()
+
             self.late_copy(k).start()
+            return
+
+        @on_section(1, 2)
+        def _():
+            self.line_copy(stage - 3, k).wait_recv()
+            if stage == 3:
+                add_rows(self.summed(k), self.from_outer.at[k], CUT)
+                self.line_copy(1, k).start()
+            elif stage == 4:
+                rows = pl.ds(self.mine, HALF)
+                self.whole[k, rows, :] = low(
+                    wide(self.summed(k)[rows, :]) + wide(self.from_inner[k])
+                )
+                self.line_copy(2, k).start()
+                self.line_copy(3, k).start()
+            else:
+                self.line_copy(4, k).start()
+
+    def line_sent(self, k):
+        @on_section(0, 3)
+        def _():
+            self.line_copy(0, k).wait_send()
+
+        @on_section(1, 2)
+        def _():
+            for n in range(1, 5):
+                self.line_copy(n, k).wait_send()
 
     def shard_copy(self, c):
         return pltpu.make_async_copy(
@@ -1357,6 +1413,15 @@
     def late_copy(self, k):
         return pltpu.make_async_copy(
             self.whole.at[k], self.late_out.at[pl.ds(k * CUT, CUT)], self.out_sems.at[1, k]
+        )
+
+    def moved_copy(self, n):
+        return self.remote(
+            self.moved[n],
+            self.moved_out[n],
+            self.moved_send.at[n],
+            self.moved_recv.at[n],
+            partners()[4],
         )
 
     def vec_copy(self, stage):
@@ -1365,7 +1430,7 @@
             self.vec_in.at[stage],
             self.vec_send.at[stage],
             self.vec_recv.at[stage],
-            partners()[stage],
+            partners()[self.plan.vector_order[stage]],
         )
 
     def vec_step(self, stage):
@@ -1384,6 +1449,8 @@
             self.load(s).start()
         for k in range(self.plan.arrived):
             self.arrive(k).start()
+        for n in range(len(self.moved)):
+            self.moved_copy(n).start()
 
     def step(self, stage, c):
         if stage == "vec":
@@ -1422,6 +1489,8 @@
                 self.shard_copy(c).start()
 
     def finish(self):
+        for n in range(len(self.moved)):
+            self.moved_copy(n).wait()
         for s in range(len(self.plan.sources)):
             self.cross(s).wait_send()
         for c in range(self.plan.fresh):
@@ -1431,8 +1500,7 @@
             if not self.plan.onward:
                 self.shard_copy(c).wait()
         for k in range(self.plan.late):
-            for stage in (3, 4, 5, 6):
-                self.across(stage, k).wait_send()
+            self.line_sent(k)
             self.late_copy(k).wait()
 
     def slot(self, grid_step, steps, slots, slot):
@@ -1476,81 +1544,39 @@
     )(*[p[0] for p in pairs], *[p[1] for p in pairs], *arrived, vector)
 
 
-def landing_order(fresh, arrived, onward, vector=False, first=0.0):
-    free = {}
-    events, steps = [], []
-
-    def send(time, takes, *links):
-        begin = max([time] + [free.get(link, 0.0) for link in links])
-        for link in links:
-            free[link] = begin + takes
-        return begin + takes + 1.5
-
-    def push(time, stage, c):
-        events.append((time, len(steps) + len(events), stage, c))
-
-    for c in range(fresh):
-        push(first + 4.0 + 2.2 * c, 0, c)
-    for k in range(arrived):
-        push(first + 3.0 + 0.3 * k, "go", k)
-    if vector:
-        push(first, "vec", 0)
-    while events:
-        event = min(events)
-        events.remove(event)
-        time, _, stage, c = event
-        steps.append((time, stage, c))
-        if stage == "vec":
-            if c < 5:
-                push(time + 5.0, "vec", c + 1)
-        elif stage == 0:
-            if free.get("xy", 0.0) > time + 2.5:
-                steps.pop()
-                push(free["xy"] - 2.0, 0, c)
-            else:
-                push(send(time, 6.6, "xy"), 1, c)
-        elif stage == 1:
-            push(send(time, 3.3, "xy"), 2, c)
-        elif stage == 2 and not onward:
-            pass
-        elif stage in ("go", 2):
-            push(send(time, 3.3, "out"), 3, c + (arrived if stage == 2 else 0))
-        elif stage == 3:
-            push(send(time, 3.3, "mid", "out"), 4, c)
-        elif stage == 4:
-            push(send(time, 3.3, "mid", "out"), 5, c)
-        elif stage == 5:
-            push(send(time, 3.3, "out"), 6, c)
-    return steps
-
-
-def feed_plan():
+def feed_plan(moved):
     schedule = {
         0: [("begin", 0)],
         1: [(0, 0), (0, 1), (0, 2)],
         9: [(1, 0), (1, 1), (1, 2)],
         11: [(2, 0), (2, 1), (2, 2), ("finish", 0)],
     }
-    return Plan(((0, 0, 288), (1, 0, 96), (2, 0, 192)), (), schedule, 1)
+    return Plan(((0, 0, 288), (1, 0, 96), (2, 0, 192)), (), schedule, 1, moved=moved)
 
 
 def attend_plan():
     schedule = {
-        0: [("begin", 0)],
-        1: [(0, 0), (0, 1), (0, 2), (0, 3), (0, 4)],
-        6: [(1, 0), (1, 1), (1, 2)],
-        7: [(1, 3), (1, 4), (2, 0), (2, 1)],
-        8: [(2, 2), (2, 3), (2, 4), ("finish", 0)],
+        0: [("begin", 0), ("vec", 0)],
+        1: [("vec", 1), (0, 0), (0, 1), (0, 2), (0, 3), (0, 4)],
+        3: [("vec", 2)],
+        4: [("vec", 3)],
+        6: [("vec", 4), (1, 0), (1, 1), (1, 2)],
+        7: [("vec", 5), (1, 3), (1, 4)],
+        8: [(2, 0), (2, 1), (2, 2), (2, 3), (2, 4), ("finish", 0)],
     }
-    return Plan(((0, 192, 192), (1, 0, 384), (2, 0, 384)), (), schedule, 2)
+    return Plan(((0, 192, 192), (1, 0, 384), (2, 0, 384)), (), schedule, 2, vector=32)
 
 
 def last_plan():
-    order = [step[1:] for step in landing_order(2, 5, True, True)]
-    return Plan(((0, 0, 288), (1, 0, 96)), (5,), order, 3, onward=True, vector=True)
-
-
-def unpack_kernel(first_ref, last_ref, vec_ref, *outs):
+    order = [("vec", 0), *[("go", k) for k in range(5)], ("vec", 1), (0, 0), ("vec", 2), (0, 1)]
+    order += [("vec", 3), (1, 0), (1, 1), (3, 0), (2, 0), (2, 1), (3, 1), (4, 0), (3, 2), (4, 1)]
+    order += [(5, 0), (3, 3), (4, 2), (5, 1), (6, 0), (3, 4), ("vec", 4), (4, 3), (5, 2), (6, 1)]
+    order += [(3, 5), (4, 4), (5, 3), (6, 2), (3, 6), (4, 5), (5, 4), (6, 3), (4, 6), (5, 5)]
+    order += [(6, 4), ("vec", 5), (5, 6), (6, 5), (6, 6)]
+    return Plan(((0, 0, 288), (1, 0, 96)), (5,), order, 3, onward=True, vector=8)
+
+
+def unpack_kernel(feed_ref, first_ref, last_ref, vec_ref, bias_ref, *outs):
     (
         e_in, e_out, e_bias, e_norm, e_expand, e_expand_bias, e_shrink, e_shrink_bias,
         s_in, s_out, c_in, c_out, d_bias, d_norm, d_expand, d_expand_bias, d_shrink, d_shrink_bias,
@@ -1562,22 +1588,23 @@
 
     for i in range(4):
         part = slice(i * WIDTH, (i + 1) * WIDTH)
-        d_expand[:, part] = rows_of(first_ref, i)
+        d_expand[:, part] = rows_of(feed_ref, i)
         e_expand[:, part] = rows_of(last_ref, 2 + i)
-    d_shrink[...] = rows_of(first_ref, 4, 4)
+    d_shrink[...] = rows_of(feed_ref, 4, 4)
     for i in range(3):
-        c_in[i] = rows_of(first_ref, 8 + i)
+        c_in[i] = rows_of(first_ref, i)
         e_in[i] = rows_of(last_ref, 10 + i)
-    c_out[...] = rows_of(first_ref, 11)
-    s_in[0] = rows_of(first_ref, 12)
-    s_in[1] = rows_of(first_ref, 13)
+    c_out[...] = rows_of(first_ref, 3)
+    s_in[0] = rows_of(first_ref, 4)
+    s_in[1] = rows_of(first_ref, 5)
     s_in[2] = rows_of(last_ref, 0)
     s_out[...] = rows_of(last_ref, 1)
     e_shrink[...] = rows_of(last_ref, 6, 4)
     e_out[...] = rows_of(last_ref, 13)
     me = lax.axis_index("dp")
     mine = pltpu.roll(vec_ref[...], WIDTH - me * rows, 1)
-    e_bias[...] = mine[0:3, 0:rows]
+    e_bias[0:2] = pltpu.roll(bias_ref[...], WIDTH - me * rows, 1)[0:2, 0:rows]
+    e_bias[2:3] = mine[2:3, 0:rows]
     e_norm[0] = mine[3:5, 0:rows]
     e_norm[1] = mine[5:7, 0:rows]
     e_shrink_bias[...] = mine[11:12, 0:rows]
@@ -1592,7 +1619,7 @@
         to[...] = jnp.where(me % 2 == 0, row[:, : WIDTH // 2], row[:, WIDTH // 2 :])
 
 
-def unpack(first, last, vector):
+def unpack(feed, first, last, vector, biases):
     rows, width = WIDTH // 8, WIDTH
     square, cube = (rows, width), (3, rows, width)
     wide_one, tall_one = (rows, 4 * width), (4 * rows, width)
@@ -1604,13 +1631,13 @@
     here = pl.BlockSpec(memory_space=VMEM)
     return pl.pallas_call(
         unpack_kernel,
-        in_specs=[here] * 3,
+        in_specs=[here] * 5,
         out_specs=[here] * len(shapes),
         out_shape=[like(shape, wide_type) for shape in shapes],
         compiler_params=params(40),
         cost_estimate=cost(1e7, 1.3e7),
         name="unpack",
-    )(first, last, vector)
+    )(feed, first, last, vector, biases)
 
 
 def sum_whole(grads):
@@ -1770,13 +1797,12 @@
         cross_inward,
         decoder_norms,
     )
-    decoder_out = shifted(out, "section", half_way)
-    decoder_grad = shifted(dy, "section", half_way)
     states_back = spread_rows(table, returned.reshape(-1, WIDTH), x.shape[0])
 
     hosts = paired()
-    plan = feed_plan() if hosts else None
-    guests = [pair[k] for k in range(2) for pair in (d_cross_in, d_cross_out, d_self)] if hosts else []
+    plan = feed_plan([like(out.shape, out.dtype), like(dy.shape, dy.dtype)]) if hosts else None
+    pairs = (d_cross_in, d_cross_out, d_self)
+    guests = [pair[k] for k in range(2) for pair in pairs] + [out, dy] if hosts else []
     (dmix, feed_vec, feed_expand), (e_expand, e_shrink, e_out), from_feed = encoder_feed_back(
         states_back,
         summed,
@@ -1790,17 +1816,13 @@
         plan,
         guests,
     )
-    plan = attend_plan() if hosts else None
     if hosts:
-        guests = [pair[k] for k in range(2) for pair in (d_self, e_expand, e_shrink)]
-        early = jnp.concatenate([d_feed, from_feed[0]], 0)
-        early, dmix = lax.optimization_barrier((early, dmix))
-        early = lax.psum(early, "section")
-    (dx, attend_vec), e_in, from_attend = encoder_attend_back(
-        dmix, x, qkv, context, stats, encoder_inward, encoder_outward, plan, guests
-    )
-    vectors = [
-        jnp.concatenate([attend_vec[0:2], feed_vec[5:6]], 0),
+        decoder_out, decoder_grad = from_feed[1:]
+    else:
+        decoder_out = shifted(out, "section", half_way)
+        decoder_grad = shifted(dy, "section", half_way)
+    rest = [
+        jnp.concatenate([jnp.zeros((2, WIDTH), wide_type), feed_vec[5:6]], 0),
         jnp.stack([feed_vec[3:5], feed_vec[0:2]]),
         feed_expand[0],
         feed_vec[2],
@@ -1809,15 +1831,26 @@
         mid_expand[0],
         mid_vec[2],
     ]
+    plan = attend_plan() if hosts else None
     if hosts:
-        flat = jnp.concatenate([v.reshape(-1) for v in vectors])
-        flat = jnp.pad(flat, (0, VEC_ROWS * WIDTH - flat.size)).reshape(VEC_ROWS, WIDTH)
-        last, vector = last_sums(last_plan(), (e_in, e_out), from_attend, flat)
-        results = unpack(early, last, vector)
+        guests = [pair[k] for k in range(2) for pair in (d_self, e_expand, e_shrink)]
+        flat = jnp.concatenate([v.reshape(-1) for v in rest])
+        flat = jnp.pad(flat, (0, 32 * WIDTH - flat.size)).reshape(32, WIDTH)
+        guests.append(flat)
+        early, dmix = lax.optimization_barrier(((d_feed, from_feed[0]), dmix))
+        early = lax.psum(early, "section")
+    (dx, attend_vec), e_in, from_attend = encoder_attend_back(
+        dmix, x, qkv, context, stats, encoder_inward, encoder_outward, plan, guests
+    )
+    if hosts:
+        last, vector = last_sums(last_plan(), (e_in, e_out), from_attend[:1], attend_vec)
+        results = unpack(*early, last, from_attend[1], vector)
         results = [r[0] if n in (5, 7, 15, 17) else r for n, r in enumerate(results)]
     else:
         results = sum_any(
-            [e_in, e_out, e_expand, e_shrink, d_self, d_cross_in, d_cross_out], d_feed, vectors
+            [e_in, e_out, e_expand, e_shrink, d_self, d_cross_in, d_cross_out],
+            d_feed,
+            [rest[0] + jnp.pad(attend_vec[0:2], ((0, 1), (0, 0)))] + rest[1:],
         )
     return (decoder_out[None], dx[None], decoder_grad[None], *results)
 

time: 503 us -> 491 us (0.976)
  Pallas kernels: 377 us -> 367 us
    all_to_all x1, waiting for transfers between devices: 16.7 us -> 25.5 us  [on_device(): lax.all_to_all(dpool.reshape(owners, -1, WIDTH), 'dp', split_axis=0, conc...]
    ppermute x4 -> x2, waiting for transfers between devices: 7.4 us -> 0.01 us  [shifted(): lax.ppermute(value, axis, [(i, (i + by) % length) for i in range(length)])]
    unnamed x84 -> x90, local copies, waits for them, and re-layouts: 25.6 us -> 27.4 us
  transfers between devices with their start and end apart: 8 -> 6, of which waited for: 3 -> 2; matrix products, arithmetic and copies ran while one was open for 2% -> 2% of each run, Pallas kernels for 67% -> 67%
where the time goes in v4:
time: 491 us; the launch traced here: 482 us
  Pallas kernels  367 us (75%)
  waiting for transfers between devices  48.6 us (10%)
  local copies, waits for them, and re-layouts  34.6 us (7%)
  between operations  14.8 us (3%)
  starting transfers between devices  12.9 us (3%)
    pallas_call x1, Pallas kernels, last_sums(): pl.pallas_call(functools.partial(last_sums_kernel, plan), in_specs=plan.i...  84.2 us
    pallas_call x1, Pallas kernels, encoder_attend_back(): pl.pallas_call(functools.partial(encoder_attend_back_kernel, plan), grid=...  69.9 us
    pallas_call x1, Pallas kernels, encoder_feed_back(): pl.pallas_call(functools.partial(encoder_feed_back_kernel, plan), grid=(4...  50.3 us
    pallas_call x1, Pallas kernels, encoder_attend(): pl.pallas_call(encoder_attend_kernel, grid=(groups,), in_specs=[full(toke...  30.9 us
    pallas_call x1, Pallas kernels, encoder_feed(): pl.pallas_call(encoder_feed_kernel, grid=(4,), in_specs=[full(tokens, wid...  27.8 us
    unnamed x90, local copies, waits for them, and re-layouts  27.4 us
    all_to_all x1, waiting for transfers between devices, on_device(): lax.all_to_all(dpool.reshape(owners, -1, WIDTH), 'dp', split_axis=0, conc...  25.5 us
    pallas_call x1, Pallas kernels, cross_back(): pl.pallas_call(cross_back_kernel, grid=(groups,), in_specs=[pl.BlockSpec(...  24.4 us
  transfers between devices with their start and end apart: 6, of which 2 were waited for; matrix products, arithmetic and copies ran while one was open for 2% of the time, Pallas kernels for 67%

profile of v4, /device:TPU:0, one launch (start us, length us, event | category | flops | bytes accessed | tf_op | source)
XLA Modules:
  0.0 481.7 jit_solution(12714415482587824553)
XLA Ops:
  8.2 4.1 collective-permute-start.1
  15.5 30.9 %encoder_attend.1 = (bf16[3,1024,768]{2,1,0:T(8,128)(2,1)}, f32[1024,768]{1,0:T(8,128)}, bf16[1024,768]{1,0:T(8,128)(2,1)}, f32[3,8,1024]{2,1,0:T(8,128)}, f32[1024,768]{1,0:T(8,128)}) custom-call(bf16[1024,768]{1,0:T(8,128)(2,1)} %bitcast.58, bf16[3,768,768]{2,1,0:T(8,128)(2,1)} %refs_5_.1, bf16[768,768]{1,0:T(8,128)(2,1)} %refs_6_.3, f32[3,768]{1,0:T(4,128)} %b_ref.3, ...), custom_call_target="tpu_custom_call" | custom-call | flops 30000001024 | bytes 20000000 | tf_op jit(solution)/shard_map/encoder_attend/pallas_call | solution.py:200
  46.5 27.8 %encoder_feed.1 = (bf16[1024,3072]{1,0:T(8,128)(2,1)}, bf16[1024,3072]{1,0:T(8,128)(2,1)}, f32[1024,768]{1,0:T(8,128)}, bf16[1024,768]{1,0:T(8,128)(2,1)}) custom-call(f32[1024,768]{1,0:T(8,128)} %get-tuple-element.98.mixed_ref.refs_2_, f32[2,2,768]{2,1,0:T(2,128)} %refs_6_.2, bf16[768,3072]{1,0:T(8,128)(2,1)} %refs_7_.1, f32[1,3072]{1,0:T(1,128)} %bitcast.60, ...), custom_call_target="tpu_custom_call" | custom-call | flops 20000000000 | bytes 30000000 | tf_op jit(solution)/shard_map/encoder_feed/pallas_call | solution.py:270
  76.8 6.4 %pick_rows.1 = bf16[2048,768]{1,0:T(8,128)(2,1)} custom-call(s32[2048,1]{1,0:T(8,128)S(1)} %bitcast.43, bf16[1024,768]{1,0:T(8,128)(2,1)S(1)} %copy-done.12), custom_call_target="tpu_custom_call" | custom-call | flops 4000000000 | bytes 5000000 | tf_op jit(solution)/shard_map/pick_rows/pallas_call | solution.py:619
  83.2 4.4 all-to-all-start
  88.9 6.5 %slot_mask.1 = (f32[128,2048]{1,0:T(8,128)S(1)}, f32[2048,128]{1,0:T(8,128)S(1)}) custom-call(s32[1024,128]{1,0:T(8,128)S(1)} %bitcast.44), custom_call_target="tpu_custom_call" | custom-call | flops 10000000000 | bytes 1000000 | tf_op jit(solution)/shard_map/slot_mask/pallas_call | solution.py:600
  96.4 3.1 self_forward.1
  102.5 23.1 %all-to-all-done = bf16[8,256,768]{2,1,0:T(8,128)(2,1)} async-done(((bf16[8,256,768]{2,1,0:T(8,128)(2,1)}), bf16[8,256,768]{2,1,0:T(8,128)(2,1)}, u32[]{:S(2)}, u32[]{:S(2)}) %all-to-all-start) | async-done | bytes 3145760 | tf_op jit(solution)/shard_map/all_to_all | solution.py:1757
  125.5 17.4 %cross_forward.1 = (bf16[2,2048,768]{2,1,0:T(8,128)(2,1)}, f32[128,768]{1,0:T(8,128)}, f32[3,8,512]{2,1,0:T(8,128)}) custom-call(bf16[2048,768]{1,0:T(8,128)(2,1)} %bitcast.5.pooled_ref, bf16[128,768]{1,0:T(8,128)(2,1)} %copy-done.30, f32[128,2048]{1,0:T(8,128)} %copy-done.17, bf16[3,768,768]{2,1,0:T(8,128)(2,1)} %cw_ref.3, f32[6,768]{1,0:T(8,128)} %b_ref.5), custom_call_target="tpu_custom_call" | custom-call | flops 20000000000 | bytes 12000000 | tf_op jit(solution)/shard_map/cross_forward/pallas_call | solution.py:782
  142.9 17.6 %middle.1 = (bf16[128,768]{1,0:T(8,128)(2,1)}, f32[128,768]{1,0:T(8,128)}, bf16[128,768]{1,0:T(8,128)(2,1)}, f32[8,768]{1,0:T(8,128)}, f32[1,3072]{1,0:T(1,128)}...) custom-call(f32[128,768]{1,0:T(8,128)} %copy-done.19, ...), custom_call_target="tpu_custom_call" | custom-call | flops 20000000000 | bytes 22000000 | tf_op jit(solution)/shard_map/middle/pallas_call | solution.py:879
  160.5 24.4 %cross_back.1 = (bf16[2,2048,768]{2,1,0:T(8,128)(2,1)}, bf16[128,768]{1,0:T(8,128)(2,1)}, f32[8,768]{1,0:T(8,128)}, bf16[2048,768]{1,0:T(8,128)(2,1)}) custom-call(bf16[2,2048,768]{2,1,0:T(8,128)(2,1)} %get-tuple-element.102.kv_ref, bf16[128,768]{1,0:T(8,128)(2,1)} %copy-done.30, f32[128,768]{1,0:T(8,128)} %get-tuple-element.103.c_ref, ...), custom_call_target="tpu_custom_call" | custom-call | flops 30000001024 | bytes 22000000 | tf_op jit(solution)/shard_map/cross_back/pallas_call | solution.py:964
  184.9 3.7 all-to-all-start.1
  194.9 9.4 %self_back.1 = (f32[128,768]{1,0:T(8,128)S(1)}, f32[8,768]{1,0:T(8,128)S(1)}, bf16[4,384,768]{2,1,0:T(8,128)(2,1)S(1)}, bf16[4,384,768]{2,1,0:T(8,128)(2,1)}) custom-call(s32[4]{0:T(128)S(1)} %slice_bitcast_fusion.6.lengths_ref, bf16[128,768]{1,0:T(8,128)(2,1)S(1)} %get-tuple-element.178.y_ref, f32[128,768]{1,0:T(8,128)S(1)} %copy-done.20, ...), custom_call_target="tpu_custom_call" | custom-call | flops 20000000000 | bytes 15000000 | tf_op jit(solution)/shard_map/self_back/pallas_call | solution.py:1082
  204.3 1.4 copy-done.18
  209.3 11.0 %cross_grads.1 = (bf16[4,288,768]{2,1,0:T(8,128)(2,1)S(1)}, bf16[4,288,768]{2,1,0:T(8,128)(2,1)S(1)}) custom-call(bf16[2048,768]{1,0:T(8,128)(2,1)} %bitcast.5.pooled_ref, bf16[2,2048,768]{2,1,0:T(8,128)(2,1)} %get-tuple-element.113.dkv_ref, f32[128,768]{1,0:T(8,128)S(1)} %copy-done.21, bf16[128,768]{1,0:T(8,128)(2,1)S(1)} %copy-done.23, ...), custom_call_target="tpu_custom_call" | custom-call | flops 10000000000 | bytes 15000000 | tf_op jit(solution)/shard_map/cross_grads/pallas_call | solution.py:1018
  222.7 25.5 %all-to-all-done.1 = bf16[8,256,768]{2,1,0:T(8,128)(2,1)S(1)} async-done(((bf16[8,256,768]{2,1,0:T(8,128)(2,1)}), bf16[8,256,768]{2,1,0:T(8,128)(2,1)S(1)}, u32[]{:S(2)}, u32[]{:S(2)}) %all-to-all-start.1) | async-done | bytes 3145760 | tf_op jit(solution)/shard_map/all_to_all | solution.py:1783
  248.2 5.3 %spread_rows.1.refs_0_ = bf16[1024,768]{1,0:T(8,128)(2,1)S(1)} custom-call(s32[1,2048]{1,0:T(1,128)S(1)} %bitcast.46, bf16[2048,768]{1,0:T(8,128)(2,1)S(1)} %bitcast.42), custom_call_target="tpu_custom_call" | custom-call | flops 4000000000 | bytes 5000000 | tf_op jit(solution)/shard_map/spread_rows/pallas_call | solution.py:652
  254.6 50.3 %encoder_feed_back.1 = (f32[1024,768]{1,0:T(8,128)}, f32[8,768]{1,0:T(8,128)}, f32[1,3072]{1,0:T(1,128)}, bf16[4,384,768]{2,1,0:T(8,128)(2,1)}, bf16[4,384,768]{...) custom-call(bf16[1024,768]{1,0:T(8,128)(2,1)} %copy-done.13, ...), custom_call_target="tpu_custom_call" | custom-call | flops 40000000000 | bytes 50000000 | tf_op jit(solution)/shard_map/encoder_feed_back/pallas_call | solution.py:397
  308.1 69.9 %encoder_attend_back.1 = (f32[1024,768]{1,0:T(8,128)}, f32[8,768]{1,0:T(8,128)}, bf16[4,288,768]{2,1,0:T(8,128)(2,1)}, bf16[4,288,768]{2,1,0:T(8,128)(2,1)}, bf1...) custom-call(f32[1024,768]{1,0:T(8,128)} %get-tuple-element.130.refs_0_, bf16[1024,768]{1,0:T(8,128)(2,1)} %bitcast.59, ...), custom_call_target="tpu_custom_call" | custom-call | flops 49999998976 | bytes 40000000 | tf_op jit(solution)/shard_map/encoder_attend_back/pallas_call | solution.py:526
  378.0 84.2 %last_sums.1 = (bf16[1344,768]{1,0:T(8,128)(2,1)}, f32[8,768]{1,0:T(8,128)}) custom-call(bf16[4,288,768]{2,1,0:T(8,128)(2,1)} %get-tuple-element.148.refs_0_, bf16[4,96,768]{2,1,0:T(8,128)(2,1)} %get-tuple-element.149.refs_1_, bf16[4,288,768]{2,1,0:T(8,128)(2,1)} %get-tuple-element.150.refs_2_, bf16[4,96,768]{2,1,0:T(8,128)(2,1)} %get-tuple-element.151.refs_3_, ...), custom_call_target="tpu_custom_call" | custom-call | flops 100000000 | bytes 100000000 | tf_op jit(solution)/shard_map/last_sums/pallas_call | solution.py:1535
  462.3 1.6 copy-done
  463.9 1.3 copy-done.1
  467.1 3.3 unpack.1
  472.2 1.7 copy.74
  (124 shorter events, 32.8 us)
Async XLA Ops:
  8.2 66.7 %collective-permute-start.1 = (bf16[256,768]{1,0:T(8,128)(2,1)S(1)}, bf16[256,768]{1,0:T(8,128)(2,1)S(1)}, u32[]{:S(2)}, u32[]{:S(2)}) collective-permute-start(bf16[256,768]{1,0:T(8,128)(2,1)S(1)} %pad_maximum_fusion), channel_id=1, source_target_pairs={{0,2},{1,3},{2,0},{3,1},{4,6},{5,7},{6,4},{7,5},{8,10},{9,11},{10,... | collective-permute-start | bytes 1179656 | tf_op jit(solution)/shard_map/ppermute | solution.py:1112
  14.2 61.4 %collective-permute-start = (s32[131,1024]{1,0:T(8,128)S(1)}, s32[131,1024]{1,0:T(8,128)S(1)}, u32[]{:S(2)}, u32[]{:S(2)}) collective-permute-start(s32[131,1024]{1,0:T(8,128)S(1)} %pad_add_fusion), channel_id=1, source_target_pairs={{0,2},{1,3},{2,0},{3,1},{4,6},{5,7},{6,4},{7,5},{8,10},{9,11},{10,... | collective-permute-start | bytes 1609736 | tf_op jit(solution)/shard_map/ppermute | solution.py:1112
  46.5 27.8 %copy-start.37 = (f32[768]{0:T(1024)S(1)}, f32[768]{0:T(1024)}, u32[]{:S(2)}) copy-start(f32[768]{0:T(1024)} %param.47) | copy-start | bytes 9220
  74.3 2.5 copy-start.12
  83.2 42.3 %all-to-all-start = ((bf16[8,256,768]{2,1,0:T(8,128)(2,1)}), bf16[8,256,768]{2,1,0:T(8,128)(2,1)}, u32[]{:S(2)}, u32[]{:S(2)}) async-start(bf16[8,256,768]{2,1,0:T(8,128)(2,1)} %bitcast.4), calls=%async_computation | async-start | bytes 6291456 | tf_op jit(solution)/shard_map/all_to_all | solution.py:1757
  87.6 220.5 %reduce-scatter.2.cloned.1.call-start = ((), (), s32[]{:S(2)}) async-start(), calls=%async_computation.3 | async-start | bytes 10616832 | tf_op jit(solution)/shard_map/reduce_scatter | solution.py:1779
  88.9 7.5 %copy-start.5 = (bf16[3,768,768]{2,1,0:T(8,128)(2,1)S(1)}, bf16[3,768,768]{2,1,0:T(8,128)(2,1)}, u32[]{:S(2)}) copy-start(bf16[3,768,768]{2,1,0:T(8,128)(2,1)} %w_ref.9) | copy-start | bytes 10616836
  88.9 7.5 %copy-start.6 = (bf16[3,768,768]{2,1,0:T(8,128)(2,1)S(1)}, bf16[3,768,768]{2,1,0:T(8,128)(2,1)}, u32[]{:S(2)}) copy-start(bf16[3,768,768]{2,1,0:T(8,128)(2,1)} %cw_ref.3) | copy-start | bytes 10616836
  88.9 7.5 %copy-start.7 = (bf16[768,768]{1,0:T(8,128)(2,1)S(1)}, bf16[768,768]{1,0:T(8,128)(2,1)}, u32[]{:S(2)}) copy-start(bf16[768,768]{1,0:T(8,128)(2,1)} %wo_ref.5) | copy-start | bytes 3538948
  88.9 7.5 %copy-start.9 = (f32[6,768]{1,0:T(8,128)S(1)}, f32[6,768]{1,0:T(8,128)}, u32[]{:S(2)}) copy-start(f32[6,768]{1,0:T(8,128)} %b_ref.5) | copy-start | bytes 55300
  88.9 7.5 %copy-start.10 = (f32[3,2,768]{2,1,0:T(2,128)S(1)}, f32[3,2,768]{2,1,0:T(2,128)}, u32[]{:S(2)}) copy-start(f32[3,2,768]{2,1,0:T(2,128)} %n_ref.9) | copy-start | bytes 55300
  96.4 3.1 copy-start.16
  184.9 3.7 copy-start.11
  184.9 63.3 %all-to-all-start.1 = ((bf16[8,256,768]{2,1,0:T(8,128)(2,1)}), bf16[8,256,768]{2,1,0:T(8,128)(2,1)S(1)}, u32[]{:S(2)}, u32[]{:S(2)}) async-start(bf16[8,256,768]{2,1,0:T(8,128)(2,1)} %bitcast.48), calls=%async_computation.1 | async-start | bytes 6291456 | tf_op jit(solution)/shard_map/all_to_all | solution.py:1783
  188.6 273.7 %all-reduce.6.cloned.1.call-start = ((), (), s32[]{:S(2)}) async-start(), calls=%async_computation.4 | async-start | bytes 4128768 | tf_op jit(solution)/shard_map/psum | solution.py:1841
  188.7 1.3 copy-start.8
  194.9 12.3 %copy-start.35 = (f32[8,768]{1,0:T(8,128)S(1)}, f32[8,768]{1,0:T(8,128)}, u32[]{:S(2)}) copy-start(f32[8,768]{1,0:T(8,128)} %get-tuple-element.142) | copy-start | bytes 73732
  204.3 1.4 copy-start.18
  254.6 52.8 %copy-start.36 = (f32[1,3072]{1,0:T(1,128)S(1)}, f32[1,3072]{1,0:T(1,128)}, u32[]{:S(2)}) copy-start(f32[1,3072]{1,0:T(1,128)} %get-tuple-element.143) | copy-start | bytes 36868
  378.0 84.3 %copy-start.3 = (f32[32,768]{1,0:T(8,128)S(1)}, f32[32,768]{1,0:T(8,128)}, u32[]{:S(2)}) copy-start(f32[32,768]{1,0:T(8,128)} %get-tuple-element.155.vec_ref) | copy-start | bytes 294916
  378.0 93.6 %copy-start.34 = (bf16[128,768]{1,0:T(8,128)(2,1)S(1)}, bf16[128,768]{1,0:T(8,128)(2,1)}, u32[]{:S(2)}) copy-start(bf16[128,768]{1,0:T(8,128)(2,1)} %get-tuple-element.126) | copy-start | bytes 589828
  378.0 94.2 %copy-start.31 = (f32[1024,768]{1,0:T(8,128)S(1)}, f32[1024,768]{1,0:T(8,128)}, u32[]{:S(2)}) copy-start(f32[1024,768]{1,0:T(8,128)} %get-tuple-element.144) | copy-start | bytes 9437188
  462.3 1.6 copy-start
  472.2 1.7 copy-start.33
  (20 other events, 19.1 us)
Sparse Core Ops, SparseCore 0:
  160.6 109.9 reduce-scatter.1
  308.2 100.4 all-reduce.5

commit v5 on v4

--- a/solution.py
+++ b/solution.py
@@ -925,9 +925,10 @@
     column = jnp.sum(product, -1, keepdims=True)
     inner = jnp.broadcast_to(column, (heads * rows, 128)).T[0:1]
     stat = stat_ref[0, 0:1]
-    for h in range(heads):
-        part = slice(h * rows, (h + 1) * rows)
-        weight = jnp.exp(dot(kv_ref[0], q_heads[part], NT) + mask_ref[...] - stat[:, part])
+    mask = jnp.concatenate([mask_ref[...]] * 2, 1)
+    for h in range(0, heads, 2):
+        part = slice(h * rows, (h + 2) * rows)
+        weight = jnp.exp(dot(kv_ref[0], q_heads[part], NT) + mask - stat[:, part])
         weight_back = dot(kv_ref[1], dc_heads[part], NT)
         weights[:, part] = low(weight)
         scores_back[:, part] = low(weight * (weight_back - inner[:, part]))
@@ -1634,7 +1635,7 @@
         in_specs=[here] * 5,
         out_specs=[here] * len(shapes),
         out_shape=[like(shape, wide_type) for shape in shapes],
-        compiler_params=params(40),
+        compiler_params=params(),
         cost_estimate=cost(1e7, 1.3e7),
         name="unpack",
     )(feed, first, last, vector, biases)
@@ -1727,19 +1728,17 @@
 ):
     x = encoder_input[0]
     half_way = lax.axis_size("section") // 2
-    queries = decoder_input.shape[1]
-    topk = retrieved.shape[2]
-    rows_low = shifted(jnp.concatenate([decoder_input[0], cotangent[0]], 0), "section", -half_way)
-    y, grad = rows_low[:queries], rows_low[queries:]
-    lengths_row = jnp.pad(decoder_lengths[0], ((0, 0), (0, topk - decoder_lengths.shape[2])))
-    integers = shifted(
-        jnp.concatenate([retrieved[0], pool_table[0, 0].reshape(-1, topk), lengths_row], 0),
-        "section",
-        -half_way,
-    )
-    slots = integers[:queries]
-    table = integers[queries:-1].reshape(-1)
-    lengths = integers[-1, : decoder_lengths.shape[2]]
+    y, grad, slots, table, lengths = [
+        shifted(value, "section", -half_way)
+        for value in (
+            decoder_input[0],
+            cotangent[0],
+            retrieved[0],
+            pool_table[0, 0],
+            decoder_lengths[0],
+        )
+    ]
+    table, lengths = table.reshape(-1), lengths[0]
     owners = pool_table.shape[2]
 
     qkv, context, context_low, stats, mixed = encoder_attend(

time: 491 us -> 493 us (level)
  starting transfers between devices: 12.9 us -> 18.9 us
    ppermute x2 -> x5, starting transfers between devices: 4.18 us -> 10 us  [shifted(): lax.ppermute(value, axis, [(i, (i + by) % length) for i in range(length)])]
    unnamed x90 -> x79, local copies, waits for them, and re-layouts: 27.4 us -> 29.3 us
  transfers between devices with their start and end apart: 6 -> 9, of which waited for: 2 -> 2; matrix products, arithmetic and copies ran while one was open for 2% -> 2% of each run, Pallas kernels for 67% -> 71%
where the time goes in v5:
time: 493 us; the launch traced here: 483 us
  Pallas kernels  367 us (74%)
  waiting for transfers between devices  45.6 us (9%)
  local copies, waits for them, and re-layouts  34.3 us (7%)
  starting transfers between devices  18.9 us (4%)
  between operations  14.8 us (3%)
    pallas_call x1, Pallas kernels, last_sums(): pl.pallas_call(functools.partial(last_sums_kernel, plan), in_specs=plan.i...  84.3 us
    pallas_call x1, Pallas kernels, encoder_attend_back(): pl.pallas_call(functools.partial(encoder_attend_back_kernel, plan), grid=...  69.9 us
    pallas_call x1, Pallas kernels, encoder_feed_back(): pl.pallas_call(functools.partial(encoder_feed_back_kernel, plan), grid=(4...  50.3 us
    pallas_call x1, Pallas kernels, encoder_attend(): pl.pallas_call(encoder_attend_kernel, grid=(groups,), in_specs=[full(toke...  30.9 us
    unnamed x79, local copies, waits for them, and re-layouts  29.3 us
    pallas_call x1, Pallas kernels, encoder_feed(): pl.pallas_call(encoder_feed_kernel, grid=(4,), in_specs=[full(tokens, wid...  27.9 us
    all_to_all x1, waiting for transfers between devices, on_device(): lax.all_to_all(dpool.reshape(owners, -1, WIDTH), 'dp', split_axis=0, conc...  25.8 us
    pallas_call x1, Pallas kernels, cross_back(): pl.pallas_call(cross_back_kernel, grid=(groups,), in_specs=[pl.BlockSpec(...  21.8 us
  transfers between devices with their start and end apart: 9, of which 2 were waited for; matrix products, arithmetic and copies ran while one was open for 2% of the time, Pallas kernels for 71%

profile of v5, /device:TPU:0, one launch (start us, length us, event | category | flops | bytes accessed | tf_op | source)
XLA Modules:
  0.0 483.4 jit_solution(17796061536785903480)
XLA Ops:
  7.2 4.1 collective-permute-start.1
  11.4 2.8 collective-permute-start.2
  15.5 2.9 collective-permute-start.3
  19.7 30.9 %encoder_attend.1 = (bf16[3,1024,768]{2,1,0:T(8,128)(2,1)}, f32[1024,768]{1,0:T(8,128)}, bf16[1024,768]{1,0:T(8,128)(2,1)}, f32[3,8,1024]{2,1,0:T(8,128)}, f32[1024,768]{1,0:T(8,128)}) custom-call(bf16[1024,768]{1,0:T(8,128)(2,1)} %bitcast.55, bf16[3,768,768]{2,1,0:T(8,128)(2,1)} %refs_5_.1, bf16[768,768]{1,0:T(8,128)(2,1)} %refs_6_.3, f32[3,768]{1,0:T(4,128)} %b_ref.3, ...), custom_call_target="tpu_custom_call" | custom-call | flops 30000001024 | bytes 20000000 | tf_op jit(solution)/shard_map/encoder_attend/pallas_call | solution.py:200
  50.7 27.9 %encoder_feed.1 = (bf16[1024,3072]{1,0:T(8,128)(2,1)}, bf16[1024,3072]{1,0:T(8,128)(2,1)}, f32[1024,768]{1,0:T(8,128)}, bf16[1024,768]{1,0:T(8,128)(2,1)}) custom-call(f32[1024,768]{1,0:T(8,128)} %get-tuple-element.98.mixed_ref.refs_2_, f32[2,2,768]{2,1,0:T(2,128)} %refs_6_.2, bf16[768,3072]{1,0:T(8,128)(2,1)} %refs_7_.1, f32[1,3072]{1,0:T(1,128)} %bitcast.59, ...), custom_call_target="tpu_custom_call" | custom-call | flops 20000000000 | bytes 30000000 | tf_op jit(solution)/shard_map/encoder_feed/pallas_call | solution.py:270
  80.9 6.4 %pick_rows.1 = bf16[2048,768]{1,0:T(8,128)(2,1)} custom-call(s32[2048,1]{1,0:T(8,128)S(1)} %bitcast.40, bf16[1024,768]{1,0:T(8,128)(2,1)S(1)} %copy-done.7), custom_call_target="tpu_custom_call" | custom-call | flops 4000000000 | bytes 5000000 | tf_op jit(solution)/shard_map/pick_rows/pallas_call | solution.py:619
  87.3 4.6 all-to-all-start
  92.5 2.0 copy-done
  94.5 2.0 copy-done.1
  96.5 3.1 self_forward.1
  102.5 6.5 %slot_mask.1 = (f32[128,2048]{1,0:T(8,128)S(1)}, f32[2048,128]{1,0:T(8,128)S(1)}) custom-call(s32[1024,128]{1,0:T(8,128)S(1)} %bitcast.43), custom_call_target="tpu_custom_call" | custom-call | flops 10000000000 | bytes 1000000 | tf_op jit(solution)/shard_map/slot_mask/pallas_call | solution.py:600
  110.0 19.8 %all-to-all-done = bf16[8,256,768]{2,1,0:T(8,128)(2,1)} async-done(((bf16[8,256,768]{2,1,0:T(8,128)(2,1)}), bf16[8,256,768]{2,1,0:T(8,128)(2,1)}, u32[]{:S(2)}, u32[]{:S(2)}) %all-to-all-start) | async-done | bytes 3145760 | tf_op jit(solution)/shard_map/all_to_all | solution.py:1756
  129.8 17.4 %cross_forward.1 = (bf16[2,2048,768]{2,1,0:T(8,128)(2,1)}, f32[128,768]{1,0:T(8,128)}, f32[3,8,512]{2,1,0:T(8,128)}) custom-call(bf16[2048,768]{1,0:T(8,128)(2,1)} %bitcast.4.pooled_ref, bf16[128,768]{1,0:T(8,128)(2,1)} %copy-done.25, f32[128,2048]{1,0:T(8,128)} %copy-done.12, bf16[3,768,768]{2,1,0:T(8,128)(2,1)} %cw_ref.3, f32[6,768]{1,0:T(8,128)} %b_ref.5), custom_call_target="tpu_custom_call" | custom-call | flops 20000000000 | bytes 12000000 | tf_op jit(solution)/shard_map/cross_forward/pallas_call | solution.py:782
  147.8 17.5 %middle.1 = (bf16[128,768]{1,0:T(8,128)(2,1)}, f32[128,768]{1,0:T(8,128)}, bf16[128,768]{1,0:T(8,128)(2,1)}, f32[8,768]{1,0:T(8,128)}, f32[1,3072]{1,0:T(1,128)}...) custom-call(f32[128,768]{1,0:T(8,128)} %copy-done.14, ...), custom_call_target="tpu_custom_call" | custom-call | flops 20000000000 | bytes 22000000 | tf_op jit(solution)/shard_map/middle/pallas_call | solution.py:879
  165.4 21.8 %cross_back.1 = (bf16[2,2048,768]{2,1,0:T(8,128)(2,1)}, bf16[128,768]{1,0:T(8,128)(2,1)}, f32[8,768]{1,0:T(8,128)}, bf16[2048,768]{1,0:T(8,128)(2,1)}) custom-call(bf16[2,2048,768]{2,1,0:T(8,128)(2,1)} %get-tuple-element.102.kv_ref, bf16[128,768]{1,0:T(8,128)(2,1)} %copy-done.25, f32[128,768]{1,0:T(8,128)} %get-tuple-element.103.c_ref, ...), custom_call_target="tpu_custom_call" | custom-call | flops 30000001024 | bytes 22000000 | tf_op jit(solution)/shard_map/cross_back/pallas_call | solution.py:965
  187.2 3.7 all-to-all-start.1
  197.2 9.5 %self_back.1 = (f32[128,768]{1,0:T(8,128)S(1)}, f32[8,768]{1,0:T(8,128)S(1)}, bf16[4,384,768]{2,1,0:T(8,128)(2,1)S(1)}, bf16[4,384,768]{2,1,0:T(8,128)(2,1)}) custom-call(s32[4]{0:T(128)S(1)} %bitcast.45, bf16[128,768]{1,0:T(8,128)(2,1)S(1)} %collective-permute-done.2.y_ref, f32[128,768]{1,0:T(8,128)S(1)} %copy-done.15, f32[128,768]{1,0:T(8,128)S(1)} %copy-done.21, ...), custom_call_target="tpu_custom_call" | custom-call | flops 20000000000 | bytes 15000000 | tf_op jit(solution)/shard_map/self_back/pallas_call | solution.py:1083
  211.6 11.0 %cross_grads.1 = (bf16[4,288,768]{2,1,0:T(8,128)(2,1)S(1)}, bf16[4,288,768]{2,1,0:T(8,128)(2,1)S(1)}) custom-call(bf16[2048,768]{1,0:T(8,128)(2,1)} %bitcast.4.pooled_ref, bf16[2,2048,768]{2,1,0:T(8,128)(2,1)} %get-tuple-element.113.dkv_ref, f32[128,768]{1,0:T(8,128)S(1)} %copy-done.16, bf16[128,768]{1,0:T(8,128)(2,1)S(1)} %copy-done.18, ...), custom_call_target="tpu_custom_call" | custom-call | flops 10000000000 | bytes 15000000 | tf_op jit(solution)/shard_map/cross_grads/pallas_call | solution.py:1019
  225.0 25.8 %all-to-all-done.1 = bf16[8,256,768]{2,1,0:T(8,128)(2,1)S(1)} async-done(((bf16[8,256,768]{2,1,0:T(8,128)(2,1)}), bf16[8,256,768]{2,1,0:T(8,128)(2,1)S(1)}, u32[]{:S(2)}, u32[]{:S(2)}) %all-to-all-start.1) | async-done | bytes 3145760 | tf_op jit(solution)/shard_map/all_to_all | solution.py:1782
  250.8 5.3 %spread_rows.1.refs_0_ = bf16[1024,768]{1,0:T(8,128)(2,1)S(1)} custom-call(s32[1,2048]{1,0:T(1,128)S(1)} %bitcast.42, bf16[2048,768]{1,0:T(8,128)(2,1)S(1)} %bitcast.39), custom_call_target="tpu_custom_call" | custom-call | flops 4000000000 | bytes 5000000 | tf_op jit(solution)/shard_map/spread_rows/pallas_call | solution.py:652
  257.2 50.3 %encoder_feed_back.1 = (f32[1024,768]{1,0:T(8,128)}, f32[8,768]{1,0:T(8,128)}, f32[1,3072]{1,0:T(1,128)}, bf16[4,384,768]{2,1,0:T(8,128)(2,1)}, bf16[4,384,768]{...) custom-call(bf16[1024,768]{1,0:T(8,128)(2,1)} %copy-done.8, ...), custom_call_target="tpu_custom_call" | custom-call | flops 40000000000 | bytes 50000000 | tf_op jit(solution)/shard_map/encoder_feed_back/pallas_call | solution.py:397
  310.7 69.9 %encoder_attend_back.1 = (f32[1024,768]{1,0:T(8,128)}, f32[8,768]{1,0:T(8,128)}, bf16[4,288,768]{2,1,0:T(8,128)(2,1)}, bf16[4,288,768]{2,1,0:T(8,128)(2,1)}, bf1...) custom-call(f32[1024,768]{1,0:T(8,128)} %get-tuple-element.130.refs_0_, bf16[1024,768]{1,0:T(8,128)(2,1)} %bitcast.56, ...), custom_call_target="tpu_custom_call" | custom-call | flops 49999998976 | bytes 40000000 | tf_op jit(solution)/shard_map/encoder_attend_back/pallas_call | solution.py:526
  380.5 84.3 %last_sums.1 = (bf16[1344,768]{1,0:T(8,128)(2,1)}, f32[8,768]{1,0:T(8,128)}) custom-call(bf16[4,288,768]{2,1,0:T(8,128)(2,1)} %get-tuple-element.148.refs_0_, bf16[4,96,768]{2,1,0:T(8,128)(2,1)} %get-tuple-element.149.refs_1_, bf16[4,288,768]{2,1,0:T(8,128)(2,1)} %get-tuple-element.150.refs_2_, bf16[4,96,768]{2,1,0:T(8,128)(2,1)} %get-tuple-element.151.refs_3_, ...), custom_call_target="tpu_custom_call" | custom-call | flops 100000000 | bytes 100000000 | tf_op jit(solution)/shard_map/last_sums/pallas_call | solution.py:1536
  464.9 5.8 %unpack.1 = (f32[3,96,768]{2,1,0:T(8,128)}, f32[96,768]{1,0:T(8,128)}, f32[3,96]{1,0:T(4,128)}, f32[2,2,96]{2,1,0:T(2,128)}, f32[96,3072]{1,0:T(8,128)}, /*index...) custom-call(bf16[768,768]{1,0:T(8,128)(2,1)} %get-tuple-element.175., ...), custom_call_target="tpu_custom_call" | custom-call | flops 10000000 | bytes 13000000 | tf_op jit(solution)/shard_map/unpack/pallas_call | solution.py:1633
  (113 shorter events, 33.7 us)
Async XLA Ops:
  7.2 85.3 %collective-permute-start.1 = (s32[1,4]{1,0:T(1,128)}, s32[1,4]{1,0:T(1,128)S(1)}, u32[]{:S(2)}, u32[]{:S(2)}) collective-permute-start(s32[1,4]{1,0:T(1,128)} %bitcast.62), channel_id=1, source_target_pairs={{0,2},{1,3},{2,0},{3,1},{4,6},{5,7},{6,4},{7,5},{8,10},{9,11},{10,... | collective-permute-start | bytes 56 | tf_op jit(solution)/shard_map/ppermute | solution.py:1113
  11.3 67.8 %collective-permute-start = (s32[8,256]{1,0:T(8,128)}, s32[8,256]{1,0:T(8,128)S(1)}, u32[]{:S(2)}, u32[]{:S(2)}) collective-permute-start(s32[8,256]{1,0:T(8,128)} %bitcast.61), channel_id=1, source_target_pairs={{0,2},{1,3},{2,0},{3,1},{4,6},{5,7},{6,4},{7,5},{8,10},{9,11},{10,... | collective-permute-start | bytes 24584 | tf_op jit(solution)/shard_map/ppermute | solution.py:1113
  11.4 81.1 %collective-permute-start.2 = (bf16[128,768]{1,0:T(8,128)(2,1)}, bf16[128,768]{1,0:T(8,128)(2,1)S(1)}, u32[]{:S(2)}, u32[]{:S(2)}) collective-permute-start(bf16[128,768]{1,0:T(8,128)(2,1)} %bitcast.57), channel_id=1, source_target_pairs={{0,2},{1,3},{2,0},{3,1},{4,6},{5,7},{6,4},{7,5},{8,10},{9,11},{10,... | collective-permute-start | bytes 589832 | tf_op jit(solution)/shard_map/ppermute | solution.py:1113
  14.2 132.9 %collective-permute-start.4 = (bf16[128,768]{1,0:T(8,128)(2,1)}, bf16[128,768]{1,0:T(8,128)(2,1)S(1)}, u32[]{:S(2)}, u32[]{:S(2)}) collective-permute-start(bf16[128,768]{1,0:T(8,128)(2,1)} %bitcast.58), channel_id=1, source_target_pairs={{0,2},{1,3},{2,0},{3,1},{4,6},{5,7},{6,4},{7,5},{8,10},{9,11},{10,... | collective-permute-start | bytes 589832 | tf_op jit(solution)/shard_map/ppermute | solution.py:1113
  15.5 87.0 %collective-permute-start.3 = (s32[128,1024]{0,1:T(8,128)S(1)}, s32[128,1024]{0,1:T(8,128)S(1)}, u32[]{:S(2)}, u32[]{:S(2)}) collective-permute-start(s32[128,1024]{0,1:T(8,128)S(1)} %bitcast.49), channel_id=1, source_target_pairs={{0,2},{1,3},{2,0},{3,1},{4,6},{5,7},{6,4},{7,5},{8,10},{9,11},{10,... | collective-permute-start | bytes 1572872 | tf_op jit(solution)/shard_map/ppermute | solution.py:1113
  50.7 27.9 %copy-start.31 = (f32[768]{0:T(1024)S(1)}, f32[768]{0:T(1024)}, u32[]{:S(2)}) copy-start(f32[768]{0:T(1024)} %param.47) | copy-start | bytes 9220
  79.5 1.4 copy-start.7
  87.3 5.2 %copy-start.2 = (bf16[768,768]{1,0:T(8,128)(2,1)S(1)}, bf16[768,768]{1,0:T(8,128)(2,1)}, u32[]{:S(2)}) copy-start(bf16[768,768]{1,0:T(8,128)(2,1)} %wo_ref.5) | copy-start | bytes 3538948
  87.3 5.2 %copy-start.4 = (f32[6,768]{1,0:T(8,128)S(1)}, f32[6,768]{1,0:T(8,128)}, u32[]{:S(2)}) copy-start(f32[6,768]{1,0:T(8,128)} %b_ref.5) | copy-start | bytes 55300
  87.3 5.2 %copy-start.5 = (f32[3,2,768]{2,1,0:T(2,128)S(1)}, f32[3,2,768]{2,1,0:T(2,128)}, u32[]{:S(2)}) copy-start(f32[3,2,768]{2,1,0:T(2,128)} %n_ref.9) | copy-start | bytes 55300
  87.3 42.5 %all-to-all-start = ((bf16[8,256,768]{2,1,0:T(8,128)(2,1)}), bf16[8,256,768]{2,1,0:T(8,128)(2,1)}, u32[]{:S(2)}, u32[]{:S(2)}) async-start(bf16[8,256,768]{2,1,0:T(8,128)(2,1)} %bitcast.3), calls=%async_computation | async-start | bytes 6291456 | tf_op jit(solution)/shard_map/all_to_all | solution.py:1756
  91.9 218.8 %reduce-scatter.2.cloned.1.call-start = ((), (), s32[]{:S(2)}) async-start(), calls=%async_computation.3 | async-start | bytes 10616832 | tf_op jit(solution)/shard_map/reduce_scatter | solution.py:1778
  92.5 2.0 copy-start
  94.5 2.0 copy-start.1
  110.0 37.1 %copy-start.11 = (f32[2048,128]{1,0:T(8,128)}, f32[2048,128]{1,0:T(8,128)S(1)}, u32[]{:S(2)}) copy-start(f32[2048,128]{1,0:T(8,128)S(1)} %get-tuple-element.107.mask_ref) | copy-start | bytes 3145732
  187.2 3.7 copy-start.6
  187.2 63.6 %all-to-all-start.1 = ((bf16[8,256,768]{2,1,0:T(8,128)(2,1)}), bf16[8,256,768]{2,1,0:T(8,128)(2,1)S(1)}, u32[]{:S(2)}, u32[]{:S(2)}) async-start(bf16[8,256,768]{2,1,0:T(8,128)(2,1)} %bitcast.47), calls=%async_computation.1 | async-start | bytes 6291456 | tf_op jit(solution)/shard_map/all_to_all | solution.py:1782
  190.9 274.0 %all-reduce.5.cloned.1.call-start = ((), (), s32[]{:S(2)}) async-start(), calls=%async_computation.4 | async-start | bytes 4128768 | tf_op jit(solution)/shard_map/psum | solution.py:1840
  197.2 12.3 %copy-start.29 = (f32[8,768]{1,0:T(8,128)S(1)}, f32[8,768]{1,0:T(8,128)}, u32[]{:S(2)}) copy-start(f32[8,768]{1,0:T(8,128)} %get-tuple-element.142) | copy-start | bytes 73732
  206.6 1.4 copy-start.13
  257.2 52.8 %copy-start.30 = (f32[1,3072]{1,0:T(1,128)S(1)}, f32[1,3072]{1,0:T(1,128)}, u32[]{:S(2)}) copy-start(f32[1,3072]{1,0:T(1,128)} %get-tuple-element.143) | copy-start | bytes 36868
  464.9 8.4 %copy-start.28 = (bf16[128,768]{1,0:T(8,128)(2,1)S(1)}, bf16[128,768]{1,0:T(8,128)(2,1)}, u32[]{:S(2)}) copy-start(bf16[128,768]{1,0:T(8,128)(2,1)} %get-tuple-element.126) | copy-start | bytes 589828
  464.9 9.0 %copy-start.26 = (f32[1024,768]{1,0:T(8,128)S(1)}, f32[1024,768]{1,0:T(8,128)}, u32[]{:S(2)}) copy-start(f32[1024,768]{1,0:T(8,128)} %get-tuple-element.144) | copy-start | bytes 9437188
  473.9 1.7 copy-start.27
  (18 other events, 17.0 us)
Sparse Core Ops, SparseCore 0:
  165.5 107.4 reduce-scatter.1
  310.8 100.6 all-reduce.4

commit v6 on v4

--- a/solution.py
+++ b/solution.py
@@ -925,9 +925,10 @@
     column = jnp.sum(product, -1, keepdims=True)
     inner = jnp.broadcast_to(column, (heads * rows, 128)).T[0:1]
     stat = stat_ref[0, 0:1]
-    for h in range(heads):
-        part = slice(h * rows, (h + 1) * rows)
-        weight = jnp.exp(dot(kv_ref[0], q_heads[part], NT) + mask_ref[...] - stat[:, part])
+    mask = jnp.concatenate([mask_ref[...]] * 2, 1)
+    for h in range(0, heads, 2):
+        part = slice(h * rows, (h + 2) * rows)
+        weight = jnp.exp(dot(kv_ref[0], q_heads[part], NT) + mask - stat[:, part])
         weight_back = dot(kv_ref[1], dc_heads[part], NT)
         weights[:, part] = low(weight)
         scores_back[:, part] = low(weight * (weight_back - inner[:, part]))
@@ -1634,7 +1635,7 @@
         in_specs=[here] * 5,
         out_specs=[here] * len(shapes),
         out_shape=[like(shape, wide_type) for shape in shapes],
-        compiler_params=params(40),
+        compiler_params=params(),
         cost_estimate=cost(1e7, 1.3e7),
         name="unpack",
     )(feed, first, last, vector, biases)

time: 491 us -> 490 us (level)
    unnamed x90 -> x80, local copies, waits for them, and re-layouts: 27.4 us -> 23 us
  transfers between devices with their start and end apart: 6 -> 6, of which waited for: 2 -> 2; matrix products, arithmetic and copies ran while one was open for 2% -> 2% of each run, Pallas kernels for 67% -> 66%
where the time goes in v6:
time: 490 us; the launch traced here: 481 us
  Pallas kernels  367 us (75%)
  waiting for transfers between devices  51.4 us (10%)
  local copies, waits for them, and re-layouts  30.2 us (6%)
  between operations  14.8 us (3%)
  starting transfers between devices  12.9 us (3%)
    pallas_call x1, Pallas kernels, last_sums(): pl.pallas_call(functools.partial(last_sums_kernel, plan), in_specs=plan.i...  84.3 us
    pallas_call x1, Pallas kernels, encoder_attend_back(): pl.pallas_call(functools.partial(encoder_attend_back_kernel, plan), grid=...  69.8 us
    pallas_call x1, Pallas kernels, encoder_feed_back(): pl.pallas_call(functools.partial(encoder_feed_back_kernel, plan), grid=(4...  50.2 us
    pallas_call x1, Pallas kernels, encoder_attend(): pl.pallas_call(encoder_attend_kernel, grid=(groups,), in_specs=[full(toke...  30.9 us
    all_to_all x1, waiting for transfers between devices, on_device(): lax.all_to_all(dpool.reshape(owners, -1, WIDTH), 'dp', split_axis=0, conc...  28.3 us
    pallas_call x1, Pallas kernels, encoder_feed(): pl.pallas_call(encoder_feed_kernel, grid=(4,), in_specs=[full(tokens, wid...  27.8 us
    all_to_all x1, waiting for transfers between devices, on_device(): lax.all_to_all(picked, 'dp', split_axis=0, concat_axis=0, tiled=True)  23.1 us
    unnamed x80, local copies, waits for them, and re-layouts  23 us
  transfers between devices with their start and end apart: 6, of which 2 were waited for; matrix products, arithmetic and copies ran while one was open for 2% of the time, Pallas kernels for 66%

profile of v6, /device:TPU:0, one launch (start us, length us, event | category | flops | bytes accessed | tf_op | source)
XLA Modules:
  0.0 480.8 jit_solution(9911455131604410849)
XLA Ops:
  8.2 4.1 collective-permute-start.1
  15.5 30.9 %encoder_attend.1 = (bf16[3,1024,768]{2,1,0:T(8,128)(2,1)}, f32[1024,768]{1,0:T(8,128)}, bf16[1024,768]{1,0:T(8,128)(2,1)}, f32[3,8,1024]{2,1,0:T(8,128)}, f32[1024,768]{1,0:T(8,128)}) custom-call(bf16[1024,768]{1,0:T(8,128)(2,1)} %bitcast.58, bf16[3,768,768]{2,1,0:T(8,128)(2,1)} %refs_5_.1, bf16[768,768]{1,0:T(8,128)(2,1)} %refs_6_.3, f32[3,768]{1,0:T(4,128)} %b_ref.3, ...), custom_call_target="tpu_custom_call" | custom-call | flops 30000001024 | bytes 20000000 | tf_op jit(solution)/shard_map/encoder_attend/pallas_call | solution.py:200
  46.5 27.8 %encoder_feed.1 = (bf16[1024,3072]{1,0:T(8,128)(2,1)}, bf16[1024,3072]{1,0:T(8,128)(2,1)}, f32[1024,768]{1,0:T(8,128)}, bf16[1024,768]{1,0:T(8,128)(2,1)}) custom-call(f32[1024,768]{1,0:T(8,128)} %get-tuple-element.98.mixed_ref.refs_2_, f32[2,2,768]{2,1,0:T(2,128)} %refs_6_.2, bf16[768,3072]{1,0:T(8,128)(2,1)} %refs_7_.1, f32[1,3072]{1,0:T(1,128)} %bitcast.60, ...), custom_call_target="tpu_custom_call" | custom-call | flops 20000000000 | bytes 30000000 | tf_op jit(solution)/shard_map/encoder_feed/pallas_call | solution.py:270
  76.8 6.4 %pick_rows.1 = bf16[2048,768]{1,0:T(8,128)(2,1)} custom-call(s32[2048,1]{1,0:T(8,128)S(1)} %bitcast.43, bf16[1024,768]{1,0:T(8,128)(2,1)S(1)} %copy-done.7), custom_call_target="tpu_custom_call" | custom-call | flops 4000000000 | bytes 5000000 | tf_op jit(solution)/shard_map/pick_rows/pallas_call | solution.py:619
  83.2 4.4 all-to-all-start
  88.9 6.5 %slot_mask.1 = (f32[128,2048]{1,0:T(8,128)S(1)}, f32[2048,128]{1,0:T(8,128)S(1)}) custom-call(s32[1024,128]{1,0:T(8,128)S(1)} %bitcast.44), custom_call_target="tpu_custom_call" | custom-call | flops 10000000000 | bytes 1000000 | tf_op jit(solution)/shard_map/slot_mask/pallas_call | solution.py:600
  96.5 3.1 self_forward.1
  102.5 23.1 %all-to-all-done = bf16[8,256,768]{2,1,0:T(8,128)(2,1)} async-done(((bf16[8,256,768]{2,1,0:T(8,128)(2,1)}), bf16[8,256,768]{2,1,0:T(8,128)(2,1)}, u32[]{:S(2)}, u32[]{:S(2)}) %all-to-all-start) | async-done | bytes 3145760 | tf_op jit(solution)/shard_map/all_to_all | solution.py:1758
  125.5 17.4 %cross_forward.1 = (bf16[2,2048,768]{2,1,0:T(8,128)(2,1)}, f32[128,768]{1,0:T(8,128)}, f32[3,8,512]{2,1,0:T(8,128)}) custom-call(bf16[2048,768]{1,0:T(8,128)(2,1)} %bitcast.5.pooled_ref, bf16[128,768]{1,0:T(8,128)(2,1)} %copy-done.25, f32[128,2048]{1,0:T(8,128)} %copy-done.12, bf16[3,768,768]{2,1,0:T(8,128)(2,1)} %cw_ref.3, f32[6,768]{1,0:T(8,128)} %b_ref.5), custom_call_target="tpu_custom_call" | custom-call | flops 20000000000 | bytes 12000000 | tf_op jit(solution)/shard_map/cross_forward/pallas_call | solution.py:782
  142.9 17.6 %middle.1 = (bf16[128,768]{1,0:T(8,128)(2,1)}, f32[128,768]{1,0:T(8,128)}, bf16[128,768]{1,0:T(8,128)(2,1)}, f32[8,768]{1,0:T(8,128)}, f32[1,3072]{1,0:T(1,128)}...) custom-call(f32[128,768]{1,0:T(8,128)} %copy-done.14, ...), custom_call_target="tpu_custom_call" | custom-call | flops 20000000000 | bytes 22000000 | tf_op jit(solution)/shard_map/middle/pallas_call | solution.py:879
  160.5 21.3 %cross_back.1 = (bf16[2,2048,768]{2,1,0:T(8,128)(2,1)}, bf16[128,768]{1,0:T(8,128)(2,1)}, f32[8,768]{1,0:T(8,128)}, bf16[2048,768]{1,0:T(8,128)(2,1)}) custom-call(bf16[2,2048,768]{2,1,0:T(8,128)(2,1)} %get-tuple-element.102.kv_ref, bf16[128,768]{1,0:T(8,128)(2,1)} %copy-done.25, f32[128,768]{1,0:T(8,128)} %get-tuple-element.103.c_ref, ...), custom_call_target="tpu_custom_call" | custom-call | flops 30000001024 | bytes 22000000 | tf_op jit(solution)/shard_map/cross_back/pallas_call | solution.py:965
  181.9 3.7 all-to-all-start.1
  185.6 1.6 copy-done.3
  192.1 9.5 %self_back.1 = (f32[128,768]{1,0:T(8,128)S(1)}, f32[8,768]{1,0:T(8,128)S(1)}, bf16[4,384,768]{2,1,0:T(8,128)(2,1)S(1)}, bf16[4,384,768]{2,1,0:T(8,128)(2,1)}) custom-call(s32[4]{0:T(128)S(1)} %slice_bitcast_fusion.6.lengths_ref, bf16[128,768]{1,0:T(8,128)(2,1)S(1)} %get-tuple-element.178.y_ref, f32[128,768]{1,0:T(8,128)S(1)} %copy-done.15, ...), custom_call_target="tpu_custom_call" | custom-call | flops 20000000000 | bytes 15000000 | tf_op jit(solution)/shard_map/self_back/pallas_call | solution.py:1083
  201.6 1.4 copy-done.13
  206.5 11.0 %cross_grads.1 = (bf16[4,288,768]{2,1,0:T(8,128)(2,1)S(1)}, bf16[4,288,768]{2,1,0:T(8,128)(2,1)S(1)}) custom-call(bf16[2048,768]{1,0:T(8,128)(2,1)} %bitcast.5.pooled_ref, bf16[2,2048,768]{2,1,0:T(8,128)(2,1)} %get-tuple-element.113.dkv_ref, f32[128,768]{1,0:T(8,128)S(1)} %copy-done.16, bf16[128,768]{1,0:T(8,128)(2,1)S(1)} %copy-done.18, ...), custom_call_target="tpu_custom_call" | custom-call | flops 10000000000 | bytes 15000000 | tf_op jit(solution)/shard_map/cross_grads/pallas_call | solution.py:1019
  219.9 28.3 %all-to-all-done.1 = bf16[8,256,768]{2,1,0:T(8,128)(2,1)S(1)} async-done(((bf16[8,256,768]{2,1,0:T(8,128)(2,1)}), bf16[8,256,768]{2,1,0:T(8,128)(2,1)S(1)}, u32[]{:S(2)}, u32[]{:S(2)}) %all-to-all-start.1) | async-done | bytes 3145760 | tf_op jit(solution)/shard_map/all_to_all | solution.py:1784
  248.2 5.3 %spread_rows.1.refs_0_ = bf16[1024,768]{1,0:T(8,128)(2,1)S(1)} custom-call(s32[1,2048]{1,0:T(1,128)S(1)} %bitcast.46, bf16[2048,768]{1,0:T(8,128)(2,1)S(1)} %bitcast.42), custom_call_target="tpu_custom_call" | custom-call | flops 4000000000 | bytes 5000000 | tf_op jit(solution)/shard_map/spread_rows/pallas_call | solution.py:652
  254.6 50.2 %encoder_feed_back.1 = (f32[1024,768]{1,0:T(8,128)}, f32[8,768]{1,0:T(8,128)}, f32[1,3072]{1,0:T(1,128)}, bf16[4,384,768]{2,1,0:T(8,128)(2,1)}, bf16[4,384,768]{...) custom-call(bf16[1024,768]{1,0:T(8,128)(2,1)} %copy-done.8, ...), custom_call_target="tpu_custom_call" | custom-call | flops 40000000000 | bytes 50000000 | tf_op jit(solution)/shard_map/encoder_feed_back/pallas_call | solution.py:397
  308.1 69.8 %encoder_attend_back.1 = (f32[1024,768]{1,0:T(8,128)}, f32[8,768]{1,0:T(8,128)}, bf16[4,288,768]{2,1,0:T(8,128)(2,1)}, bf16[4,288,768]{2,1,0:T(8,128)(2,1)}, bf1...) custom-call(f32[1024,768]{1,0:T(8,128)} %get-tuple-element.130.refs_0_, bf16[1024,768]{1,0:T(8,128)(2,1)} %bitcast.59, ...), custom_call_target="tpu_custom_call" | custom-call | flops 49999998976 | bytes 40000000 | tf_op jit(solution)/shard_map/encoder_attend_back/pallas_call | solution.py:526
  377.9 84.3 %last_sums.1 = (bf16[1344,768]{1,0:T(8,128)(2,1)}, f32[8,768]{1,0:T(8,128)}) custom-call(bf16[4,288,768]{2,1,0:T(8,128)(2,1)} %get-tuple-element.148.refs_0_, bf16[4,96,768]{2,1,0:T(8,128)(2,1)} %get-tuple-element.149.refs_1_, bf16[4,288,768]{2,1,0:T(8,128)(2,1)} %get-tuple-element.150.refs_2_, bf16[4,96,768]{2,1,0:T(8,128)(2,1)} %get-tuple-element.151.refs_3_, ...), custom_call_target="tpu_custom_call" | custom-call | flops 100000000 | bytes 100000000 | tf_op jit(solution)/shard_map/last_sums/pallas_call | solution.py:1536
  462.3 5.8 %unpack.1 = (f32[3,96,768]{2,1,0:T(8,128)}, f32[96,768]{1,0:T(8,128)}, f32[3,96]{1,0:T(4,128)}, f32[2,2,96]{2,1,0:T(2,128)}, f32[96,3072]{1,0:T(8,128)}, /*index...) custom-call(bf16[768,768]{1,0:T(8,128)(2,1)} %get-tuple-element.175., ...), custom_call_target="tpu_custom_call" | custom-call | flops 10000000 | bytes 13000000 | tf_op jit(solution)/shard_map/unpack/pallas_call | solution.py:1633
  468.1 1.3 reduce.2
  471.3 1.7 copy.74
  (114 shorter events, 29.7 us)
Async XLA Ops:
  8.2 66.6 %collective-permute-start.1 = (bf16[256,768]{1,0:T(8,128)(2,1)S(1)}, bf16[256,768]{1,0:T(8,128)(2,1)S(1)}, u32[]{:S(2)}, u32[]{:S(2)}) collective-permute-start(bf16[256,768]{1,0:T(8,128)(2,1)S(1)} %pad_maximum_fusion), channel_id=1, source_target_pairs={{0,2},{1,3},{2,0},{3,1},{4,6},{5,7},{6,4},{7,5},{8,10},{9,11},{10,... | collective-permute-start | bytes 1179656 | tf_op jit(solution)/shard_map/ppermute | solution.py:1113
  14.2 61.4 %collective-permute-start = (s32[131,1024]{1,0:T(8,128)S(1)}, s32[131,1024]{1,0:T(8,128)S(1)}, u32[]{:S(2)}, u32[]{:S(2)}) collective-permute-start(s32[131,1024]{1,0:T(8,128)S(1)} %pad_add_fusion), channel_id=1, source_target_pairs={{0,2},{1,3},{2,0},{3,1},{4,6},{5,7},{6,4},{7,5},{8,10},{9,11},{10,... | collective-permute-start | bytes 1609736 | tf_op jit(solution)/shard_map/ppermute | solution.py:1113
  46.5 27.8 %copy-start.32 = (f32[768]{0:T(1024)S(1)}, f32[768]{0:T(1024)}, u32[]{:S(2)}) copy-start(f32[768]{0:T(1024)} %param.47) | copy-start | bytes 9220
  74.3 2.5 copy-start.7
  83.2 42.3 %all-to-all-start = ((bf16[8,256,768]{2,1,0:T(8,128)(2,1)}), bf16[8,256,768]{2,1,0:T(8,128)(2,1)}, u32[]{:S(2)}, u32[]{:S(2)}) async-start(bf16[8,256,768]{2,1,0:T(8,128)(2,1)} %bitcast.4), calls=%async_computation | async-start | bytes 6291456 | tf_op jit(solution)/shard_map/all_to_all | solution.py:1758
  87.6 220.4 %reduce-scatter.2.cloned.1.call-start = ((), (), s32[]{:S(2)}) async-start(), calls=%async_computation.3 | async-start | bytes 10616832 | tf_op jit(solution)/shard_map/reduce_scatter | solution.py:1780
  88.9 7.5 %copy-start = (bf16[3,768,768]{2,1,0:T(8,128)(2,1)S(1)}, bf16[3,768,768]{2,1,0:T(8,128)(2,1)}, u32[]{:S(2)}) copy-start(bf16[3,768,768]{2,1,0:T(8,128)(2,1)} %w_ref.9) | copy-start | bytes 10616836
  88.9 7.5 %copy-start.1 = (bf16[3,768,768]{2,1,0:T(8,128)(2,1)S(1)}, bf16[3,768,768]{2,1,0:T(8,128)(2,1)}, u32[]{:S(2)}) copy-start(bf16[3,768,768]{2,1,0:T(8,128)(2,1)} %cw_ref.3) | copy-start | bytes 10616836
  88.9 7.5 %copy-start.2 = (bf16[768,768]{1,0:T(8,128)(2,1)S(1)}, bf16[768,768]{1,0:T(8,128)(2,1)}, u32[]{:S(2)}) copy-start(bf16[768,768]{1,0:T(8,128)(2,1)} %wo_ref.5) | copy-start | bytes 3538948
  88.9 7.5 %copy-start.4 = (f32[6,768]{1,0:T(8,128)S(1)}, f32[6,768]{1,0:T(8,128)}, u32[]{:S(2)}) copy-start(f32[6,768]{1,0:T(8,128)} %b_ref.5) | copy-start | bytes 55300
  88.9 7.5 %copy-start.5 = (f32[3,2,768]{2,1,0:T(2,128)S(1)}, f32[3,2,768]{2,1,0:T(2,128)}, u32[]{:S(2)}) copy-start(f32[3,2,768]{2,1,0:T(2,128)} %n_ref.9) | copy-start | bytes 55300
  96.4 3.1 copy-start.11
  181.8 3.7 copy-start.6
  181.9 66.3 %all-to-all-start.1 = ((bf16[8,256,768]{2,1,0:T(8,128)(2,1)}), bf16[8,256,768]{2,1,0:T(8,128)(2,1)S(1)}, u32[]{:S(2)}, u32[]{:S(2)}) async-start(bf16[8,256,768]{2,1,0:T(8,128)(2,1)} %bitcast.48), calls=%async_computation.1 | async-start | bytes 6291456 | tf_op jit(solution)/shard_map/all_to_all | solution.py:1784
  185.5 276.8 %all-reduce.6.cloned.1.call-start = ((), (), s32[]{:S(2)}) async-start(), calls=%async_computation.4 | async-start | bytes 4128768 | tf_op jit(solution)/shard_map/psum | solution.py:1842
  185.6 1.6 copy-start.3
  192.1 12.4 %copy-start.30 = (f32[8,768]{1,0:T(8,128)S(1)}, f32[8,768]{1,0:T(8,128)}, u32[]{:S(2)}) copy-start(f32[8,768]{1,0:T(8,128)} %get-tuple-element.142) | copy-start | bytes 73732
  201.6 1.4 copy-start.13
  217.5 1.2 copy-start.9
  218.7 1.2 copy-start.10
  254.6 52.7 %copy-start.31 = (f32[1,3072]{1,0:T(1,128)S(1)}, f32[1,3072]{1,0:T(1,128)}, u32[]{:S(2)}) copy-start(f32[1,3072]{1,0:T(1,128)} %get-tuple-element.143) | copy-start | bytes 36868
  462.3 8.4 %copy-start.29 = (bf16[128,768]{1,0:T(8,128)(2,1)S(1)}, bf16[128,768]{1,0:T(8,128)(2,1)}, u32[]{:S(2)}) copy-start(bf16[128,768]{1,0:T(8,128)(2,1)} %get-tuple-element.126) | copy-start | bytes 589828
  462.3 9.0 %copy-start.26 = (f32[1024,768]{1,0:T(8,128)S(1)}, f32[1024,768]{1,0:T(8,128)}, u32[]{:S(2)}) copy-start(f32[1024,768]{1,0:T(8,128)} %get-tuple-element.144) | copy-start | bytes 9437188
  471.3 1.7 copy-start.28
  (15 other events, 13.4 us)
Sparse Core Ops, SparseCore 0:
  160.6 109.8 reduce-scatter.1
  308.2 100.6 all-reduce.5
